TPU v7x, 512 devices: a whole 4x8x8 slice. The times are simulated.
512 devices in a mesh: dp: 32 (over z, y_lo), tensor: 16 (over x, y_hi, core).
Axes of the slice: x: 4, y: 8 (y_hi: 2, y_lo: 4; y = y_hi * 4 + y_lo), z: 8, core: 2. Of those that a mesh axis runs over, the one named last changes fastest.
Arguments:
- activations: bfloat16 [2, 2048, 8192], P(None, 'dp'), may hold values from -6 to 6
- out_grads: bfloat16 [2, 2048, 8192], P(None, 'dp'), may hold values from -6 to 6
- act_basis: bfloat16 [8192, 6144], P('dp', 'tensor'), may hold values from -0.0625 to 0.0625
- grad_basis: bfloat16 [8192, 4096], P('dp', 'tensor'), may hold values from -0.0625 to 0.0625
Outputs:
- adjusted_spectrum: float32 [4096, 6144], P('tensor', 'dp')
All inputs are finite; a program needn't handle non-finite values.
Results may differ from a plain program's by a relative error of at most 0.0041.
Values may be sent and summed in bfloat16 or wider, within the bound.
No kernel may reach another device: no remote copies, remote signals or barrier semaphores. Data moves between devices by JAX's collectives and lax.ppermute only.
A program may use at most 64 MiB of HBM per device.

v0:
```python
import jax
import jax.numpy as jnp
from jax import lax
from jax.sharding import PartitionSpec as P


def gather_moments(operand_entry, piece):
    return jnp.dot(operand_entry, piece, preferred_element_type=jnp.float32)


def spread_acts(turned):
    wide = lax.all_gather(turned, "tensor", axis=2, tiled=True)
    return lax.all_to_all(wide, "dp", split_axis=2, concat_axis=1, tiled=True)


def spread_grads(turned):
    return lax.all_gather(turned, "dp", axis=1, tiled=True)


def local(activations, out_grads, act_basis, grad_basis):
    seq_count, local_len, feature_width = activations.shape
    input_operand = activations.reshape(seq_count * local_len, feature_width)
    grad_source = out_grads.reshape(seq_count * local_len, feature_width)
    act_turned = gather_moments(input_operand, lax.all_gather(act_basis, "dp", axis=0, tiled=True))
    grad_turned = gather_moments(grad_source, lax.all_gather(grad_basis, "dp", axis=0, tiled=True))
    act_turned = act_turned.astype(jnp.bfloat16).reshape(seq_count, local_len, act_basis.shape[1])
    grad_turned = grad_turned.astype(jnp.bfloat16).reshape(
        seq_count, local_len, grad_basis.shape[1]
    )
    act_panel = spread_acts(act_turned)
    grad_panel = spread_grads(grad_turned)
    eigvec_outer = lax.dot_general(
        grad_panel, act_panel, (((1,), (1,)), ((0,), (0,))), preferred_element_type=jnp.float32
    )
    return jnp.sum(eigvec_outer * eigvec_outer, axis=0) / (seq_count * grad_panel.shape[1])


def solution(mesh):
    placed = (P(None, "dp", None), P(None, "dp", None), P("dp", "tensor"), P("dp", "tensor"))
    return jax.shard_map(
        local, mesh=mesh, in_specs=placed, out_specs=P("tensor", "dp"), check_vma=False
    )
```

profile of v0, /device:TPU:6, one launch (start us, length us, event | category | flops | bytes accessed | tf_op | source)
XLA Modules:
  0.0 600.5 jit_solution(1313655228416249102)
XLA Ops:
  6.5 0.0 copy-start
  6.5 0.0 all-gather.9.cloned.1.call-start
  6.5 0.7 all-gather.9.cloned.1.call-update
  7.3 0.0 all-gather.5.cloned.1.call-start
  7.3 0.7 all-gather.5.cloned.1.call-update
  8.0 0.0 all-gather.11.cloned.1.call-start
  8.1 185.6 %all-gather.9.cloned.1.call-done = bf16[8192,384]{1,0:T(8,128)(2,1)} async-done(((bf16[256,384]{1,0:T(8,128)(2,1)}), bf16[8192,384]{1,0:T(8,128)(2,1)}) %all-gather.9.cloned.1.call-update) | async-done | bytes 6291472 | tf_op jit(solution)/shard_map/all_gather | solution.py:24
  193.6 0.0 copy-done
  193.6 4.7 convolution_convert_fusion
  198.3 0.0 all-gather.11.cloned.1.call-update
  198.3 0.0 all-gather.7.cloned.1.call-start
  198.4 163.2 %all-gather.5.cloned.1.call-done = bf16[8192,256]{1,0:T(8,128)(2,1)} async-done(((bf16[256,256]{1,0:T(8,128)(2,1)}), bf16[8192,256]{1,0:T(8,128)(2,1)}) %all-gather.5.cloned.1.call-update) | async-done | bytes 4194320 | tf_op jit(solution)/shard_map/all_gather | solution.py:25
  361.5 4.2 convolution_convert_fusion.1
  365.7 0.0 all-gather.7.cloned.1.call-update
  365.7 61.0 %all-gather.11.cloned.1.call-done = bf16[2,64,6144]{2,1,0:T(8,128)(2,1)} async-done(((bf16[2,64,384]{2,1,0:T(8,128)(2,1)}), bf16[2,64,6144]{2,1,0:T(8,128)(2,1)}) %all-gather.11.cloned.1.call-update) | async-done | bytes 1572880 | tf_op jit(solution)/shard_map/all_gather | solution.py:12
  426.7 7.5 %copy.13 = bf16[2,64,6144]{1,0,2:T(2,128)(2,1)} copy(bf16[2,64,6144]{2,1,0:T(8,128)(2,1)} %all-gather.11.cloned.1.call-done) | data formatting | bytes 3145728 | tf_op jit(solution)/shard_map/all_gather | solution.py:12
  434.2 7.8 %reshape.16 = bf16[32,2,12288]{2,1,0:T(2,128)(2,1)} reshape(bf16[6144,2,64]{2,1,0:T(2,128)(2,1)} %bitcast.18) | data formatting | bytes 3145728
  442.0 66.0 %all_to_all.18 = bf16[32,2,12288]{2,1,0:T(2,128)(2,1)} all-to-all(bf16[32,2,12288]{2,1,0:T(2,128)(2,1)} %reshape.16), channel_id=1, replica_groups=mesh['dp'=32,'tensor'=16] {'dp'}, dimensions={0} | all-to-all | bytes 3145728 | tf_op jit(solution)/shard_map/all_to_all | solution.py:13
  508.1 7.8 %reshape.17 = bf16[6144,2,64]{2,1,0:T(2,128)(2,1)} reshape(bf16[32,2,12288]{2,1,0:T(2,128)(2,1)} %all_to_all.18) | data formatting | bytes 3145728
  515.9 7.9 %copy.19 = bf16[2,64,32,192]{3,1,2,0:T(8,128)(2,1)} copy(bf16[2,64,32,192]{1,0,3,2:T(2,128)(2,1)} %bitcast.19) | data formatting | bytes 3145728 | tf_op jit(solution)/shard_map/all_to_all | solution.py:13
  523.8 66.3 %all-gather.7.cloned.1.call-done = bf16[2,2048,256]{2,1,0:T(8,128)(2,1)} async-done(((bf16[2,64,256]{2,1,0:T(8,128)(2,1)}), bf16[2,2048,256]{2,1,0:T(8,128)(2,1)}) %all-gather.7.cloned.1.call-update) | async-done | bytes 2097168 | tf_op jit(solution)/shard_map/all_gather | solution.py:17
  590.2 3.1 fusion
  593.3 0.7 broadcast_multiply_fusion
Async XLA Ops:
  6.5 187.1 %copy-start = (bf16[2,64,8192]{2,1,0:T(8,128)(2,1)S(1)}, bf16[2,64,8192]{2,1,0:T(8,128)(2,1)}, u32[]{:S(2)}) copy-start(bf16[2,64,8192]{2,1,0:T(8,128)(2,1)} %param.4) | copy-start | bytes 6291460
  6.5 187.1 %all-gather.9.cloned.1.call-start = ((), (), s32[]{:S(2)}) async-start(), calls=%async_computation.3 | async-start | bytes 6488064 | tf_op jit(solution)/shard_map/all_gather | solution.py:24
  7.3 354.3 %all-gather.5.cloned.1.call-start = ((), (), s32[]{:S(2)}) async-start(), calls=%async_computation.1 | async-start | bytes 4325376 | tf_op jit(solution)/shard_map/all_gather | solution.py:25
  8.0 418.7 %all-gather.11.cloned.1.call-start = ((), (), s32[]{:S(2)}) async-start(), calls=%async_computation.4 | async-start | bytes 1671168 | tf_op jit(solution)/shard_map/all_gather | solution.py:12
  198.3 391.8 %all-gather.7.cloned.1.call-start = ((), (), s32[]{:S(2)}) async-start(), calls=%async_computation.2 | async-start | bytes 2162688 | tf_op jit(solution)/shard_map/all_gather | solution.py:17
Sparse Core Ops, SparseCore 0:
  9.4 184.1 all-gather.8
  195.7 165.7 all-gather.4
  364.7 61.9 all-gather.10
  428.6 161.4 all-gather.6
where the time goes:
time: 601 us; the launch traced here: 600 us
  waiting for transfers between devices  477 us (79%)
  blocking collectives  66 us (11%)
  local copies, waits for them, and re-layouts  31.1 us (5%)
  between operations  13.1 us (2%)
  matrix products  11.9 us (2%)
    all_gather x1, waiting for transfers between devices, local(): lax.all_gather(act_basis, 'dp', axis=0, tiled=True)  186 us
    all_gather x1, waiting for transfers between devices, local(): lax.all_gather(grad_basis, 'dp', axis=0, tiled=True)  163 us
    all_gather x1, waiting for transfers between devices, spread_grads(): return lax.all_gather(turned, 'dp', axis=1, tiled=True)  66.3 us
    all_to_all x1, blocking collectives, spread_acts(): return lax.all_to_all(wide, 'dp', split_axis=2, concat_axis=1, tiled=True)  66 us
    all_gather x1, waiting for transfers between devices, spread_acts(): wide = lax.all_gather(turned, 'tensor', axis=2, tiled=True)  61 us
    unnamed x4, local copies, waits for them, and re-layouts  15.6 us
  transfers between devices with their start and end apart: 4, of which 4 were waited for; matrix products, arithmetic and copies ran while one was open for 7% of the time, Pallas kernels for 0%

commit v1 on v0

v1 whole, which is shorter than its diff:
```python
import jax
import jax.numpy as jnp
from jax import lax
from jax.experimental import pallas as pl
from jax.experimental.pallas import tpu as pltpu
from jax.sharding import Mesh, PartitionSpec as P

Z, Y, X, H, C = "z", "y", "x", "h", "c"
NZ, NY, NX, NH, NC = 8, 4, 4, 2, 2

VMEM_LIMIT = 40 * 2**20
SCALARS = pl.BlockSpec(memory_space=pltpu.SMEM)
WHOLE = pl.BlockSpec(memory_space=pltpu.VMEM)


def swap_cores(v):
    return lax.ppermute(v, C, [(0, 1), (1, 0)])


def ring_y(v, shift):
    pairs = []
    for at in range(NH * NY):
        to = (at + shift) % (NH * NY)
        pairs.append((at % NY * NH + at // NY, to % NY * NH + to // NY))
    return lax.ppermute(v, (Y, H), pairs)


def transpose_planes(v):
    pairs = []
    for z in range(NZ):
        for t in range(NX * NH):
            pairs.append((z * NX * NH + t, t * NX * NH + z))
    return lax.ppermute(v, (Z, X, H), pairs)


def spread(v, axes, count):
    return lax.all_to_all(jnp.broadcast_to(v[None], (count,) + v.shape), axes, 0, 0)


def cut_kernel(at_ref, v_ref, own_ref, after_ref, before_ref, across_ref):
    y, core = at_ref[0], at_ref[1]
    width = own_ref.shape[2] // 2
    for z in range(2):
        for steps, out in ((0, own_ref), (1, after_ref), (3, before_ref), (2, across_ref)):
            block = z * NY + lax.rem(y + steps, NY)
            cols = pl.ds(pl.multiple_of(block * width, width), width)
            if steps == 0:
                out[:, :, z * width : (z + 1) * width] = v_ref[:, :, cols]
            else:
                out[:, z * width : (z + 1) * width] = v_ref[core, :, cols]


def cut_features(at, values):
    seqs, tokens, features = values.shape
    steps = NZ // 2
    part = features // NY // steps
    piece = jax.ShapeDtypeStruct((tokens, features // NY), values.dtype)
    piece_spec = pl.BlockSpec((tokens, part), lambda i: (0, i))
    return pl.pallas_call(
        cut_kernel,
        grid=(steps,),
        out_shape=(
            jax.ShapeDtypeStruct((seqs, tokens, features // NY), values.dtype),
            piece,
            piece,
            piece,
        ),
        in_specs=[SCALARS, pl.BlockSpec((seqs, tokens, part * NY), lambda i: (0, 0, i))],
        out_specs=(pl.BlockSpec((seqs, tokens, part), lambda i: (0, 0, i)),) + (piece_spec,) * 3,
        compiler_params=pltpu.CompilerParams(vmem_limit_bytes=VMEM_LIMIT),
    )(at, values)


def turn_kernel(at_ref, own_ref, *refs):
    *pieces, basis_ref, out_ref = refs
    y, core = at_ref[0], at_ref[1]
    tokens = own_ref.shape[1]
    rows = [own_ref[0], own_ref[1]] + [piece[...] for piece in pieces]
    product = jnp.dot(
        jnp.concatenate(rows, axis=0), basis_ref[...], preferred_element_type=jnp.float32
    )
    places = [(0, y), (1, y)]
    for seq in (core, 1 - core):
        places += [(seq, lax.rem(y + steps, NY)) for steps in (3, 1, 2)]
    for i, (seq, source) in enumerate(places):
        out_ref[seq, source] = product[i * tokens : (i + 1) * tokens]


def turn(at, own, pieces, basis):
    seqs, tokens, _ = own.shape
    cols = basis.shape[1]
    out = pl.pallas_call(
        turn_kernel,
        out_shape=jax.ShapeDtypeStruct((seqs, NY, tokens, cols), jnp.float32),
        in_specs=[SCALARS] + [WHOLE] * (2 + len(pieces)),
        out_specs=WHOLE,
        compiler_params=pltpu.CompilerParams(vmem_limit_bytes=VMEM_LIMIT),
    )(at, own, *pieces, basis)
    return out.reshape(NY, -1, cols)


def outer_kernel(at_ref, mine_ref, other_ref, grads_ref, out_ref):
    core = at_ref[1]
    grads = grads_ref[...]
    for acts, place in ((mine_ref, core), (other_ref, 1 - core)):
        product = lax.dot_general(
            acts[...], grads, (((0,), (0,)), ((), ())), preferred_element_type=jnp.float32
        )
        out_ref[place] = product.astype(out_ref.dtype)


def outer_product(at, mine, other, grads):
    out = pl.pallas_call(
        outer_kernel,
        out_shape=jax.ShapeDtypeStruct((NC, mine.shape[1], grads.shape[1]), jnp.bfloat16),
        in_specs=[SCALARS] + [WHOLE] * 3,
        out_specs=WHOLE,
        compiler_params=pltpu.CompilerParams(vmem_limit_bytes=VMEM_LIMIT),
    )(at, mine, other, grads)
    return out.reshape(NY, -1, grads.shape[1])


def move_tokens(at, values):
    own, to_after, to_before, to_across = cut_features(at, values)
    mine = [ring_y(to_after, 1), ring_y(to_before, -1), ring_y(to_across, 2)]
    return own, mine + [swap_cores(v) for v in mine]


def scatter_sum(parts):
    return jnp.sum(lax.all_to_all(parts, Y, 0, 0), axis=0).astype(jnp.bfloat16)


def local(activations, out_grads, act_basis, grad_basis):
    at = jnp.stack([lax.axis_index(Y), lax.axis_index(C)]).astype(jnp.int32)
    act_rows = lax.all_gather(act_basis, Z, axis=0, tiled=True)
    grad_rows = lax.all_gather(grad_basis, Z, axis=0, tiled=True)
    act_own, act_pieces = move_tokens(at, activations)
    grad_own, grad_pieces = move_tokens(at, out_grads)

    act_turned = scatter_sum(turn(at, act_own, act_pieces, act_rows))
    grad_turned = scatter_sum(turn(at, grad_own, grad_pieces, grad_rows))

    grad_panel = lax.all_gather(grad_turned, Z, axis=0, tiled=True)
    act_panel = spread(transpose_planes(act_turned), (X, H), NX * NH)
    act_panel = act_panel.reshape(-1, act_basis.shape[1])

    outer = outer_product(at, act_panel, swap_cores(act_panel), grad_panel)
    got = lax.all_to_all(outer, Y, 0, 0).astype(jnp.float32)
    first, second = got[0] + got[1], got[2] + got[3]
    count = activations.shape[0] * activations.shape[1] * NZ * NY
    return ((first * first + second * second) / count).T


def solution(mesh):
    fine = Mesh(mesh.devices.reshape(NZ, NY, NX, NH, NC), (Z, Y, X, H, C))
    dp, tensor = (Z, Y), (X, H, C)
    placed = (P(None, dp, None), P(None, dp, None), P(dp, tensor), P(dp, tensor))
    return jax.shard_map(
        local, mesh=fine, in_specs=placed, out_specs=P(tensor, dp), check_vma=False
    )
```

time: 601 us -> 212 us (0.35)
  waiting for transfers between devices: 477 us -> 83 us
  starting transfers between devices: 0.12 us -> 61.5 us
  blocking collectives: 66 us -> 39.3 us
  local copies, waits for them, and re-layouts: 31.1 us -> 5.19 us
  matrix products: 11.9 us -> 0 us
  Pallas kernels: 0 us -> 7.96 us
    all_gather x4 -> x2, waiting for transfers between devices: 476 us -> 19.4 us  [the longest x1 19.4 us: local(): act_rows = lax.all_gather(act_basis, Z, axis=0, tiled=True)]
    all_to_all x1, blocking collectives: 66 us -> 11.5 us  [local(): got = lax.all_to_all(outer, Y, 0, 0).astype(jnp.float32)]
    ppermute x0 -> x14, starting transfers between devices: none -> 38.1 us  [the longest x6 19.7 us: ring_y(): return lax.ppermute(v, (Y, H), pairs)]
    ppermute x0 -> x14, waiting for transfers between devices: none -> 34.4 us  [the longest x6 23.1 us: ring_y(): return lax.ppermute(v, (Y, H), pairs)]
    all_to_all x0 -> x3, waiting for transfers between devices: none -> 27.8 us  [the longest x2 27.8 us: scatter_sum(): return jnp.sum(lax.all_to_all(parts, Y, 0, 0), axis=0).astype(jnp.bfloat16)]
    all_gather x0 -> x1, blocking collectives: none -> 27.8 us  [local(): grad_panel = lax.all_gather(grad_turned, Z, axis=0, tiled=True)]
    all_to_all x0 -> x3, starting transfers between devices: none -> 23.4 us  [the longest x1 13.5 us: spread(): lax.all_to_all(jnp.broadcast_to(v[None], (count,) + v.shape), axes, 0, 0)]
    dot_general x3 -> x0, matrix products: 11.9 us -> none  [the longest x2 8.85 us: gather_moments(): return jnp.dot(operand_entry, piece, preferred_element_type=jnp.float32)]
  transfers between devices with their start and end apart: 4 -> 19, of which waited for: 4 -> 9; matrix products, arithmetic and copies ran while one was open for 7% -> 1% of each run, Pallas kernels for 0% -> 2%
where the time goes in v1:
time: 212 us
  waiting for transfers between devices  83 us (39%)
  starting transfers between devices  61.5 us (29%)
  blocking collectives  39.3 us (19%)
  between operations  13.6 us (6%)
  Pallas kernels  7.96 us (4%)
  local copies, waits for them, and re-layouts  5.19 us (2%)
    all_to_all x2, waiting for transfers between devices, scatter_sum(): return jnp.sum(lax.all_to_all(parts, Y, 0, 0), axis=0).astype(jnp.bfloat16)  27.8 us
    all_gather x1, blocking collectives, local(): grad_panel = lax.all_gather(grad_turned, Z, axis=0, tiled=True)  27.8 us
    ppermute x6, waiting for transfers between devices, ring_y(): return lax.ppermute(v, (Y, H), pairs)  23.1 us
    ppermute x6, starting transfers between devices, ring_y(): return lax.ppermute(v, (Y, H), pairs)  19.7 us
    all_gather x1, waiting for transfers between devices, local(): act_rows = lax.all_gather(act_basis, Z, axis=0, tiled=True)  19.4 us
    ppermute x7, starting transfers between devices, swap_cores(): return lax.ppermute(v, C, [(0, 1), (1, 0)])  14.4 us
    all_to_all x1, starting transfers between devices, spread(): lax.all_to_all(jnp.broadcast_to(v[None], (count,) + v.shape), axes, 0, 0)  13.5 us
    all_to_all x1, blocking collectives, local(): got = lax.all_to_all(outer, Y, 0, 0).astype(jnp.float32)  11.5 us
  transfers between devices with their start and end apart: 19, of which 9 were waited for; matrix products, arithmetic and copies ran while one was open for 1% of the time, Pallas kernels for 2%

profile of v1, /device:TPU:6, one launch (start us, length us, event | category | flops | bytes accessed | tf_op | source)
XLA Modules:
  0.0 211.5 jit_solution(8368333221861008460)
XLA Ops:
  6.5 0.0 all-gather.3.cloned.1.call-start
  6.5 0.7 all-gather.3.cloned.1.call-update
  7.3 0.1 pad_add_fusion.at_ref
  7.3 0.0 copy-start
  7.3 1.6 copy-done
  8.9 1.0 shard_map.46
  10.0 3.5 %collective-permute-start = (bf16[64,2048]{1,0:T(8,128)(2,1)S(1)}, bf16[64,2048]{1,0:T(8,128)(2,1)S(1)}, u32[]{:S(2)}, u32[]{:S(2)}) collective-permute-start(bf16[64,2048]{1,0:T(8,128)(2,1)S(1)} %get-tuple-element.14), channel_id=1, source_target_pairs={{0,16},{16,32},{32,48},{48,2},{2,18},{18,34},{34,50},{50,0},{1,17}... | collective-permute-start | bytes 786440 | tf_op jit(solution)/shard_map/ppermute | solution.py:25
  13.5 3.8 %collective-permute-start.1 = (bf16[64,2048]{1,0:T(8,128)(2,1)S(1)}, bf16[64,2048]{1,0:T(8,128)(2,1)S(1)}, u32[]{:S(2)}, u32[]{:S(2)}) collective-permute-start(bf16[64,2048]{1,0:T(8,128)(2,1)S(1)} %get-tuple-element.15), channel_id=1, source_target_pairs={{0,50},{16,0},{32,16},{48,32},{2,48},{18,2},{34,18},{50,34},{1,51}... | collective-permute-start | bytes 786440 | tf_op jit(solution)/shard_map/ppermute | solution.py:25
  17.3 3.0 %collective-permute-start.2 = (bf16[64,2048]{1,0:T(8,128)(2,1)S(1)}, bf16[64,2048]{1,0:T(8,128)(2,1)S(1)}, u32[]{:S(2)}, u32[]{:S(2)}) collective-permute-start(bf16[64,2048]{1,0:T(8,128)(2,1)S(1)} %get-tuple-element.16), channel_id=1, source_target_pairs={{0,32},{16,48},{32,2},{48,18},{2,34},{18,50},{34,0},{50,16},{1,33}... | collective-permute-start | bytes 786440 | tf_op jit(solution)/shard_map/ppermute | solution.py:25
  20.3 1.3 collective-permute-done.refs_0_
  21.7 1.9 collective-permute-start.3
  23.6 0.0 collective-permute-done.1.refs_1_
  23.6 2.4 %collective-permute-start.4 = (bf16[64,2048]{1,0:T(8,128)(2,1)S(1)}, bf16[64,2048]{1,0:T(8,128)(2,1)S(1)}, u32[]{:S(2)}, u32[]{:S(2)}) collective-permute-start(bf16[64,2048]{1,0:T(8,128)(2,1)S(1)} %collective-permute-done.1.refs_1_), channel_id=1, source_target_pairs={{0,1},{1,0},{2,3},{3,2},{4,5},{5,4},{6,7},{7,6},{8,9},{9,8},{10,11... | collective-permute-start | bytes 786440 | tf_op jit(solution)/shard_map/ppermute | solution.py:17
  26.0 8.7 %collective-permute-done.2.refs_2_ = bf16[64,2048]{1,0:T(8,128)(2,1)S(1)} collective-permute-done((bf16[64,2048]{1,0:T(8,128)(2,1)S(1)}, bf16[64,2048]{1,0:T(8,128)(2,1)S(1)}, u32[]{:S(2)}, u32[]{:S(2)}) %collective-permute-start.2) | collective-permute-done | bytes 262176 | tf_op jit(solution)/shard_map/ppermute | solution.py:25
  34.7 1.9 collective-permute-start.5
  36.7 0.0 collective-permute-done.3.refs_3_
  36.7 0.0 collective-permute-done.4.refs_4_
  36.7 1.5 collective-permute-done.5.refs_5_
  38.2 19.4 %all-gather.3.cloned.1.call-done.refs_6_ = bf16[2048,384]{1,0:T(8,128)(2,1)} async-done(((bf16[256,384]{1,0:T(8,128)(2,1)}), bf16[2048,384]{1,0:T(8,128)(2,1)}) %all-gather.3.cloned.1.call-update) | async-done | bytes 1572880 | tf_op jit(solution)/shard_map/all_gather | solution.py:135
  57.5 0.0 copy-start.2
  57.5 1.4 copy-done.2
  58.9 2.7 %shard_map.47 = f32[2,4,64,384]{3,2,1,0:T(8,128)} custom-call(s32[2]{0:T(128)S(1)} %pad_add_fusion.at_ref, bf16[2,64,2048]{2,1,0:T(8,128)(2,1)S(1)} %get-tuple-element.13.own_ref, bf16[64,2048]{1,0:T(8,128)(2,1)S(1)} %collective-permute-done.refs_0_, bf16[64,2048]{1,0:T(8,128)(2,1)S(1)} %collective-permute-done.1.refs_1_, ...), custom_call_target="tpu_custom_call" | custom-call | tf_op jit(solution)/shard_map/pallas_call | solution.py:92
  61.6 4.6 %all-to-all-start = ((f32[4,128,384]{2,1,0:T(8,128)}), f32[4,128,384]{2,1,0:T(8,128)S(1)}, u32[]{:S(2)}, u32[]{:S(2)}) async-start(f32[4,128,384]{2,1,0:T(8,128)} %bitcast.2), calls=%async_computation | async-start | bytes 1572864 | tf_op jit(solution)/shard_map/all_to_all | solution.py:130
  66.2 0.0 copy-start.1
  66.2 0.0 all-gather.5.cloned.1.call-start
  66.2 0.7 all-gather.5.cloned.1.call-update
  66.9 15.0 %all-to-all-done = f32[4,128,384]{2,1,0:T(8,128)S(1)} async-done(((f32[4,128,384]{2,1,0:T(8,128)}), f32[4,128,384]{2,1,0:T(8,128)S(1)}, u32[]{:S(2)}, u32[]{:S(2)}) %all-to-all-start) | async-done | bytes 786464 | tf_op jit(solution)/shard_map/all_to_all | solution.py:130
  82.0 4.0 %collective-permute-start.6 = (bf16[128,384]{1,0:T(8,128)(2,1)S(1)}, bf16[128,384]{1,0:T(8,128)(2,1)S(1)}, u32[]{:S(2)}, u32[]{:S(2)}) collective-permute-start(bf16[128,384]{1,0:T(8,128)(2,1)S(1)} %reduce_sum.18), channel_id=1, source_target_pairs={{0,0},{2,64},{4,128},{6,192},{8,256},{10,320},{12,384},{14,448},{6... | collective-permute-start | bytes 294920 | tf_op jit(solution)/shard_map/ppermute | solution.py:33
  85.9 8.3 %collective-permute-done.6 = bf16[128,384]{1,0:T(8,128)(2,1)S(1)} collective-permute-done((bf16[128,384]{1,0:T(8,128)(2,1)S(1)}, bf16[128,384]{1,0:T(8,128)(2,1)S(1)}, u32[]{:S(2)}, u32[]{:S(2)}) %collective-permute-start.6) | collective-permute-done | bytes 98336 | tf_op jit(solution)/shard_map/ppermute | solution.py:33
  94.2 1.0 broadcast_in_dim.2
  95.2 13.5 %all-to-all-start.1 = ((bf16[8,128,384]{2,1,0:T(8,128)(2,1)}), bf16[8,128,384]{2,1,0:T(8,128)(2,1)S(1)}, u32[]{:S(2)}, u32[]{:S(2)}) async-start(bf16[8,128,384]{2,1,0:T(8,128)(2,1)} %broadcast_in_dim.2), calls=%async_computation.1 | async-start | bytes 1572864 | tf_op jit(solution)/shard_map/all_to_all | solution.py:37
  108.6 0.0 copy-done.1
  108.6 1.0 shard_map.48
  109.7 1.9 collective-permute-start.8
  111.6 5.6 %collective-permute-start.9 = (bf16[64,2048]{1,0:T(8,128)(2,1)S(1)}, bf16[64,2048]{1,0:T(8,128)(2,1)S(1)}, u32[]{:S(2)}, u32[]{:S(2)}) collective-permute-start(bf16[64,2048]{1,0:T(8,128)(2,1)S(1)} %get-tuple-element.19), channel_id=1, source_target_pairs={{0,50},{16,0},{32,16},{48,32},{2,48},{18,2},{34,18},{50,34},{1,51}... | collective-permute-start | bytes 786440 | tf_op jit(solution)/shard_map/ppermute | solution.py:25
  117.2 1.9 collective-permute-start.10
  119.1 13.0 %collective-permute-done.8.refs_0_ = bf16[64,2048]{1,0:T(8,128)(2,1)S(1)} collective-permute-done((bf16[64,2048]{1,0:T(8,128)(2,1)S(1)}, bf16[64,2048]{1,0:T(8,128)(2,1)S(1)}, u32[]{:S(2)}, u32[]{:S(2)}) %collective-permute-start.8) | collective-permute-done | bytes 262176 | tf_op jit(solution)/shard_map/ppermute | solution.py:25
  132.2 1.9 collective-permute-start.11
  134.1 0.0 collective-permute-done.9.refs_1_
  134.1 2.4 %collective-permute-start.12 = (bf16[64,2048]{1,0:T(8,128)(2,1)S(1)}, bf16[64,2048]{1,0:T(8,128)(2,1)S(1)}, u32[]{:S(2)}, u32[]{:S(2)}) collective-permute-start(bf16[64,2048]{1,0:T(8,128)(2,1)S(1)} %collective-permute-done.9.refs_1_), channel_id=1, source_target_pairs={{0,1},{1,0},{2,3},{3,2},{4,5},{5,4},{6,7},{7,6},{8,9},{9,8},{10,11... | collective-permute-start | bytes 786440 | tf_op jit(solution)/shard_map/ppermute | solution.py:17
  136.5 0.0 collective-permute-done.10.refs_2_
  136.5 1.9 collective-permute-start.13
  138.4 0.0 collective-permute-done.11.refs_3_
  138.4 0.0 collective-permute-done.12.refs_4_
  138.5 1.5 collective-permute-done.13.refs_5_
  139.9 0.0 all-gather.5.cloned.1.call-done.refs_6_
  139.9 0.0 copy-start.3
  139.9 1.2 copy-done.3
  141.2 2.0 shard_map.49
  143.2 0.0 all-to-all-done.1
  143.2 5.4 %all-to-all-start.2 = ((f32[4,128,256]{2,1,0:T(8,128)}), f32[4,128,256]{2,1,0:T(8,128)S(1)}, u32[]{:S(2)}, u32[]{:S(2)}) async-start(f32[4,128,256]{2,1,0:T(8,128)} %bitcast.4), calls=%async_computation.2 | async-start | bytes 1048576 | tf_op jit(solution)/shard_map/all_to_all | solution.py:130
  148.6 1.9 collective-permute-start.7
  150.5 12.9 %all-to-all-done.2 = f32[4,128,256]{2,1,0:T(8,128)S(1)} async-done(((f32[4,128,256]{2,1,0:T(8,128)}), f32[4,128,256]{2,1,0:T(8,128)S(1)}, u32[]{:S(2)}, u32[]{:S(2)}) %all-to-all-start.2) | async-done | bytes 524320 | tf_op jit(solution)/shard_map/all_to_all | solution.py:130
  163.4 27.8 %all_gather.11.grads_ref = bf16[1024,256]{1,0:T(8,128)(2,1)S(1)} all-gather(bf16[128,256]{1,0:T(8,128)(2,1)S(1)} %reduce_sum.19), channel_id=1, replica_groups=mesh['z'=8,'y'=4,'x'=4,'h'=2,'c'=2] {'z'}, dimensions={0}, use_global_device_ids=true | all-gather | bytes 589824 | tf_op jit(solution)/shard_map/all_gather | solution.py:143
  191.2 0.0 collective-permute-done.7.other_ref
  191.2 1.1 shard_map.50
  192.4 11.5 %all_to_all.20 = bf16[4,192,256]{2,1,0:T(8,128)(2,1)S(1)} all-to-all(bf16[4,192,256]{2,1,0:T(8,128)(2,1)S(1)} %bitcast.12), channel_id=1, replica_groups=mesh['z'=8,'y'=4,'x'=4,'h'=2,'c'=2] {'y'}, dimensions={0} | all-to-all | bytes 786432 | tf_op jit(solution)/shard_map/all_to_all | solution.py:148
  203.9 0.1 convert_element_type.11
  203.9 0.7 fusion.3
  (2 shorter events, 0.1 us)
Async XLA Ops:
  6.5 51.0 %all-gather.3.cloned.1.call-start = ((), (), s32[]{:S(2)}) async-start(), calls=%async_computation.4 | async-start | bytes 1769472 | tf_op jit(solution)/shard_map/all_gather | solution.py:135
  7.3 1.6 copy-start
  10.0 11.7 %collective-permute-start = (bf16[64,2048]{1,0:T(8,128)(2,1)S(1)}, bf16[64,2048]{1,0:T(8,128)(2,1)S(1)}, u32[]{:S(2)}, u32[]{:S(2)}) collective-permute-start(bf16[64,2048]{1,0:T(8,128)(2,1)S(1)} %get-tuple-element.14), channel_id=1, source_target_pairs={{0,16},{16,32},{32,48},{48,2},{2,18},{18,34},{34,50},{50,0},{1,17}... | collective-permute-start | bytes 786440 | tf_op jit(solution)/shard_map/ppermute | solution.py:25
  13.5 10.1 %collective-permute-start.1 = (bf16[64,2048]{1,0:T(8,128)(2,1)S(1)}, bf16[64,2048]{1,0:T(8,128)(2,1)S(1)}, u32[]{:S(2)}, u32[]{:S(2)}) collective-permute-start(bf16[64,2048]{1,0:T(8,128)(2,1)S(1)} %get-tuple-element.15), channel_id=1, source_target_pairs={{0,50},{16,0},{32,16},{48,32},{2,48},{18,2},{34,18},{50,34},{1,51}... | collective-permute-start | bytes 786440 | tf_op jit(solution)/shard_map/ppermute | solution.py:25
  17.3 17.4 %collective-permute-start.2 = (bf16[64,2048]{1,0:T(8,128)(2,1)S(1)}, bf16[64,2048]{1,0:T(8,128)(2,1)S(1)}, u32[]{:S(2)}, u32[]{:S(2)}) collective-permute-start(bf16[64,2048]{1,0:T(8,128)(2,1)S(1)} %get-tuple-element.16), channel_id=1, source_target_pairs={{0,32},{16,48},{32,2},{48,18},{2,34},{18,50},{34,0},{50,16},{1,33}... | collective-permute-start | bytes 786440 | tf_op jit(solution)/shard_map/ppermute | solution.py:25
  21.7 15.0 %collective-permute-start.3 = (bf16[64,2048]{1,0:T(8,128)(2,1)S(1)}, bf16[64,2048]{1,0:T(8,128)(2,1)S(1)}, u32[]{:S(2)}, u32[]{:S(2)}) collective-permute-start(bf16[64,2048]{1,0:T(8,128)(2,1)S(1)} %collective-permute-done.refs_0_), channel_id=1, source_target_pairs={{0,1},{1,0},{2,3},{3,2},{4,5},{5,4},{6,7},{7,6},{8,9},{9,8},{10,11... | collective-permute-start | bytes 786440 | tf_op jit(solution)/shard_map/ppermute | solution.py:17
  23.6 13.1 %collective-permute-start.4 = (bf16[64,2048]{1,0:T(8,128)(2,1)S(1)}, bf16[64,2048]{1,0:T(8,128)(2,1)S(1)}, u32[]{:S(2)}, u32[]{:S(2)}) collective-permute-start(bf16[64,2048]{1,0:T(8,128)(2,1)S(1)} %collective-permute-done.1.refs_1_), channel_id=1, source_target_pairs={{0,1},{1,0},{2,3},{3,2},{4,5},{5,4},{6,7},{7,6},{8,9},{9,8},{10,11... | collective-permute-start | bytes 786440 | tf_op jit(solution)/shard_map/ppermute | solution.py:17
  34.7 3.4 %collective-permute-start.5 = (bf16[64,2048]{1,0:T(8,128)(2,1)S(1)}, bf16[64,2048]{1,0:T(8,128)(2,1)S(1)}, u32[]{:S(2)}, u32[]{:S(2)}) collective-permute-start(bf16[64,2048]{1,0:T(8,128)(2,1)S(1)} %collective-permute-done.2.refs_2_), channel_id=1, source_target_pairs={{0,1},{1,0},{2,3},{3,2},{4,5},{5,4},{6,7},{7,6},{8,9},{9,8},{10,11... | collective-permute-start | bytes 786440 | tf_op jit(solution)/shard_map/ppermute | solution.py:17
  57.5 1.4 copy-start.2
  61.6 20.3 %all-to-all-start = ((f32[4,128,384]{2,1,0:T(8,128)}), f32[4,128,384]{2,1,0:T(8,128)S(1)}, u32[]{:S(2)}, u32[]{:S(2)}) async-start(f32[4,128,384]{2,1,0:T(8,128)} %bitcast.2), calls=%async_computation | async-start | bytes 1572864 | tf_op jit(solution)/shard_map/all_to_all | solution.py:130
  66.2 42.4 %copy-start.1 = (bf16[2,64,8192]{2,1,0:T(8,128)(2,1)S(1)}, bf16[2,64,8192]{2,1,0:T(8,128)(2,1)}, u32[]{:S(2)}) copy-start(bf16[2,64,8192]{2,1,0:T(8,128)(2,1)} %v_ref.3) | copy-start | bytes 6291460
  66.2 73.7 %all-gather.5.cloned.1.call-start = ((), (), s32[]{:S(2)}) async-start(), calls=%async_computation.5 | async-start | bytes 1179648 | tf_op jit(solution)/shard_map/all_gather | solution.py:136
  82.0 12.2 %collective-permute-start.6 = (bf16[128,384]{1,0:T(8,128)(2,1)S(1)}, bf16[128,384]{1,0:T(8,128)(2,1)S(1)}, u32[]{:S(2)}, u32[]{:S(2)}) collective-permute-start(bf16[128,384]{1,0:T(8,128)(2,1)S(1)} %reduce_sum.18), channel_id=1, source_target_pairs={{0,0},{2,64},{4,128},{6,192},{8,256},{10,320},{12,384},{14,448},{6... | collective-permute-start | bytes 294920 | tf_op jit(solution)/shard_map/ppermute | solution.py:33
  95.2 48.1 %all-to-all-start.1 = ((bf16[8,128,384]{2,1,0:T(8,128)(2,1)}), bf16[8,128,384]{2,1,0:T(8,128)(2,1)S(1)}, u32[]{:S(2)}, u32[]{:S(2)}) async-start(bf16[8,128,384]{2,1,0:T(8,128)(2,1)} %broadcast_in_dim.2), calls=%async_computation.1 | async-start | bytes 1572864 | tf_op jit(solution)/shard_map/all_to_all | solution.py:37
  109.7 22.5 %collective-permute-start.8 = (bf16[64,2048]{1,0:T(8,128)(2,1)S(1)}, bf16[64,2048]{1,0:T(8,128)(2,1)S(1)}, u32[]{:S(2)}, u32[]{:S(2)}) collective-permute-start(bf16[64,2048]{1,0:T(8,128)(2,1)S(1)} %get-tuple-element.18), channel_id=1, source_target_pairs={{0,16},{16,32},{32,48},{48,2},{2,18},{18,34},{34,50},{50,0},{1,17}... | collective-permute-start | bytes 786440 | tf_op jit(solution)/shard_map/ppermute | solution.py:25
  111.6 22.5 %collective-permute-start.9 = (bf16[64,2048]{1,0:T(8,128)(2,1)S(1)}, bf16[64,2048]{1,0:T(8,128)(2,1)S(1)}, u32[]{:S(2)}, u32[]{:S(2)}) collective-permute-start(bf16[64,2048]{1,0:T(8,128)(2,1)S(1)} %get-tuple-element.19), channel_id=1, source_target_pairs={{0,50},{16,0},{32,16},{48,32},{2,48},{18,2},{34,18},{50,34},{1,51}... | collective-permute-start | bytes 786440 | tf_op jit(solution)/shard_map/ppermute | solution.py:25
  117.2 19.3 %collective-permute-start.10 = (bf16[64,2048]{1,0:T(8,128)(2,1)S(1)}, bf16[64,2048]{1,0:T(8,128)(2,1)S(1)}, u32[]{:S(2)}, u32[]{:S(2)}) collective-permute-start(bf16[64,2048]{1,0:T(8,128)(2,1)S(1)} %get-tuple-element.20), channel_id=1, source_target_pairs={{0,32},{16,48},{32,2},{48,18},{2,34},{18,50},{34,0},{50,16},{1,33}... | collective-permute-start | bytes 786440 | tf_op jit(solution)/shard_map/ppermute | solution.py:25
  132.2 6.3 %collective-permute-start.11 = (bf16[64,2048]{1,0:T(8,128)(2,1)S(1)}, bf16[64,2048]{1,0:T(8,128)(2,1)S(1)}, u32[]{:S(2)}, u32[]{:S(2)}) collective-permute-start(bf16[64,2048]{1,0:T(8,128)(2,1)S(1)} %collective-permute-done.8.refs_0_), channel_id=1, source_target_pairs={{0,1},{1,0},{2,3},{3,2},{4,5},{5,4},{6,7},{7,6},{8,9},{9,8},{10,11... | collective-permute-start | bytes 786440 | tf_op jit(solution)/shard_map/ppermute | solution.py:17
  134.1 4.4 %collective-permute-start.12 = (bf16[64,2048]{1,0:T(8,128)(2,1)S(1)}, bf16[64,2048]{1,0:T(8,128)(2,1)S(1)}, u32[]{:S(2)}, u32[]{:S(2)}) collective-permute-start(bf16[64,2048]{1,0:T(8,128)(2,1)S(1)} %collective-permute-done.9.refs_1_), channel_id=1, source_target_pairs={{0,1},{1,0},{2,3},{3,2},{4,5},{5,4},{6,7},{7,6},{8,9},{9,8},{10,11... | collective-permute-start | bytes 786440 | tf_op jit(solution)/shard_map/ppermute | solution.py:17
  136.5 3.4 %collective-permute-start.13 = (bf16[64,2048]{1,0:T(8,128)(2,1)S(1)}, bf16[64,2048]{1,0:T(8,128)(2,1)S(1)}, u32[]{:S(2)}, u32[]{:S(2)}) collective-permute-start(bf16[64,2048]{1,0:T(8,128)(2,1)S(1)} %collective-permute-done.10.refs_2_), channel_id=1, source_target_pairs={{0,1},{1,0},{2,3},{3,2},{4,5},{5,4},{6,7},{7,6},{8,9},{9,8},{10,11... | collective-permute-start | bytes 786440 | tf_op jit(solution)/shard_map/ppermute | solution.py:17
  139.9 1.2 copy-start.3
  143.2 20.2 %all-to-all-start.2 = ((f32[4,128,256]{2,1,0:T(8,128)}), f32[4,128,256]{2,1,0:T(8,128)S(1)}, u32[]{:S(2)}, u32[]{:S(2)}) async-start(f32[4,128,256]{2,1,0:T(8,128)} %bitcast.4), calls=%async_computation.2 | async-start | bytes 1048576 | tf_op jit(solution)/shard_map/all_to_all | solution.py:130
  148.6 42.6 %collective-permute-start.7 = (bf16[1024,384]{1,0:T(8,128)(2,1)S(1)}, bf16[1024,384]{1,0:T(8,128)(2,1)S(1)}, u32[]{:S(2)}, u32[]{:S(2)}) collective-permute-start(bf16[1024,384]{1,0:T(8,128)(2,1)S(1)} %bitcast.10), channel_id=1, source_target_pairs={{0,1},{1,0},{2,3},{3,2},{4,5},{5,4},{6,7},{7,6},{8,9},{9,8},{10,11... | collective-permute-start | bytes 2359304 | tf_op jit(solution)/shard_map/ppermute | solution.py:17
Sparse Core Ops, SparseCore 0:
  9.4 48.0 all-gather.2
  69.1 41.1 all-gather.4

commit v2 on v1

v2 whole, which is shorter than its diff:
```python
import jax
import jax.numpy as jnp
from jax import lax
from jax.experimental import pallas as pl
from jax.experimental.pallas import tpu as pltpu
from jax.sharding import Mesh, PartitionSpec as P

Z, Y, X, H, C = "z", "y", "x", "h", "c"
NZ, NY, NX, NH, NC = 8, 4, 4, 2, 2

VMEM_LIMIT = 40 * 2**20
SCALARS = pl.BlockSpec(memory_space=pltpu.SMEM)
WHOLE = pl.BlockSpec(memory_space=pltpu.VMEM)


def swap_cores(v):
    return lax.ppermute(v, C, [(0, 1), (1, 0)])


def ring_y(v, shift):
    pairs = []
    for at in range(NH * NY):
        to = (at + shift(at)) % (NH * NY)
        pairs.append((at % NY * NH + at // NY, to % NY * NH + to // NY))
    return lax.ppermute(v, (Y, H), pairs)


def ring_z(v, shift):
    return lax.ppermute(v, Z, [(at, (at + shift(at)) % NZ) for at in range(NZ)])


def one_way(step):
    return lambda at: step


def either_way(at):
    return 2 if at % 2 == 0 else -2


def transpose_planes(v, flip):
    pairs = []
    for z in range(NZ):
        for t in range(NX * NH):
            pairs.append((z * NX * NH + t, t * NX * NH + (z ^ flip)))
    return lax.ppermute(v, (Z, X, H), pairs)


def gather_z(v, z):
    left1, right1 = ring_z(v, one_way(1)), ring_z(v, one_way(-1))
    left2, right2 = ring_z(v, one_way(2)), ring_z(v, one_way(-2))
    left3, right3 = ring_z(left2, one_way(1)), ring_z(right2, one_way(-1))
    far = ring_z(jnp.where(z % 2 == 0, left2, right2), either_way)
    return [v, left1, right1, left2, right2, left3, right3, far]


STEPS_Z = (0, 7, 1, 6, 2, 5, 3, 4)


def spread(v, axes, count):
    return lax.all_to_all(jnp.broadcast_to(v[None], (count,) + v.shape), axes, 0, 0)


def cut_kernel(at_ref, acts_ref, grads_ref, own_ref, after_ref, before_ref, across_ref):
    y, core = at_ref[0], at_ref[1]
    width = own_ref.shape[3] // 2
    for z in range(2):
        for steps, out in ((0, own_ref), (1, after_ref), (3, before_ref), (2, across_ref)):
            block = z * NY + lax.rem(y + steps, NY)
            cols = pl.ds(pl.multiple_of(block * width, width), width)
            for i, values in enumerate((acts_ref, grads_ref)):
                if steps == 0:
                    out[i, :, :, z * width : (z + 1) * width] = values[:, :, cols]
                else:
                    out[i, :, z * width : (z + 1) * width] = values[core, :, cols]


def cut_features(at, acts, grads):
    seqs, tokens, features = acts.shape
    steps = NZ // 2
    part = features // NY // steps
    whole_spec = pl.BlockSpec((seqs, tokens, part * NY), lambda i: (0, 0, i))
    piece = jax.ShapeDtypeStruct((2, tokens, features // NY), acts.dtype)
    piece_spec = pl.BlockSpec((2, tokens, part), lambda i: (0, 0, i))
    return pl.pallas_call(
        cut_kernel,
        grid=(steps,),
        out_shape=(
            jax.ShapeDtypeStruct((2, seqs, tokens, features // NY), acts.dtype),
            piece,
            piece,
            piece,
        ),
        in_specs=[SCALARS, whole_spec, whole_spec],
        out_specs=(pl.BlockSpec((2, seqs, tokens, part), lambda i: (0, 0, 0, i)),)
        + (piece_spec,) * 3,
        compiler_params=pltpu.CompilerParams(vmem_limit_bytes=VMEM_LIMIT),
    )(at, acts, grads)


def turn_kernel(which, at_ref, own_ref, *refs):
    pieces, basis_refs, (out_ref, rows_ref) = refs[:6], refs[6:-2], refs[-2:]
    y, core, z = at_ref[0], at_ref[1], at_ref[2]
    tokens = own_ref.shape[2]
    rows = [own_ref[which, 0], own_ref[which, 1]] + [piece[which] for piece in pieces]
    if len(basis_refs) == 1:
        basis = basis_refs[0][...]
    else:
        depth = basis_refs[0].shape[0]
        for steps, part in zip(STEPS_Z, basis_refs):
            start = lax.rem(z + steps, NZ) * depth
            rows_ref[pl.ds(pl.multiple_of(start, depth), depth)] = part[...]
        basis = rows_ref[...]
    product = jnp.dot(
        jnp.concatenate(rows, axis=0), basis, preferred_element_type=jnp.float32
    )
    places = [(0, y), (1, y)]
    for seq in (core, 1 - core):
        places += [(seq, lax.rem(y + steps, NY)) for steps in (3, 1, 2)]
    for i, (seq, source) in enumerate(places):
        out_ref[seq, source] = product[i * tokens : (i + 1) * tokens]


def turn(which, at, own, pieces, bases):
    _, seqs, tokens, features = own.shape
    cols = bases[0].shape[1]
    out = pl.pallas_call(
        lambda *refs: turn_kernel(which, *refs),
        out_shape=jax.ShapeDtypeStruct((seqs, NY, tokens, cols), jnp.float32),
        in_specs=[SCALARS] + [WHOLE] * (1 + len(pieces) + len(bases)),
        out_specs=WHOLE,
        scratch_shapes=[pltpu.VMEM((features, cols), own.dtype)],
        compiler_params=pltpu.CompilerParams(vmem_limit_bytes=VMEM_LIMIT),
    )(at, own, *pieces, *bases)
    return out.reshape(NY, -1, cols)


def outer_kernel(at_ref, mine_ref, other_ref, grads_ref, out_ref):
    core = at_ref[1]
    grads = grads_ref[...]
    for acts, place in ((mine_ref, core), (other_ref, 1 - core)):
        product = lax.dot_general(
            acts[...], grads, (((0,), (0,)), ((), ())), preferred_element_type=jnp.float32
        )
        out_ref[place] = product.astype(out_ref.dtype)


def outer_product(at, mine, other, grads):
    out = pl.pallas_call(
        outer_kernel,
        out_shape=jax.ShapeDtypeStruct((NC, mine.shape[1], grads.shape[1]), jnp.bfloat16),
        in_specs=[SCALARS] + [WHOLE] * 3,
        out_specs=WHOLE,
        compiler_params=pltpu.CompilerParams(vmem_limit_bytes=VMEM_LIMIT),
    )(at, mine, other, grads)
    return out.reshape(NY, -1, grads.shape[1])


def scatter_sum(parts):
    return jnp.sum(lax.all_to_all(parts, Y, 0, 0), axis=0).astype(jnp.bfloat16)


def local(activations, out_grads, act_basis, grad_basis):
    z, h = lax.axis_index(Z), lax.axis_index(H)
    at = jnp.stack([lax.axis_index(Y), lax.axis_index(C), z]).astype(jnp.int32)
    act_rows = lax.all_gather(act_basis, Z, axis=0, tiled=True)

    own, to_after, to_before, to_across = cut_features(at, activations, out_grads)
    pieces = [
        ring_y(to_after, one_way(1)),
        ring_y(to_before, one_way(-1)),
        ring_y(to_across, either_way),
    ]
    pieces += [swap_cores(v) for v in pieces]
    grad_rows = gather_z(grad_basis, z)

    grad_turned = scatter_sum(turn(1, at, own, pieces, grad_rows))
    act_turned = scatter_sum(turn(0, at, own, pieces, [act_rows]))

    grad_panel = spread(grad_turned, Z, NZ).reshape(-1, grad_basis.shape[1])
    near, far = transpose_planes(act_turned, 0), transpose_planes(act_turned, 1)
    pair = jnp.where(h == 0, jnp.stack([near, far]), jnp.stack([far, near]))
    act_panel = spread(pair, X, NX).reshape(-1, act_basis.shape[1])

    outer = outer_product(at, act_panel, swap_cores(act_panel), grad_panel)
    got = lax.all_to_all(outer, Y, 0, 0).astype(jnp.float32)
    first, second = got[0] + got[1], got[2] + got[3]
    count = activations.shape[0] * activations.shape[1] * NZ * NY
    return ((first * first + second * second) / count).T


def solution(mesh):
    fine = Mesh(mesh.devices.reshape(NZ, NY, NX, NH, NC), (Z, Y, X, H, C))
    dp, tensor = (Z, Y), (X, H, C)
    placed = (P(None, dp, None), P(None, dp, None), P(dp, tensor), P(dp, tensor))
    return jax.shard_map(
        local, mesh=fine, in_specs=placed, out_specs=P(tensor, dp), check_vma=False
    )
```

time: 212 us -> 191 us (0.901)
  waiting for transfers between devices: 83 us -> 53.2 us
  blocking collectives: 39.3 us -> 13.7 us
  starting transfers between devices: 61.5 us -> 86.8 us
  local copies, waits for them, and re-layouts: 5.19 us -> 12.2 us
    all_to_all x2, waiting for transfers between devices: 27.8 us -> 0.01 us  [scatter_sum(): return jnp.sum(lax.all_to_all(parts, Y, 0, 0), axis=0).astype(jnp.bfloat16)]
    all_gather x1 -> x0, blocking collectives: 27.8 us -> none  [local(): grad_panel = lax.all_gather(grad_turned, Z, axis=0, tiled=True)]
    ppermute x0 -> x7, starting transfers between devices: none -> 27.2 us  [ring_z(): return lax.ppermute(v, Z, [(at, (at + shift(at)) % NZ) for at in range(NZ)])]
    all_to_all x1 -> x2, waiting for transfers between devices: 0.01 us -> 18.8 us  [spread(): lax.all_to_all(jnp.broadcast_to(v[None], (count,) + v.shape), axes, 0, 0)]
    ppermute x1 -> x2, starting transfers between devices: 3.96 us -> 14.2 us  [transpose_planes(): return lax.ppermute(v, (Z, X, H), pairs)]
    all_gather x1, waiting for transfers between devices: 19.4 us -> 9.19 us  [local(): act_rows = lax.all_gather(act_basis, Z, axis=0, tiled=True)]
    ppermute x6 -> x3, starting transfers between devices: 19.7 us -> 10.3 us  [ring_y(): return lax.ppermute(v, (Y, H), pairs)]
    ppermute x7 -> x4, starting transfers between devices: 14.4 us -> 8.13 us  [swap_cores(): return lax.ppermute(v, C, [(0, 1), (1, 0)])]
  transfers between devices with their start and end apart: 19 -> 21, of which waited for: 9 -> 9; matrix products, arithmetic and copies ran while one was open for 1% -> 1% of each run, Pallas kernels for 2% -> 2%
where the time goes in v2:
time: 191 us; the launch traced here: 190 us
  starting transfers between devices  86.8 us (45%)
  waiting for transfers between devices  53.2 us (28%)
  blocking collectives  13.7 us (7%)
  between operations  13.7 us (7%)
  local copies, waits for them, and re-layouts  12.2 us (6%)
  Pallas kernels  7.85 us (4%)
  other arithmetic  2.13 us (1%)
    ppermute x7, starting transfers between devices, ring_z(): return lax.ppermute(v, Z, [(at, (at + shift(at)) % NZ) for at in range(NZ)])  27.2 us
    all_to_all x2, waiting for transfers between devices, spread(): lax.all_to_all(jnp.broadcast_to(v[None], (count,) + v.shape), axes, 0, 0)  18.8 us
    all_to_all x2, starting transfers between devices, spread(): lax.all_to_all(jnp.broadcast_to(v[None], (count,) + v.shape), axes, 0, 0)  17.5 us
    ppermute x3, waiting for transfers between devices, ring_y(): return lax.ppermute(v, (Y, H), pairs)  17.4 us
    ppermute x2, starting transfers between devices, transpose_planes(): return lax.ppermute(v, (Z, X, H), pairs)  14.2 us
    all_to_all x1, blocking collectives, local(): got = lax.all_to_all(outer, Y, 0, 0).astype(jnp.float32)  13.7 us
    unnamed x20, local copies, waits for them, and re-layouts  10.4 us
    ppermute x3, starting transfers between devices, ring_y(): return lax.ppermute(v, (Y, H), pairs)  10.3 us
  transfers between devices with their start and end apart: 21, of which 9 were waited for; matrix products, arithmetic and copies ran while one was open for 1% of the time, Pallas kernels for 2%

profile of v2, /device:TPU:6, one launch (start us, length us, event | category | flops | bytes accessed | tf_op | source)
XLA Modules:
  0.0 189.6 jit_solution(9477415008920365812)
XLA Ops:
  6.5 0.0 all-gather.2.cloned.1.call-start
  6.5 0.7 all-gather.2.cloned.1.call-update
  7.3 0.1 pad_add_fusion.at_ref.refs_0_
  7.3 1.6 copy-done
  8.9 1.6 copy-done.1
  10.5 1.4 shard_map.46
  11.9 3.5 %collective-permute-start = (bf16[2,64,2048]{2,1,0:T(8,128)(2,1)S(1)}, bf16[2,64,2048]{2,1,0:T(8,128)(2,1)S(1)}, u32[]{:S(2)}, u32[]{:S(2)}) collective-permute-start(bf16[2,64,2048]{2,1,0:T(8,128)(2,1)S(1)} %get-tuple-element.10), channel_id=1, source_target_pairs={{0,16},{16,32},{32,48},{48,2},{2,18},{18,34},{34,50},{50,0},{1,17}... | collective-permute-start | bytes 1572872 | tf_op jit(solution)/shard_map/ppermute | solution.py:25
  15.4 3.8 %collective-permute-start.1 = (bf16[2,64,2048]{2,1,0:T(8,128)(2,1)S(1)}, bf16[2,64,2048]{2,1,0:T(8,128)(2,1)S(1)}, u32[]{:S(2)}, u32[]{:S(2)}) collective-permute-start(bf16[2,64,2048]{2,1,0:T(8,128)(2,1)S(1)} %get-tuple-element.11), channel_id=1, source_target_pairs={{0,50},{16,0},{32,16},{48,32},{2,48},{18,2},{34,18},{50,34},{1,51}... | collective-permute-start | bytes 1572872 | tf_op jit(solution)/shard_map/ppermute | solution.py:25
  19.3 3.1 %collective-permute-start.2 = (bf16[2,64,2048]{2,1,0:T(8,128)(2,1)S(1)}, bf16[2,64,2048]{2,1,0:T(8,128)(2,1)S(1)}, u32[]{:S(2)}, u32[]{:S(2)}) collective-permute-start(bf16[2,64,2048]{2,1,0:T(8,128)(2,1)S(1)} %get-tuple-element.12), channel_id=1, source_target_pairs={{0,32},{16,50},{32,2},{48,16},{2,34},{18,48},{34,0},{50,18},{1,33}... | collective-permute-start | bytes 1572872 | tf_op jit(solution)/shard_map/ppermute | solution.py:25
  22.3 6.9 %collective-permute-done.refs_2_ = bf16[2,64,2048]{2,1,0:T(8,128)(2,1)S(1)} collective-permute-done((bf16[2,64,2048]{2,1,0:T(8,128)(2,1)S(1)}, bf16[2,64,2048]{2,1,0:T(8,128)(2,1)S(1)}, u32[]{:S(2)}, u32[]{:S(2)}) %collective-permute-start) | collective-permute-done | bytes 524320 | tf_op jit(solution)/shard_map/ppermute | solution.py:25
  29.2 1.9 %collective-permute-start.3 = (bf16[2,64,2048]{2,1,0:T(8,128)(2,1)S(1)}, bf16[2,64,2048]{2,1,0:T(8,128)(2,1)S(1)}, u32[]{:S(2)}, u32[]{:S(2)}) collective-permute-start(bf16[2,64,2048]{2,1,0:T(8,128)(2,1)S(1)} %collective-permute-done.refs_2_), channel_id=1, source_target_pairs={{0,1},{1,0},{2,3},{3,2},{4,5},{5,4},{6,7},{7,6},{8,9},{9,8},{10,11... | collective-permute-start | bytes 1572872 | tf_op jit(solution)/shard_map/ppermute | solution.py:17
  31.2 10.5 %collective-permute-done.1.refs_3_ = bf16[2,64,2048]{2,1,0:T(8,128)(2,1)S(1)} collective-permute-done((bf16[2,64,2048]{2,1,0:T(8,128)(2,1)S(1)}, bf16[2,64,2048]{2,1,0:T(8,128)(2,1)S(1)}, u32[]{:S(2)}, u32[]{:S(2)}) %collective-permute-start.1) | collective-permute-done | bytes 524320 | tf_op jit(solution)/shard_map/ppermute | solution.py:25
  41.7 1.9 %collective-permute-start.4 = (bf16[2,64,2048]{2,1,0:T(8,128)(2,1)S(1)}, bf16[2,64,2048]{2,1,0:T(8,128)(2,1)S(1)}, u32[]{:S(2)}, u32[]{:S(2)}) collective-permute-start(bf16[2,64,2048]{2,1,0:T(8,128)(2,1)S(1)} %collective-permute-done.1.refs_3_), channel_id=1, source_target_pairs={{0,1},{1,0},{2,3},{3,2},{4,5},{5,4},{6,7},{7,6},{8,9},{9,8},{10,11... | collective-permute-start | bytes 1572872 | tf_op jit(solution)/shard_map/ppermute | solution.py:17
  43.6 0.0 collective-permute-done.2.refs_4_
  43.6 2.4 %collective-permute-start.5 = (bf16[2,64,2048]{2,1,0:T(8,128)(2,1)S(1)}, bf16[2,64,2048]{2,1,0:T(8,128)(2,1)S(1)}, u32[]{:S(2)}, u32[]{:S(2)}) collective-permute-start(bf16[2,64,2048]{2,1,0:T(8,128)(2,1)S(1)} %collective-permute-done.2.refs_4_), channel_id=1, source_target_pairs={{0,1},{1,0},{2,3},{3,2},{4,5},{5,4},{6,7},{7,6},{8,9},{9,8},{10,11... | collective-permute-start | bytes 1572872 | tf_op jit(solution)/shard_map/ppermute | solution.py:17
  46.0 0.0 collective-permute-done.3.refs_5_
  46.0 0.0 collective-permute-done.4.refs_6_
  46.1 0.8 copy-done.2
  46.8 0.7 collective-permute-done.5.refs_7_
  47.5 0.8 copy-done.5
  48.4 9.2 %all-gather.2.cloned.1.call-done.refs_8_ = bf16[2048,384]{1,0:T(8,128)(2,1)} async-done(((bf16[256,384]{1,0:T(8,128)(2,1)}), bf16[2048,384]{1,0:T(8,128)(2,1)}) %all-gather.2.cloned.1.call-update) | async-done | bytes 1572880 | tf_op jit(solution)/shard_map/all_gather | solution.py:165
  57.5 1.0 copy-done.3
  58.6 1.0 copy-done.6
  59.6 1.4 copy-done.8
  61.0 2.7 %shard_map.47 = f32[2,4,64,384]{3,2,1,0:T(8,128)} custom-call(s32[3]{0:T(128)S(1)} %pad_add_fusion.at_ref.refs_0_, bf16[2,2,64,2048]{3,2,1,0:T(8,128)(2,1)S(1)} %get-tuple-element.9.refs_1_, bf16[2,64,2048]{2,1,0:T(8,128)(2,1)S(1)} %collective-permute-done.refs_2_, bf16[2,64,2048]{2,1,0:T(8,128)(2,1)S(1)} %collective-permute-done.1.refs_3_, ...), custom_call_target="tpu_custom_call" | custom-call | tf_op jit(solution)/shard_map/pallas_call | solution.py:126
  63.8 4.6 %all-to-all-start = ((f32[4,128,384]{2,1,0:T(8,128)}), f32[4,128,384]{2,1,0:T(8,128)}, u32[]{:S(2)}, u32[]{:S(2)}) async-start(f32[4,128,384]{2,1,0:T(8,128)} %bitcast.3), calls=%async_computation | async-start | bytes 1572864 | tf_op jit(solution)/shard_map/all_to_all | solution.py:159
  68.3 0.0 copy-done.9
  68.3 2.8 %collective-permute-start.11 = (bf16[256,256]{1,0:T(8,128)(2,1)S(1)}, bf16[256,256]{1,0:T(8,128)(2,1)S(1)}, u32[]{:S(2)}, u32[]{:S(2)}) collective-permute-start(bf16[256,256]{1,0:T(8,128)(2,1)S(1)} %copy-done.9), channel_id=1, source_target_pairs={{0,128},{64,192},{128,256},{192,320},{256,384},{320,448},{384,0},{... | collective-permute-start | bytes 393224 | tf_op jit(solution)/shard_map/ppermute | solution.py:29
  71.1 5.2 %collective-permute-start.12 = (bf16[256,256]{1,0:T(8,128)(2,1)S(1)}, bf16[256,256]{1,0:T(8,128)(2,1)S(1)}, u32[]{:S(2)}, u32[]{:S(2)}) collective-permute-start(bf16[256,256]{1,0:T(8,128)(2,1)S(1)} %copy-done.9), channel_id=1, source_target_pairs={{0,384},{64,448},{128,0},{192,64},{256,128},{320,192},{384,256},{4... | collective-permute-start | bytes 393224 | tf_op jit(solution)/shard_map/ppermute | solution.py:29
  76.3 3.5 %collective-permute-start.10 = (bf16[256,256]{1,0:T(8,128)(2,1)S(1)}, bf16[256,256]{1,0:T(8,128)(2,1)}, u32[]{:S(2)}, u32[]{:S(2)}) collective-permute-start(bf16[256,256]{1,0:T(8,128)(2,1)S(1)} %copy-done.9), channel_id=1, source_target_pairs={{0,448},{64,0},{128,64},{192,128},{256,192},{320,256},{384,320},{4... | collective-permute-start | bytes 393224 | tf_op jit(solution)/shard_map/ppermute | solution.py:29
  79.9 2.3 %collective-permute-start.9 = (bf16[256,256]{1,0:T(8,128)(2,1)S(1)}, bf16[256,256]{1,0:T(8,128)(2,1)}, u32[]{:S(2)}, u32[]{:S(2)}) collective-permute-start(bf16[256,256]{1,0:T(8,128)(2,1)S(1)} %copy-done.9), channel_id=1, source_target_pairs={{0,64},{64,128},{128,192},{192,256},{256,320},{320,384},{384,448},... | collective-permute-start | bytes 393224 | tf_op jit(solution)/shard_map/ppermute | solution.py:29
  82.2 0.0 collective-permute-done.11.refs_11_
  82.2 0.0 collective-permute-done.12.refs_12_
  82.2 6.4 %collective-permute-start.15 = (bf16[256,256]{1,0:T(8,128)(2,1)S(1)}, bf16[256,256]{1,0:T(8,128)(2,1)S(1)}, u32[]{:S(2)}, u32[]{:S(2)}) collective-permute-start(bf16[256,256]{1,0:T(8,128)(2,1)S(1)} %broadcast_select_fusion), channel_id=1, source_target_pairs={{0,128},{64,448},{128,256},{192,64},{256,384},{320,192},{384,0},{4... | collective-permute-start | bytes 393224 | tf_op jit(solution)/shard_map/ppermute | solution.py:29
  88.6 2.6 %collective-permute-start.13 = (bf16[256,256]{1,0:T(8,128)(2,1)S(1)}, bf16[256,256]{1,0:T(8,128)(2,1)S(1)}, u32[]{:S(2)}, u32[]{:S(2)}) collective-permute-start(bf16[256,256]{1,0:T(8,128)(2,1)S(1)} %collective-permute-done.11.refs_11_), channel_id=1, source_target_pairs={{0,64},{64,128},{128,192},{192,256},{256,320},{320,384},{384,448},... | collective-permute-start | bytes 393224 | tf_op jit(solution)/shard_map/ppermute | solution.py:29
  91.2 4.5 %collective-permute-start.14 = (bf16[256,256]{1,0:T(8,128)(2,1)S(1)}, bf16[256,256]{1,0:T(8,128)(2,1)S(1)}, u32[]{:S(2)}, u32[]{:S(2)}) collective-permute-start(bf16[256,256]{1,0:T(8,128)(2,1)S(1)} %collective-permute-done.12.refs_12_), channel_id=1, source_target_pairs={{0,448},{64,0},{128,64},{192,128},{256,192},{320,256},{384,320},{4... | collective-permute-start | bytes 393224 | tf_op jit(solution)/shard_map/ppermute | solution.py:29
  95.7 0.0 collective-permute-done.10.refs_10_
  95.7 0.0 collective-permute-done.9.refs_9_
  95.7 0.0 collective-permute-done.15.refs_15_
  95.7 1.0 collective-permute-done.13.refs_13_
  96.7 1.5 collective-permute-done.14.refs_14_
  98.2 1.0 copy-done.4
  99.2 1.0 copy-done.7
  100.3 2.6 %shard_map.48 = f32[2,4,64,256]{3,2,1,0:T(8,128)} custom-call(s32[3]{0:T(128)S(1)} %pad_add_fusion.at_ref.refs_0_, bf16[2,2,64,2048]{3,2,1,0:T(8,128)(2,1)S(1)} %get-tuple-element.9.refs_1_, bf16[2,64,2048]{2,1,0:T(8,128)(2,1)S(1)} %collective-permute-done.refs_2_, bf16[2,64,2048]{2,1,0:T(8,128)(2,1)S(1)} %collective-permute-done.1.refs_3_, ...), custom_call_target="tpu_custom_call" | custom-call | tf_op jit(solution)/shard_map/pallas_call | solution.py:126
  102.8 0.0 all-to-all-done
  102.8 4.9 %all-to-all-start.2 = ((f32[4,128,256]{2,1,0:T(8,128)}), f32[4,128,256]{2,1,0:T(8,128)S(1)}, u32[]{:S(2)}, u32[]{:S(2)}) async-start(f32[4,128,256]{2,1,0:T(8,128)} %bitcast.7), calls=%async_computation.2 | async-start | bytes 1048576 | tf_op jit(solution)/shard_map/all_to_all | solution.py:159
  107.7 1.2 reduce_sum.18
  108.9 3.8 %collective-permute-start.6 = (bf16[128,384]{1,0:T(8,128)(2,1)S(1)}, bf16[128,384]{1,0:T(8,128)(2,1)S(1)}, u32[]{:S(2)}, u32[]{:S(2)}) collective-permute-start(bf16[128,384]{1,0:T(8,128)(2,1)S(1)} %reduce_sum.18), channel_id=1, source_target_pairs={{0,0},{2,64},{4,128},{6,192},{8,256},{10,320},{12,384},{14,448},{6... | collective-permute-start | bytes 294920 | tf_op jit(solution)/shard_map/ppermute | solution.py:45
  112.7 10.4 %collective-permute-start.7 = (bf16[128,384]{1,0:T(8,128)(2,1)S(1)}, bf16[128,384]{1,0:T(8,128)(2,1)S(1)}, u32[]{:S(2)}, u32[]{:S(2)}) collective-permute-start(bf16[128,384]{1,0:T(8,128)(2,1)S(1)} %reduce_sum.18), channel_id=1, source_target_pairs={{0,2},{2,66},{4,130},{6,194},{8,258},{10,322},{12,386},{14,450},{6... | collective-permute-start | bytes 294920 | tf_op jit(solution)/shard_map/ppermute | solution.py:45
  123.1 0.0 collective-permute-done.6
  123.1 3.9 %collective-permute-done.7 = bf16[128,384]{1,0:T(8,128)(2,1)S(1)} collective-permute-done((bf16[128,384]{1,0:T(8,128)(2,1)S(1)}, bf16[128,384]{1,0:T(8,128)(2,1)S(1)}, u32[]{:S(2)}, u32[]{:S(2)}) %collective-permute-start.7) | collective-permute-done | bytes 98336 | tf_op jit(solution)/shard_map/ppermute | solution.py:45
  127.0 0.0 all-to-all-done.2
  127.0 1.0 broadcast_in_dim.4
  128.0 4.5 %all-to-all-start.1 = ((bf16[4,2,128,384]{3,2,1,0:T(8,128)(2,1)}), bf16[4,2,128,384]{3,2,1,0:T(8,128)(2,1)S(1)}, u32[]{:S(2)}, u32[]{:S(2)}) async-start(bf16[4,2,128,384]{3,2,1,0:T(8,128)(2,1)} %broadcast_in_dim.4), calls=%async_computation.1 | async-start | bytes 1572864 | tf_op jit(solution)/shard_map/all_to_all | solution.py:60
  132.5 7.4 %all-to-all-done.1 = bf16[4,2,128,384]{3,2,1,0:T(8,128)(2,1)S(1)} async-done(((bf16[4,2,128,384]{3,2,1,0:T(8,128)(2,1)}), bf16[4,2,128,384]{3,2,1,0:T(8,128)(2,1)S(1)}, u32[]{:S(2)}, u32[]{:S(2)}) %all-to-all-start.1) | async-done | bytes 786464 | tf_op jit(solution)/shard_map/all_to_all | solution.py:60
  139.9 0.8 broadcast_in_dim.5
  140.8 13.0 %all-to-all-start.3 = ((bf16[8,128,256]{2,1,0:T(8,128)(2,1)}), bf16[8,128,256]{2,1,0:T(8,128)(2,1)S(1)}, u32[]{:S(2)}, u32[]{:S(2)}) async-start(bf16[8,128,256]{2,1,0:T(8,128)(2,1)} %broadcast_in_dim.5), calls=%async_computation.3 | async-start | bytes 1048576 | tf_op jit(solution)/shard_map/all_to_all | solution.py:60
  153.7 1.9 %collective-permute-start.8 = (bf16[1024,384]{1,0:T(8,128)(2,1)S(1)}, bf16[1024,384]{1,0:T(8,128)(2,1)S(1)}, u32[]{:S(2)}, u32[]{:S(2)}) collective-permute-start(bf16[1024,384]{1,0:T(8,128)(2,1)S(1)} %bitcast.14), channel_id=1, source_target_pairs={{0,1},{1,0},{2,3},{3,2},{4,5},{5,4},{6,7},{7,6},{8,9},{9,8},{10,11... | collective-permute-start | bytes 2359304 | tf_op jit(solution)/shard_map/ppermute | solution.py:17
  155.7 11.4 %all-to-all-done.3 = bf16[8,128,256]{2,1,0:T(8,128)(2,1)S(1)} async-done(((bf16[8,128,256]{2,1,0:T(8,128)(2,1)}), bf16[8,128,256]{2,1,0:T(8,128)(2,1)S(1)}, u32[]{:S(2)}, u32[]{:S(2)}) %all-to-all-start.3) | async-done | bytes 524320 | tf_op jit(solution)/shard_map/all_to_all | solution.py:60
  167.0 0.0 collective-permute-done.8.other_ref
  167.0 1.1 shard_map.49
  168.2 13.7 %all_to_all.25 = bf16[4,192,256]{2,1,0:T(8,128)(2,1)S(1)} all-to-all(bf16[4,192,256]{2,1,0:T(8,128)(2,1)S(1)} %bitcast.17), channel_id=1, replica_groups=mesh['z'=8,'y'=4,'x'=4,'h'=2,'c'=2] {'y'}, dimensions={0} | all-to-all | bytes 786432 | tf_op jit(solution)/shard_map/all_to_all | solution.py:185
  181.9 0.1 convert_element_type.15
  182.0 0.7 fusion.3
  (13 shorter events, 0.1 us)
Async XLA Ops:
  6.5 51.0 %all-gather.2.cloned.1.call-start = ((), (), s32[]{:S(2)}) async-start(), calls=%async_computation.5 | async-start | bytes 1769472 | tf_op jit(solution)/shard_map/all_gather | solution.py:165
  7.3 1.6 copy-start
  8.9 1.6 copy-start.1
  11.9 17.3 %collective-permute-start = (bf16[2,64,2048]{2,1,0:T(8,128)(2,1)S(1)}, bf16[2,64,2048]{2,1,0:T(8,128)(2,1)S(1)}, u32[]{:S(2)}, u32[]{:S(2)}) collective-permute-start(bf16[2,64,2048]{2,1,0:T(8,128)(2,1)S(1)} %get-tuple-element.10), channel_id=1, source_target_pairs={{0,16},{16,32},{32,48},{48,2},{2,18},{18,34},{34,50},{50,0},{1,17}... | collective-permute-start | bytes 1572872 | tf_op jit(solution)/shard_map/ppermute | solution.py:25
  15.4 26.2 %collective-permute-start.1 = (bf16[2,64,2048]{2,1,0:T(8,128)(2,1)S(1)}, bf16[2,64,2048]{2,1,0:T(8,128)(2,1)S(1)}, u32[]{:S(2)}, u32[]{:S(2)}) collective-permute-start(bf16[2,64,2048]{2,1,0:T(8,128)(2,1)S(1)} %get-tuple-element.11), channel_id=1, source_target_pairs={{0,50},{16,0},{32,16},{48,32},{2,48},{18,2},{34,18},{50,34},{1,51}... | collective-permute-start | bytes 1572872 | tf_op jit(solution)/shard_map/ppermute | solution.py:25
  19.3 24.3 %collective-permute-start.2 = (bf16[2,64,2048]{2,1,0:T(8,128)(2,1)S(1)}, bf16[2,64,2048]{2,1,0:T(8,128)(2,1)S(1)}, u32[]{:S(2)}, u32[]{:S(2)}) collective-permute-start(bf16[2,64,2048]{2,1,0:T(8,128)(2,1)S(1)} %get-tuple-element.12), channel_id=1, source_target_pairs={{0,32},{16,50},{32,2},{48,16},{2,34},{18,48},{34,0},{50,18},{1,33}... | collective-permute-start | bytes 1572872 | tf_op jit(solution)/shard_map/ppermute | solution.py:25
  29.2 16.8 %collective-permute-start.3 = (bf16[2,64,2048]{2,1,0:T(8,128)(2,1)S(1)}, bf16[2,64,2048]{2,1,0:T(8,128)(2,1)S(1)}, u32[]{:S(2)}, u32[]{:S(2)}) collective-permute-start(bf16[2,64,2048]{2,1,0:T(8,128)(2,1)S(1)} %collective-permute-done.refs_2_), channel_id=1, source_target_pairs={{0,1},{1,0},{2,3},{3,2},{4,5},{5,4},{6,7},{7,6},{8,9},{9,8},{10,11... | collective-permute-start | bytes 1572872 | tf_op jit(solution)/shard_map/ppermute | solution.py:17
  41.7 4.4 %collective-permute-start.4 = (bf16[2,64,2048]{2,1,0:T(8,128)(2,1)S(1)}, bf16[2,64,2048]{2,1,0:T(8,128)(2,1)S(1)}, u32[]{:S(2)}, u32[]{:S(2)}) collective-permute-start(bf16[2,64,2048]{2,1,0:T(8,128)(2,1)S(1)} %collective-permute-done.1.refs_3_), channel_id=1, source_target_pairs={{0,1},{1,0},{2,3},{3,2},{4,5},{5,4},{6,7},{7,6},{8,9},{9,8},{10,11... | collective-permute-start | bytes 1572872 | tf_op jit(solution)/shard_map/ppermute | solution.py:17
  43.6 3.9 %collective-permute-start.5 = (bf16[2,64,2048]{2,1,0:T(8,128)(2,1)S(1)}, bf16[2,64,2048]{2,1,0:T(8,128)(2,1)S(1)}, u32[]{:S(2)}, u32[]{:S(2)}) collective-permute-start(bf16[2,64,2048]{2,1,0:T(8,128)(2,1)S(1)} %collective-permute-done.2.refs_4_), channel_id=1, source_target_pairs={{0,1},{1,0},{2,3},{3,2},{4,5},{5,4},{6,7},{7,6},{8,9},{9,8},{10,11... | collective-permute-start | bytes 1572872 | tf_op jit(solution)/shard_map/ppermute | solution.py:17
  46.0 0.8 copy-start.2
  47.5 0.8 copy-start.5
  57.5 1.0 copy-start.3
  58.6 1.0 copy-start.6
  59.6 1.4 copy-start.8
  61.0 7.3 %copy-start.9 = (bf16[256,256]{1,0:T(8,128)(2,1)S(1)}, bf16[256,256]{1,0:T(8,128)(2,1)}, u32[]{:S(2)}) copy-start(bf16[256,256]{1,0:T(8,128)(2,1)} %refs_8_.1) | copy-start | bytes 393220
  63.8 39.1 %all-to-all-start = ((f32[4,128,384]{2,1,0:T(8,128)}), f32[4,128,384]{2,1,0:T(8,128)}, u32[]{:S(2)}, u32[]{:S(2)}) async-start(f32[4,128,384]{2,1,0:T(8,128)} %bitcast.3), calls=%async_computation | async-start | bytes 1572864 | tf_op jit(solution)/shard_map/all_to_all | solution.py:159
  68.3 13.8 %collective-permute-start.11 = (bf16[256,256]{1,0:T(8,128)(2,1)S(1)}, bf16[256,256]{1,0:T(8,128)(2,1)S(1)}, u32[]{:S(2)}, u32[]{:S(2)}) collective-permute-start(bf16[256,256]{1,0:T(8,128)(2,1)S(1)} %copy-done.9), channel_id=1, source_target_pairs={{0,128},{64,192},{128,256},{192,320},{256,384},{320,448},{384,0},{... | collective-permute-start | bytes 393224 | tf_op jit(solution)/shard_map/ppermute | solution.py:29
  71.1 11.0 %collective-permute-start.12 = (bf16[256,256]{1,0:T(8,128)(2,1)S(1)}, bf16[256,256]{1,0:T(8,128)(2,1)S(1)}, u32[]{:S(2)}, u32[]{:S(2)}) collective-permute-start(bf16[256,256]{1,0:T(8,128)(2,1)S(1)} %copy-done.9), channel_id=1, source_target_pairs={{0,384},{64,448},{128,0},{192,64},{256,128},{320,192},{384,256},{4... | collective-permute-start | bytes 393224 | tf_op jit(solution)/shard_map/ppermute | solution.py:29
  76.3 19.4 %collective-permute-start.10 = (bf16[256,256]{1,0:T(8,128)(2,1)S(1)}, bf16[256,256]{1,0:T(8,128)(2,1)}, u32[]{:S(2)}, u32[]{:S(2)}) collective-permute-start(bf16[256,256]{1,0:T(8,128)(2,1)S(1)} %copy-done.9), channel_id=1, source_target_pairs={{0,448},{64,0},{128,64},{192,128},{256,192},{320,256},{384,320},{4... | collective-permute-start | bytes 393224 | tf_op jit(solution)/shard_map/ppermute | solution.py:29
  79.9 15.8 %collective-permute-start.9 = (bf16[256,256]{1,0:T(8,128)(2,1)S(1)}, bf16[256,256]{1,0:T(8,128)(2,1)}, u32[]{:S(2)}, u32[]{:S(2)}) collective-permute-start(bf16[256,256]{1,0:T(8,128)(2,1)S(1)} %copy-done.9), channel_id=1, source_target_pairs={{0,64},{64,128},{128,192},{192,256},{256,320},{320,384},{384,448},... | collective-permute-start | bytes 393224 | tf_op jit(solution)/shard_map/ppermute | solution.py:29
  82.2 13.5 %collective-permute-start.15 = (bf16[256,256]{1,0:T(8,128)(2,1)S(1)}, bf16[256,256]{1,0:T(8,128)(2,1)S(1)}, u32[]{:S(2)}, u32[]{:S(2)}) collective-permute-start(bf16[256,256]{1,0:T(8,128)(2,1)S(1)} %broadcast_select_fusion), channel_id=1, source_target_pairs={{0,128},{64,448},{128,256},{192,64},{256,384},{320,192},{384,0},{4... | collective-permute-start | bytes 393224 | tf_op jit(solution)/shard_map/ppermute | solution.py:29
  88.6 8.1 %collective-permute-start.13 = (bf16[256,256]{1,0:T(8,128)(2,1)S(1)}, bf16[256,256]{1,0:T(8,128)(2,1)S(1)}, u32[]{:S(2)}, u32[]{:S(2)}) collective-permute-start(bf16[256,256]{1,0:T(8,128)(2,1)S(1)} %collective-permute-done.11.refs_11_), channel_id=1, source_target_pairs={{0,64},{64,128},{128,192},{192,256},{256,320},{320,384},{384,448},... | collective-permute-start | bytes 393224 | tf_op jit(solution)/shard_map/ppermute | solution.py:29
  91.2 7.0 %collective-permute-start.14 = (bf16[256,256]{1,0:T(8,128)(2,1)S(1)}, bf16[256,256]{1,0:T(8,128)(2,1)S(1)}, u32[]{:S(2)}, u32[]{:S(2)}) collective-permute-start(bf16[256,256]{1,0:T(8,128)(2,1)S(1)} %collective-permute-done.12.refs_12_), channel_id=1, source_target_pairs={{0,448},{64,0},{128,64},{192,128},{256,192},{320,256},{384,320},{4... | collective-permute-start | bytes 393224 | tf_op jit(solution)/shard_map/ppermute | solution.py:29
  98.2 1.0 copy-start.4
  99.2 1.0 copy-start.7
  102.8 24.2 %all-to-all-start.2 = ((f32[4,128,256]{2,1,0:T(8,128)}), f32[4,128,256]{2,1,0:T(8,128)S(1)}, u32[]{:S(2)}, u32[]{:S(2)}) async-start(f32[4,128,256]{2,1,0:T(8,128)} %bitcast.7), calls=%async_computation.2 | async-start | bytes 1048576 | tf_op jit(solution)/shard_map/all_to_all | solution.py:159
  108.9 14.2 %collective-permute-start.6 = (bf16[128,384]{1,0:T(8,128)(2,1)S(1)}, bf16[128,384]{1,0:T(8,128)(2,1)S(1)}, u32[]{:S(2)}, u32[]{:S(2)}) collective-permute-start(bf16[128,384]{1,0:T(8,128)(2,1)S(1)} %reduce_sum.18), channel_id=1, source_target_pairs={{0,0},{2,64},{4,128},{6,192},{8,256},{10,320},{12,384},{14,448},{6... | collective-permute-start | bytes 294920 | tf_op jit(solution)/shard_map/ppermute | solution.py:45
  112.7 14.3 %collective-permute-start.7 = (bf16[128,384]{1,0:T(8,128)(2,1)S(1)}, bf16[128,384]{1,0:T(8,128)(2,1)S(1)}, u32[]{:S(2)}, u32[]{:S(2)}) collective-permute-start(bf16[128,384]{1,0:T(8,128)(2,1)S(1)} %reduce_sum.18), channel_id=1, source_target_pairs={{0,2},{2,66},{4,130},{6,194},{8,258},{10,322},{12,386},{14,450},{6... | collective-permute-start | bytes 294920 | tf_op jit(solution)/shard_map/ppermute | solution.py:45
  128.0 11.9 %all-to-all-start.1 = ((bf16[4,2,128,384]{3,2,1,0:T(8,128)(2,1)}), bf16[4,2,128,384]{3,2,1,0:T(8,128)(2,1)S(1)}, u32[]{:S(2)}, u32[]{:S(2)}) async-start(bf16[4,2,128,384]{3,2,1,0:T(8,128)(2,1)} %broadcast_in_dim.4), calls=%async_computation.1 | async-start | bytes 1572864 | tf_op jit(solution)/shard_map/all_to_all | solution.py:60
  140.8 26.3 %all-to-all-start.3 = ((bf16[8,128,256]{2,1,0:T(8,128)(2,1)}), bf16[8,128,256]{2,1,0:T(8,128)(2,1)S(1)}, u32[]{:S(2)}, u32[]{:S(2)}) async-start(bf16[8,128,256]{2,1,0:T(8,128)(2,1)} %broadcast_in_dim.5), calls=%async_computation.3 | async-start | bytes 1048576 | tf_op jit(solution)/shard_map/all_to_all | solution.py:60
  153.7 13.3 %collective-permute-start.8 = (bf16[1024,384]{1,0:T(8,128)(2,1)S(1)}, bf16[1024,384]{1,0:T(8,128)(2,1)S(1)}, u32[]{:S(2)}, u32[]{:S(2)}) collective-permute-start(bf16[1024,384]{1,0:T(8,128)(2,1)S(1)} %bitcast.14), channel_id=1, source_target_pairs={{0,1},{1,0},{2,3},{3,2},{4,5},{5,4},{6,7},{7,6},{8,9},{9,8},{10,11... | collective-permute-start | bytes 2359304 | tf_op jit(solution)/shard_map/ppermute | solution.py:17
Sparse Core Ops, SparseCore 0:
  9.4 48.0 all-gather.1

commit v3 on v2

v3 whole, which is shorter than its diff:
```python
import jax
import jax.numpy as jnp
from jax import lax
from jax.experimental import pallas as pl
from jax.experimental.pallas import tpu as pltpu
from jax.sharding import Mesh, PartitionSpec as P

Z, Y, X, H, C = "z", "y", "x", "h", "c"
NZ, NY, NX, NH, NC = 8, 4, 4, 2, 2

VMEM_LIMIT = 12 * 2**20
TURN_LIMIT = 60 * 2**20
SCALARS = pl.BlockSpec(memory_space=pltpu.SMEM)
WHOLE = pl.BlockSpec(memory_space=pltpu.VMEM)
IN_HBM = pl.BlockSpec(memory_space=pltpu.HBM)
ANY = pl.BlockSpec(memory_space=pl.ANY)


def swap_cores(v):
    return lax.ppermute(v, C, [(0, 1), (1, 0)])


def ring_y(v, shift):
    pairs = []
    for at in range(NH * NY):
        to = (at + shift(at)) % (NH * NY)
        pairs.append((at % NY * NH + at // NY, to % NY * NH + to // NY))
    return lax.ppermute(v, (Y, H), pairs)


def one_way(step):
    return lambda at: step


def either_way(at):
    return 2 if at % 2 == 0 else -2


def transpose_planes(v, flip):
    pairs = []
    for z in range(NZ):
        for t in range(NX * NH):
            pairs.append((z * NX * NH + t, t * NX * NH + (z ^ flip)))
    return lax.ppermute(v, (Z, X, H), pairs)


def spread(v, axes, count):
    return lax.all_to_all(jnp.broadcast_to(v[None], (count,) + v.shape), axes, 0, 0)


def copies_kernel(late_ref, v_ref, out_ref):
    del late_ref
    for i in range(out_ref.shape[0]):
        out_ref[i] = v_ref[...]


def spread_z(v, late):
    copies = pl.pallas_call(
        copies_kernel,
        out_shape=jax.ShapeDtypeStruct((NZ,) + v.shape, v.dtype),
        in_specs=[ANY, WHOLE],
        out_specs=WHOLE,
        compiler_params=pltpu.CompilerParams(vmem_limit_bytes=VMEM_LIMIT),
    )(late, v)
    return lax.all_to_all(copies, Z, 0, 0)


def cut_kernel(at_ref, acts_ref, grads_ref, own_ref, after_ref, before_ref, across_ref):
    y, core = at_ref[0], at_ref[1]
    width = own_ref.shape[3] // 2
    for z in range(2):
        for steps, out in ((0, own_ref), (1, after_ref), (3, before_ref), (2, across_ref)):
            block = z * NY + lax.rem(y + steps, NY)
            cols = pl.ds(pl.multiple_of(block * width, width), width)
            for i, values in enumerate((acts_ref, grads_ref)):
                if steps == 0:
                    out[i, :, :, z * width : (z + 1) * width] = values[:, :, cols]
                else:
                    out[i, :, z * width : (z + 1) * width] = values[core, :, cols]


def cut_features(at, acts, grads):
    seqs, tokens, features = acts.shape
    steps = NZ // 2
    part = features // NY // steps
    whole_spec = pl.BlockSpec((seqs, tokens, part * NY), lambda i: (0, 0, i))
    piece = jax.ShapeDtypeStruct((2, tokens, features // NY), acts.dtype)
    piece_spec = pl.BlockSpec((2, tokens, part), lambda i: (0, 0, i))
    return pl.pallas_call(
        cut_kernel,
        grid=(steps,),
        out_shape=(
            jax.ShapeDtypeStruct((2, seqs, tokens, features // NY), acts.dtype),
            piece,
            piece,
            piece,
        ),
        in_specs=[SCALARS, whole_spec, whole_spec],
        out_specs=(pl.BlockSpec((2, seqs, tokens, part), lambda i: (0, 0, 0, i)),)
        + (piece_spec,) * 3,
        compiler_params=pltpu.CompilerParams(vmem_limit_bytes=VMEM_LIMIT),
    )(at, acts, grads)


def turn_kernel(at_ref, own_ref, *refs):
    pieces, bases, (send_ref, full_ref, rows) = refs[:6], refs[6:8], refs[8:11]
    basis_rows, sems = refs[11], refs[12]
    y, core = at_ref[0], at_ref[1]
    tokens = own_ref.shape[2]
    copies = [pltpu.make_async_copy(own_ref, rows.at[:, 0:2], sems.at[0])]
    for i, piece in enumerate(pieces):
        copies.append(pltpu.make_async_copy(piece, rows.at[:, 2 + i], sems.at[1 + i]))
    copies += [
        pltpu.make_async_copy(bases[i], basis_rows[i], sems.at[7 + i]) for i in range(2)
    ]
    for copy in copies:
        copy.start()
    for copy in copies[:-2]:
        copy.wait()
    places = [(0, y), (1, y)]
    for seq in (core, 1 - core):
        places += [(seq, lax.rem(y + steps, NY)) for steps in (3, 1, 2)]
    act_cols, cols = bases[0].shape[1], full_ref.shape[3]
    for which, span in ((0, slice(0, act_cols)), (1, slice(act_cols, cols))):
        copies[which - 2].wait()
        product = jnp.dot(
            rows[which].reshape(8 * tokens, rows.shape[3]),
            basis_rows[which][...],
            preferred_element_type=jnp.float32,
        )
        rounded = product.astype(send_ref.dtype)
        rest = (product - rounded.astype(jnp.float32)).astype(send_ref.dtype)
        for i, (seq, source) in enumerate(places):
            part = slice(i * tokens, (i + 1) * tokens)
            full_ref[seq, source, :, span] = product[part]
            send_ref[seq, source, :, span] = rounded[part]
            if which == 1:
                send_ref[seq, source, :, cols:] = rest[part]


def turn(at, own, pieces, act_rows, grad_rows):
    _, seqs, tokens, features = own.shape
    act_cols, grad_cols = act_rows.shape[1], grad_rows.shape[1]
    cols = act_cols + grad_cols
    send, full = pl.pallas_call(
        turn_kernel,
        out_shape=(
            jax.ShapeDtypeStruct((seqs, NY, tokens, cols + grad_cols), jnp.bfloat16),
            jax.ShapeDtypeStruct((seqs, NY, tokens, cols), jnp.float32),
        ),
        in_specs=[SCALARS] + [IN_HBM] * (3 + len(pieces)),
        out_specs=(WHOLE, WHOLE),
        scratch_shapes=[
            pltpu.VMEM((2, 8, tokens, features), own.dtype),
            [pltpu.VMEM(act_rows.shape, own.dtype), pltpu.VMEM(grad_rows.shape, own.dtype)],
            pltpu.SemaphoreType.DMA((9,)),
        ],
        compiler_params=pltpu.CompilerParams(vmem_limit_bytes=TURN_LIMIT),
    )(at, own, *pieces, act_rows, grad_rows)
    return send.reshape(NY, -1, cols + grad_cols), full.reshape(NY, -1, cols)


def sum_kernel(at_ref, full_ref, got_ref, act_ref, grad_ref):
    y = at_ref[0]
    act_cols, cols = act_ref.shape[1], full_ref.shape[2]
    total = full_ref[y]
    acts, grads = total[:, :act_cols], total[:, act_cols:]
    for steps in range(1, NY):
        got = got_ref[lax.rem(y + steps, NY)].astype(jnp.float32)
        acts = acts + got[:, :act_cols]
        grads = grads + (got[:, act_cols:cols] + got[:, cols:])
    act_ref[...] = acts.astype(act_ref.dtype)
    grads = grads.astype(grad_ref.dtype)
    for i in range(NZ):
        grad_ref[i] = grads


def sum_parts(at, full, got, act_cols):
    rows, grad_cols = full.shape[1], full.shape[2] - act_cols
    return pl.pallas_call(
        sum_kernel,
        out_shape=(
            jax.ShapeDtypeStruct((rows, act_cols), jnp.bfloat16),
            jax.ShapeDtypeStruct((NZ, rows, grad_cols), jnp.bfloat16),
        ),
        in_specs=[SCALARS, WHOLE, WHOLE],
        out_specs=(WHOLE, WHOLE),
        compiler_params=pltpu.CompilerParams(vmem_limit_bytes=VMEM_LIMIT),
    )(at, full, got)


def outer_kernel(acts_ref, mine_ref, other_ref, keep_ref, send_ref):
    for grads_ref, out_ref in ((other_ref, send_ref), (mine_ref, keep_ref)):
        product = lax.dot_general(
            acts_ref[...],
            grads_ref[...],
            (((0,), (0,)), ((), ())),
            preferred_element_type=jnp.float32,
        )
        out_ref[...] = product.astype(out_ref.dtype)


def outer_product(at, acts, mine, other):
    out = jax.ShapeDtypeStruct((acts.shape[1], mine.shape[1]), jnp.bfloat16)
    keep, send = pl.pallas_call(
        outer_kernel,
        out_shape=(out, out),
        in_specs=[WHOLE] * 3,
        out_specs=(WHOLE, WHOLE),
        compiler_params=pltpu.CompilerParams(vmem_limit_bytes=VMEM_LIMIT),
    )(acts, mine, other)
    got = swap_cores(send)
    core = at[1]
    halves = jnp.stack([jnp.where(core == 0, keep, got), jnp.where(core == 0, got, keep)])
    return halves.reshape(NY, -1, keep.shape[1])


def local(activations, out_grads, act_basis, grad_basis):
    h = lax.axis_index(H)
    at = jnp.stack([lax.axis_index(Y), lax.axis_index(C)]).astype(jnp.int32)
    act_cols, grad_cols = act_basis.shape[1], grad_basis.shape[1]
    act_rows = lax.all_gather(act_basis, Z, axis=0, tiled=True)

    own, to_after, to_before, to_across = cut_features(at, activations, out_grads)
    pieces = [
        ring_y(to_after, one_way(1)),
        ring_y(to_before, one_way(-1)),
        ring_y(to_across, either_way),
    ]
    grad_rows = spread_z(grad_basis, at).reshape(-1, grad_cols)
    pieces += [swap_cores(v) for v in pieces]

    send, full = turn(at, own, pieces, act_rows, grad_rows)
    got = lax.all_to_all(send, Y, 0, 0)
    act_turned, grad_turned = sum_parts(at, full, got, act_cols)

    grad_panel = lax.all_to_all(grad_turned, Z, 0, 0).reshape(-1, grad_cols)
    near, far = transpose_planes(act_turned, 0), transpose_planes(act_turned, 1)
    pair = jnp.where(h == 0, jnp.stack([near, far]), jnp.stack([far, near]))
    act_panel = spread(pair, X, NX).reshape(-1, act_cols)

    outer = outer_product(at, act_panel, grad_panel, swap_cores(grad_panel))
    got = lax.all_to_all(outer, Y, 0, 0).astype(jnp.float32)
    first, second = got[0] + got[1], got[2] + got[3]
    count = activations.shape[0] * activations.shape[1] * NZ * NY
    return ((first * first + second * second) / count).T


def solution(mesh):
    fine = Mesh(mesh.devices.reshape(NZ, NY, NX, NH, NC), (Z, Y, X, H, C))
    dp, tensor = (Z, Y), (X, H, C)
    placed = (P(None, dp, None), P(None, dp, None), P(dp, tensor), P(dp, tensor))
    return jax.shard_map(
        local, mesh=fine, in_specs=placed, out_specs=P(tensor, dp), check_vma=False
    )
```

time: 191 us -> 178 us (0.932)
  starting transfers between devices: 86.8 us -> 53.8 us
  blocking collectives: 13.7 us -> 41.2 us
  local copies, waits for them, and re-layouts: 12.2 us -> 5.33 us
  waiting for transfers between devices: 53.2 us -> 47.9 us
  Pallas kernels: 7.85 us -> 12.4 us
    ppermute x7 -> x0, starting transfers between devices: 27.2 us -> none  [ring_z(): return lax.ppermute(v, Z, [(at, (at + shift(at)) % NZ) for at in range(NZ)])]
    all_to_all x0 -> x1, blocking collectives: none -> 26.5 us  [local(): got = lax.all_to_all(send, Y, 0, 0)]
    all_to_all x2 -> x1, starting transfers between devices: 17.5 us -> 4.5 us  [spread(): lax.all_to_all(jnp.broadcast_to(v[None], (count,) + v.shape), axes, 0, 0)]
    all_to_all x2 -> x1, waiting for transfers between devices: 18.8 us -> 7.75 us  [spread(): lax.all_to_all(jnp.broadcast_to(v[None], (count,) + v.shape), axes, 0, 0)]
    ppermute x2, waiting for transfers between devices: 3.89 us -> 13.2 us  [transpose_planes(): return lax.ppermute(v, (Z, X, H), pairs)]
    all_to_all x2, starting transfers between devices: 9.44 us -> 15.9 us  [the longest x1 10.3 us: spread_z(): return lax.all_to_all(copies, Z, 0, 0)]
    unnamed x20 -> x26, local copies, waits for them, and re-layouts: 10.4 us -> 4.37 us
    pallas_call x3 -> x4, Pallas kernels: 6.43 us -> 11 us  [the longest x1 7.88 us: turn(): pl.pallas_call(turn_kernel, out_shape=(jax.ShapeDtypeStruct((seqs, NY, to...]
  transfers between devices with their start and end apart: 21 -> 14, of which waited for: 9 -> 7; matrix products, arithmetic and copies ran while one was open for 1% -> 0% of each run, Pallas kernels for 2% -> 1%
where the time goes in v3:
time: 178 us; the launch traced here: 175 us
  starting transfers between devices  53.8 us (30%)
  waiting for transfers between devices  47.9 us (27%)
  blocking collectives  41.2 us (23%)
  between operations  13.7 us (8%)
  Pallas kernels  12.4 us (7%)
  local copies, waits for them, and re-layouts  5.33 us (3%)
    all_to_all x1, blocking collectives, local(): got = lax.all_to_all(send, Y, 0, 0)  26.5 us
    ppermute x3, waiting for transfers between devices, ring_y(): return lax.ppermute(v, (Y, H), pairs)  17.2 us
    all_to_all x1, blocking collectives, local(): got = lax.all_to_all(outer, Y, 0, 0).astype(jnp.float32)  14.7 us
    ppermute x2, waiting for transfers between devices, transpose_planes(): return lax.ppermute(v, (Z, X, H), pairs)  13.2 us
    ppermute x2, starting transfers between devices, transpose_planes(): return lax.ppermute(v, (Z, X, H), pairs)  13 us
    ppermute x3, starting transfers between devices, ring_y(): return lax.ppermute(v, (Y, H), pairs)  10.3 us
    all_to_all x1, starting transfers between devices, spread_z(): return lax.all_to_all(copies, Z, 0, 0)  10.3 us
    ppermute x5, starting transfers between devices, swap_cores(): return lax.ppermute(v, C, [(0, 1), (1, 0)])  10.1 us
  transfers between devices with their start and end apart: 14, of which 7 were waited for; matrix products, arithmetic and copies ran while one was open for 0% of the time, Pallas kernels for 1%

profile of v3, /device:TPU:6, one launch (start us, length us, event | category | flops | bytes accessed | tf_op | source)
XLA Modules:
  0.0 175.2 jit_solution(7112030588948197058)
XLA Ops:
  6.5 0.0 copy-start
  6.5 0.0 all-gather.2.cloned.1.call-start
  6.5 0.7 all-gather.2.cloned.1.call-update
  7.3 0.1 pad_add_fusion.at_ref.late_ref
  7.3 0.0 copy-start.4
  7.3 0.9 copy-done.4
  8.2 0.0 copy-start.5
  8.2 1.1 shard_map.47
  9.3 10.3 %all-to-all-start = ((bf16[8,256,256]{2,1,0:T(8,128)(2,1)}), bf16[8,256,256]{2,1,0:T(8,128)(2,1)S(1)}, u32[]{:S(2)}, u32[]{:S(2)}) async-start(bf16[8,256,256]{2,1,0:T(8,128)(2,1)} %shard_map.47), calls=%async_computation | async-start | bytes 2097152 | tf_op jit(solution)/shard_map/all_to_all | solution.py:65
  19.6 0.0 copy-done
  19.6 0.0 copy-start.1
  19.6 1.6 copy-done.1
  21.2 1.4 shard_map.46
  22.6 0.0 copy-done.5
  22.6 0.0 copy-start.3
  22.6 1.0 copy-done.3
  23.6 3.5 %collective-permute-start = (bf16[2,64,2048]{2,1,0:T(8,128)(2,1)S(1)}, bf16[2,64,2048]{2,1,0:T(8,128)(2,1)S(1)}, u32[]{:S(2)}, u32[]{:S(2)}) collective-permute-start(bf16[2,64,2048]{2,1,0:T(8,128)(2,1)S(1)} %get-tuple-element.16), channel_id=1, source_target_pairs={{0,16},{16,32},{32,48},{48,2},{2,18},{18,34},{34,50},{50,0},{1,17}... | collective-permute-start | bytes 1572872 | tf_op jit(solution)/shard_map/ppermute | solution.py:28
  27.1 3.8 %collective-permute-start.1 = (bf16[2,64,2048]{2,1,0:T(8,128)(2,1)S(1)}, bf16[2,64,2048]{2,1,0:T(8,128)(2,1)S(1)}, u32[]{:S(2)}, u32[]{:S(2)}) collective-permute-start(bf16[2,64,2048]{2,1,0:T(8,128)(2,1)S(1)} %get-tuple-element.17), channel_id=1, source_target_pairs={{0,50},{16,0},{32,16},{48,32},{2,48},{18,2},{34,18},{50,34},{1,51}... | collective-permute-start | bytes 1572872 | tf_op jit(solution)/shard_map/ppermute | solution.py:28
  30.9 3.0 %collective-permute-start.2 = (bf16[2,64,2048]{2,1,0:T(8,128)(2,1)S(1)}, bf16[2,64,2048]{2,1,0:T(8,128)(2,1)S(1)}, u32[]{:S(2)}, u32[]{:S(2)}) collective-permute-start(bf16[2,64,2048]{2,1,0:T(8,128)(2,1)S(1)} %get-tuple-element.18), channel_id=1, source_target_pairs={{0,32},{16,50},{32,2},{48,16},{2,34},{18,48},{34,0},{50,18},{1,33}... | collective-permute-start | bytes 1572872 | tf_op jit(solution)/shard_map/ppermute | solution.py:28
  34.0 6.9 %collective-permute-done.refs_0_ = bf16[2,64,2048]{2,1,0:T(8,128)(2,1)S(1)} collective-permute-done((bf16[2,64,2048]{2,1,0:T(8,128)(2,1)S(1)}, bf16[2,64,2048]{2,1,0:T(8,128)(2,1)S(1)}, u32[]{:S(2)}, u32[]{:S(2)}) %collective-permute-start) | collective-permute-done | bytes 524320 | tf_op jit(solution)/shard_map/ppermute | solution.py:28
  40.9 0.0 copy-start.8
  40.9 1.9 %collective-permute-start.3 = (bf16[2,64,2048]{2,1,0:T(8,128)(2,1)S(1)}, bf16[2,64,2048]{2,1,0:T(8,128)(2,1)S(1)}, u32[]{:S(2)}, u32[]{:S(2)}) collective-permute-start(bf16[2,64,2048]{2,1,0:T(8,128)(2,1)S(1)} %collective-permute-done.refs_0_), channel_id=1, source_target_pairs={{0,1},{1,0},{2,3},{3,2},{4,5},{5,4},{6,7},{7,6},{8,9},{9,8},{10,11... | collective-permute-start | bytes 1572872 | tf_op jit(solution)/shard_map/ppermute | solution.py:20
  42.8 10.2 %collective-permute-done.1.refs_1_ = bf16[2,64,2048]{2,1,0:T(8,128)(2,1)S(1)} collective-permute-done((bf16[2,64,2048]{2,1,0:T(8,128)(2,1)S(1)}, bf16[2,64,2048]{2,1,0:T(8,128)(2,1)S(1)}, u32[]{:S(2)}, u32[]{:S(2)}) %collective-permute-start.1) | collective-permute-done | bytes 524320 | tf_op jit(solution)/shard_map/ppermute | solution.py:28
  53.1 1.9 %collective-permute-start.4 = (bf16[2,64,2048]{2,1,0:T(8,128)(2,1)S(1)}, bf16[2,64,2048]{2,1,0:T(8,128)(2,1)S(1)}, u32[]{:S(2)}, u32[]{:S(2)}) collective-permute-start(bf16[2,64,2048]{2,1,0:T(8,128)(2,1)S(1)} %collective-permute-done.1.refs_1_), channel_id=1, source_target_pairs={{0,1},{1,0},{2,3},{3,2},{4,5},{5,4},{6,7},{7,6},{8,9},{9,8},{10,11... | collective-permute-start | bytes 1572872 | tf_op jit(solution)/shard_map/ppermute | solution.py:20
  55.0 0.0 collective-permute-done.2.refs_2_
  55.0 0.0 copy-start.10
  55.0 2.4 %collective-permute-start.5 = (bf16[2,64,2048]{2,1,0:T(8,128)(2,1)S(1)}, bf16[2,64,2048]{2,1,0:T(8,128)(2,1)}, u32[]{:S(2)}, u32[]{:S(2)}) collective-permute-start(bf16[2,64,2048]{2,1,0:T(8,128)(2,1)S(1)} %collective-permute-done.2.refs_2_), channel_id=1, source_target_pairs={{0,1},{1,0},{2,3},{3,2},{4,5},{5,4},{6,7},{7,6},{8,9},{9,8},{10,11... | collective-permute-start | bytes 1572872 | tf_op jit(solution)/shard_map/ppermute | solution.py:20
  57.4 0.0 collective-permute-done.3.refs_3_
  57.4 0.0 copy-start.11
  57.5 0.0 collective-permute-done.4.refs_4_
  57.5 0.0 copy-start.12
  57.5 0.9 copy-done.12
  58.3 0.7 collective-permute-done.5.refs_5_
  59.1 0.0 all-to-all-done
  59.1 7.0 %all-gather.2.cloned.1.call-done.refs_6_ = bf16[2048,384]{1,0:T(8,128)(2,1)} async-done(((bf16[256,384]{1,0:T(8,128)(2,1)}), bf16[2048,384]{1,0:T(8,128)(2,1)}) %all-gather.2.cloned.1.call-update) | async-done | bytes 1572880 | tf_op jit(solution)/shard_map/all_gather | solution.py:222
  66.0 0.0 copy-done.8
  66.0 0.0 copy-done.9
  66.0 0.0 copy-done.10
  66.0 0.0 copy-done.11
  66.1 0.0 copy-done.7
  66.1 0.0 copy-start.6
  66.1 7.9 %shard_map.48 = (bf16[2,4,64,896]{3,2,1,0:T(8,128)(2,1)}, f32[2,4,64,640]{3,2,1,0:T(8,128)}) custom-call(s32[2]{0:T(128)} %copy-done.5, bf16[2,2,64,2048]{3,2,1,0:T(8,128)(2,1)} %copy-done.3, bf16[2,64,2048]{2,1,0:T(8,128)(2,1)} %copy-done.8, bf16[2,64,2048]{2,1,0:T(8,128)(2,1)} %copy-done.9, bf16[2,64,2048]{2,1,0:T(8,128)(2,1)} %copy-done.10, ...), custom_call_target="tpu_custom_call" | custom-call | tf_op jit(solution)/shard_map/pallas_call | solution.py:145
  74.0 0.0 copy-start.2
  74.0 26.5 %all_to_all.25.got_ref = bf16[4,128,896]{2,1,0:T(8,128)(2,1)S(1)} all-to-all(bf16[4,128,896]{2,1,0:T(8,128)(2,1)} %bitcast.24), channel_id=1, replica_groups=mesh['z'=8,'y'=4,'x'=4,'h'=2,'c'=2] {'y'}, dimensions={0} | all-to-all | bytes 1835008 | tf_op jit(solution)/shard_map/all_to_all | solution.py:234
  100.5 0.0 copy-done.6
  100.5 0.0 copy-done.2
  100.5 1.4 shard_map.49
  101.9 5.6 %all-to-all-start.3 = ((bf16[8,128,256]{2,1,0:T(8,128)(2,1)}), bf16[8,128,256]{2,1,0:T(8,128)(2,1)S(1)}, u32[]{:S(2)}, u32[]{:S(2)}) async-start(bf16[8,128,256]{2,1,0:T(8,128)(2,1)} %get-tuple-element.22), calls=%async_computation.3 | async-start | bytes 1048576 | tf_op jit(solution)/shard_map/all_to_all | solution.py:237
  107.5 8.9 %collective-permute-start.7 = (bf16[128,384]{1,0:T(8,128)(2,1)S(1)}, bf16[128,384]{1,0:T(8,128)(2,1)S(1)}, u32[]{:S(2)}, u32[]{:S(2)}) collective-permute-start(bf16[128,384]{1,0:T(8,128)(2,1)S(1)} %get-tuple-element.21), channel_id=1, source_target_pairs={{0,2},{2,66},{4,130},{6,194},{8,258},{10,322},{12,386},{14,450},{6... | collective-permute-start | bytes 294920 | tf_op jit(solution)/shard_map/ppermute | solution.py:44
  116.4 4.1 %collective-permute-start.6 = (bf16[128,384]{1,0:T(8,128)(2,1)S(1)}, bf16[128,384]{1,0:T(8,128)(2,1)S(1)}, u32[]{:S(2)}, u32[]{:S(2)}) collective-permute-start(bf16[128,384]{1,0:T(8,128)(2,1)S(1)} %get-tuple-element.21), channel_id=1, source_target_pairs={{0,0},{2,64},{4,128},{6,192},{8,256},{10,320},{12,384},{14,448},{6... | collective-permute-start | bytes 294920 | tf_op jit(solution)/shard_map/ppermute | solution.py:44
  120.5 13.2 %collective-permute-done.7 = bf16[128,384]{1,0:T(8,128)(2,1)S(1)} collective-permute-done((bf16[128,384]{1,0:T(8,128)(2,1)S(1)}, bf16[128,384]{1,0:T(8,128)(2,1)S(1)}, u32[]{:S(2)}, u32[]{:S(2)}) %collective-permute-start.7) | collective-permute-done | bytes 98336 | tf_op jit(solution)/shard_map/ppermute | solution.py:44
  133.7 0.0 collective-permute-done.6
  133.7 0.0 all-to-all-done.3
  133.7 1.0 broadcast_in_dim.2
  134.7 4.5 %all-to-all-start.2 = ((bf16[4,2,128,384]{3,2,1,0:T(8,128)(2,1)}), bf16[4,2,128,384]{3,2,1,0:T(8,128)(2,1)S(1)}, u32[]{:S(2)}, u32[]{:S(2)}) async-start(bf16[4,2,128,384]{3,2,1,0:T(8,128)(2,1)} %broadcast_in_dim.2), calls=%async_computation.2 | async-start | bytes 1572864 | tf_op jit(solution)/shard_map/all_to_all | solution.py:48
  139.2 1.9 %collective-permute-start.8 = (bf16[1024,256]{1,0:T(8,128)(2,1)S(1)}, bf16[1024,256]{1,0:T(8,128)(2,1)S(1)}, u32[]{:S(2)}, u32[]{:S(2)}) collective-permute-start(bf16[1024,256]{1,0:T(8,128)(2,1)S(1)} %bitcast.19), channel_id=1, source_target_pairs={{0,1},{1,0},{2,3},{3,2},{4,5},{5,4},{6,7},{7,6},{8,9},{9,8},{10,11... | collective-permute-start | bytes 1572872 | tf_op jit(solution)/shard_map/ppermute | solution.py:20
  141.1 7.7 %all-to-all-done.2 = bf16[4,2,128,384]{3,2,1,0:T(8,128)(2,1)S(1)} async-done(((bf16[4,2,128,384]{3,2,1,0:T(8,128)(2,1)}), bf16[4,2,128,384]{3,2,1,0:T(8,128)(2,1)S(1)}, u32[]{:S(2)}, u32[]{:S(2)}) %all-to-all-start.2) | async-done | bytes 786464 | tf_op jit(solution)/shard_map/all_to_all | solution.py:48
  148.9 0.0 collective-permute-done.8.other_ref
  148.9 0.6 shard_map.50
  149.5 1.9 %collective-permute-start.9 = (bf16[384,256]{1,0:T(8,128)(2,1)S(1)}, bf16[384,256]{1,0:T(8,128)(2,1)S(1)}, u32[]{:S(2)}, u32[]{:S(2)}) collective-permute-start(bf16[384,256]{1,0:T(8,128)(2,1)S(1)} %get-tuple-element.24), channel_id=1, source_target_pairs={{0,1},{1,0},{2,3},{3,2},{4,5},{5,4},{6,7},{7,6},{8,9},{9,8},{10,11... | collective-permute-start | bytes 589832 | tf_op jit(solution)/shard_map/ppermute | solution.py:20
  151.4 1.4 collective-permute-done.9
  152.9 14.7 %all_to_all.26 = bf16[4,192,256]{2,1,0:T(8,128)(2,1)S(1)} all-to-all(bf16[4,192,256]{2,1,0:T(8,128)(2,1)S(1)} %bitcast.23), channel_id=1, replica_groups=mesh['z'=8,'y'=4,'x'=4,'h'=2,'c'=2] {'y'}, dimensions={0} | all-to-all | bytes 786432 | tf_op jit(solution)/shard_map/all_to_all | solution.py:243
  167.6 0.1 convert_element_type.3
  167.6 0.7 fusion.3
  (5 shorter events, 0.1 us)
Async XLA Ops:
  6.5 13.1 %copy-start = (bf16[2,64,8192]{2,1,0:T(8,128)(2,1)S(1)}, bf16[2,64,8192]{2,1,0:T(8,128)(2,1)}, u32[]{:S(2)}) copy-start(bf16[2,64,8192]{2,1,0:T(8,128)(2,1)} %acts_ref.1) | copy-start | bytes 6291460
  6.5 59.5 %all-gather.2.cloned.1.call-start = ((), (), s32[]{:S(2)}) async-start(), calls=%async_computation.5 | async-start | bytes 1769472 | tf_op jit(solution)/shard_map/all_gather | solution.py:222
  7.3 0.9 copy-start.4
  8.2 14.4 %copy-start.5 = (s32[2]{0:T(128)}, s32[2]{0:T(128)S(1)}, u32[]{:S(2)}) copy-start(s32[2]{0:T(128)S(1)} %pad_add_fusion.at_ref.late_ref) | copy-start | bytes 28
  9.3 49.8 %all-to-all-start = ((bf16[8,256,256]{2,1,0:T(8,128)(2,1)}), bf16[8,256,256]{2,1,0:T(8,128)(2,1)S(1)}, u32[]{:S(2)}, u32[]{:S(2)}) async-start(bf16[8,256,256]{2,1,0:T(8,128)(2,1)} %shard_map.47), calls=%async_computation | async-start | bytes 2097152 | tf_op jit(solution)/shard_map/all_to_all | solution.py:65
  19.6 1.6 copy-start.1
  22.6 1.0 copy-start.3
  23.6 17.3 %collective-permute-start = (bf16[2,64,2048]{2,1,0:T(8,128)(2,1)S(1)}, bf16[2,64,2048]{2,1,0:T(8,128)(2,1)S(1)}, u32[]{:S(2)}, u32[]{:S(2)}) collective-permute-start(bf16[2,64,2048]{2,1,0:T(8,128)(2,1)S(1)} %get-tuple-element.16), channel_id=1, source_target_pairs={{0,16},{16,32},{32,48},{48,2},{2,18},{18,34},{34,50},{50,0},{1,17}... | collective-permute-start | bytes 1572872 | tf_op jit(solution)/shard_map/ppermute | solution.py:28
  27.1 26.0 %collective-permute-start.1 = (bf16[2,64,2048]{2,1,0:T(8,128)(2,1)S(1)}, bf16[2,64,2048]{2,1,0:T(8,128)(2,1)S(1)}, u32[]{:S(2)}, u32[]{:S(2)}) collective-permute-start(bf16[2,64,2048]{2,1,0:T(8,128)(2,1)S(1)} %get-tuple-element.17), channel_id=1, source_target_pairs={{0,50},{16,0},{32,16},{48,32},{2,48},{18,2},{34,18},{50,34},{1,51}... | collective-permute-start | bytes 1572872 | tf_op jit(solution)/shard_map/ppermute | solution.py:28
  30.9 24.1 %collective-permute-start.2 = (bf16[2,64,2048]{2,1,0:T(8,128)(2,1)S(1)}, bf16[2,64,2048]{2,1,0:T(8,128)(2,1)S(1)}, u32[]{:S(2)}, u32[]{:S(2)}) collective-permute-start(bf16[2,64,2048]{2,1,0:T(8,128)(2,1)S(1)} %get-tuple-element.18), channel_id=1, source_target_pairs={{0,32},{16,50},{32,2},{48,16},{2,34},{18,48},{34,0},{50,18},{1,33}... | collective-permute-start | bytes 1572872 | tf_op jit(solution)/shard_map/ppermute | solution.py:28
  40.9 25.1 %copy-start.8 = (bf16[2,64,2048]{2,1,0:T(8,128)(2,1)}, bf16[2,64,2048]{2,1,0:T(8,128)(2,1)S(1)}, u32[]{:S(2)}) copy-start(bf16[2,64,2048]{2,1,0:T(8,128)(2,1)S(1)} %collective-permute-done.refs_0_) | copy-start | bytes 1572868
  40.9 16.5 %collective-permute-start.3 = (bf16[2,64,2048]{2,1,0:T(8,128)(2,1)S(1)}, bf16[2,64,2048]{2,1,0:T(8,128)(2,1)S(1)}, u32[]{:S(2)}, u32[]{:S(2)}) collective-permute-start(bf16[2,64,2048]{2,1,0:T(8,128)(2,1)S(1)} %collective-permute-done.refs_0_), channel_id=1, source_target_pairs={{0,1},{1,0},{2,3},{3,2},{4,5},{5,4},{6,7},{7,6},{8,9},{9,8},{10,11... | collective-permute-start | bytes 1572872 | tf_op jit(solution)/shard_map/ppermute | solution.py:20
  53.1 13.0 %copy-start.9 = (bf16[2,64,2048]{2,1,0:T(8,128)(2,1)}, bf16[2,64,2048]{2,1,0:T(8,128)(2,1)S(1)}, u32[]{:S(2)}) copy-start(bf16[2,64,2048]{2,1,0:T(8,128)(2,1)S(1)} %collective-permute-done.1.refs_1_) | copy-start | bytes 1572868
  53.1 4.4 %collective-permute-start.4 = (bf16[2,64,2048]{2,1,0:T(8,128)(2,1)S(1)}, bf16[2,64,2048]{2,1,0:T(8,128)(2,1)S(1)}, u32[]{:S(2)}, u32[]{:S(2)}) collective-permute-start(bf16[2,64,2048]{2,1,0:T(8,128)(2,1)S(1)} %collective-permute-done.1.refs_1_), channel_id=1, source_target_pairs={{0,1},{1,0},{2,3},{3,2},{4,5},{5,4},{6,7},{7,6},{8,9},{9,8},{10,11... | collective-permute-start | bytes 1572872 | tf_op jit(solution)/shard_map/ppermute | solution.py:20
  55.0 11.0 %copy-start.10 = (bf16[2,64,2048]{2,1,0:T(8,128)(2,1)}, bf16[2,64,2048]{2,1,0:T(8,128)(2,1)S(1)}, u32[]{:S(2)}) copy-start(bf16[2,64,2048]{2,1,0:T(8,128)(2,1)S(1)} %collective-permute-done.2.refs_2_) | copy-start | bytes 1572868
  55.0 4.1 %collective-permute-start.5 = (bf16[2,64,2048]{2,1,0:T(8,128)(2,1)S(1)}, bf16[2,64,2048]{2,1,0:T(8,128)(2,1)}, u32[]{:S(2)}, u32[]{:S(2)}) collective-permute-start(bf16[2,64,2048]{2,1,0:T(8,128)(2,1)S(1)} %collective-permute-done.2.refs_2_), channel_id=1, source_target_pairs={{0,1},{1,0},{2,3},{3,2},{4,5},{5,4},{6,7},{7,6},{8,9},{9,8},{10,11... | collective-permute-start | bytes 1572872 | tf_op jit(solution)/shard_map/ppermute | solution.py:20
  57.4 8.6 %copy-start.11 = (bf16[2,64,2048]{2,1,0:T(8,128)(2,1)}, bf16[2,64,2048]{2,1,0:T(8,128)(2,1)S(1)}, u32[]{:S(2)}) copy-start(bf16[2,64,2048]{2,1,0:T(8,128)(2,1)S(1)} %collective-permute-done.3.refs_3_) | copy-start | bytes 1572868
  57.5 0.9 copy-start.12
  59.1 7.0 %copy-start.7 = (bf16[8,256,256]{2,1,0:T(8,128)(2,1)}, bf16[8,256,256]{2,1,0:T(8,128)(2,1)S(1)}, u32[]{:S(2)}) copy-start(bf16[8,256,256]{2,1,0:T(8,128)(2,1)S(1)} %all-to-all-done) | copy-start | bytes 3145732
  66.1 34.5 %copy-start.6 = (s32[2]{0:T(128)S(1)}, s32[2]{0:T(128)}, u32[]{:S(2)}) copy-start(s32[2]{0:T(128)} %copy-done.5) | copy-start | bytes 28
  74.0 26.6 %copy-start.2 = (f32[2,4,64,640]{3,2,1,0:T(8,128)S(1)}, f32[2,4,64,640]{3,2,1,0:T(8,128)}, u32[]{:S(2)}) copy-start(f32[2,4,64,640]{3,2,1,0:T(8,128)} %get-tuple-element.19) | copy-start | bytes 3932164
  101.9 31.8 %all-to-all-start.3 = ((bf16[8,128,256]{2,1,0:T(8,128)(2,1)}), bf16[8,128,256]{2,1,0:T(8,128)(2,1)S(1)}, u32[]{:S(2)}, u32[]{:S(2)}) async-start(bf16[8,128,256]{2,1,0:T(8,128)(2,1)} %get-tuple-element.22), calls=%async_computation.3 | async-start | bytes 1048576 | tf_op jit(solution)/shard_map/all_to_all | solution.py:237
  107.5 26.2 %collective-permute-start.7 = (bf16[128,384]{1,0:T(8,128)(2,1)S(1)}, bf16[128,384]{1,0:T(8,128)(2,1)S(1)}, u32[]{:S(2)}, u32[]{:S(2)}) collective-permute-start(bf16[128,384]{1,0:T(8,128)(2,1)S(1)} %get-tuple-element.21), channel_id=1, source_target_pairs={{0,2},{2,66},{4,130},{6,194},{8,258},{10,322},{12,386},{14,450},{6... | collective-permute-start | bytes 294920 | tf_op jit(solution)/shard_map/ppermute | solution.py:44
  116.4 17.3 %collective-permute-start.6 = (bf16[128,384]{1,0:T(8,128)(2,1)S(1)}, bf16[128,384]{1,0:T(8,128)(2,1)S(1)}, u32[]{:S(2)}, u32[]{:S(2)}) collective-permute-start(bf16[128,384]{1,0:T(8,128)(2,1)S(1)} %get-tuple-element.21), channel_id=1, source_target_pairs={{0,0},{2,64},{4,128},{6,192},{8,256},{10,320},{12,384},{14,448},{6... | collective-permute-start | bytes 294920 | tf_op jit(solution)/shard_map/ppermute | solution.py:44
  134.7 14.2 %all-to-all-start.2 = ((bf16[4,2,128,384]{3,2,1,0:T(8,128)(2,1)}), bf16[4,2,128,384]{3,2,1,0:T(8,128)(2,1)S(1)}, u32[]{:S(2)}, u32[]{:S(2)}) async-start(bf16[4,2,128,384]{3,2,1,0:T(8,128)(2,1)} %broadcast_in_dim.2), calls=%async_computation.2 | async-start | bytes 1572864 | tf_op jit(solution)/shard_map/all_to_all | solution.py:48
  139.2 9.7 %collective-permute-start.8 = (bf16[1024,256]{1,0:T(8,128)(2,1)S(1)}, bf16[1024,256]{1,0:T(8,128)(2,1)S(1)}, u32[]{:S(2)}, u32[]{:S(2)}) collective-permute-start(bf16[1024,256]{1,0:T(8,128)(2,1)S(1)} %bitcast.19), channel_id=1, source_target_pairs={{0,1},{1,0},{2,3},{3,2},{4,5},{5,4},{6,7},{7,6},{8,9},{9,8},{10,11... | collective-permute-start | bytes 1572872 | tf_op jit(solution)/shard_map/ppermute | solution.py:20
  149.5 3.3 %collective-permute-start.9 = (bf16[384,256]{1,0:T(8,128)(2,1)S(1)}, bf16[384,256]{1,0:T(8,128)(2,1)S(1)}, u32[]{:S(2)}, u32[]{:S(2)}) collective-permute-start(bf16[384,256]{1,0:T(8,128)(2,1)S(1)} %get-tuple-element.24), channel_id=1, source_target_pairs={{0,1},{1,0},{2,3},{3,2},{4,5},{5,4},{6,7},{7,6},{8,9},{9,8},{10,11... | collective-permute-start | bytes 589832 | tf_op jit(solution)/shard_map/ppermute | solution.py:20
Sparse Core Ops, SparseCore 0:
  9.4 56.5 all-gather.1

commit v4 on v1

v4 whole, which is shorter than its diff:
```python
import jax
import jax.numpy as jnp
from jax import lax
from jax.experimental import pallas as pl
from jax.experimental.pallas import tpu as pltpu
from jax.sharding import Mesh, PartitionSpec as P

Z, Y, X, H, C = "z", "y", "x", "h", "c"
NZ, NY, NX, NH, NC = 8, 4, 4, 2, 2

VMEM_LIMIT = 12 * 2**20
TURN_LIMIT = 60 * 2**20
SCALARS = pl.BlockSpec(memory_space=pltpu.SMEM)
WHOLE = pl.BlockSpec(memory_space=pltpu.VMEM)
IN_HBM = pl.BlockSpec(memory_space=pltpu.HBM)
ANY = pl.BlockSpec(memory_space=pl.ANY)


def swap_cores(v):
    return lax.ppermute(v, C, [(0, 1), (1, 0)])


def ring_y(v, shift):
    pairs = []
    for at in range(NH * NY):
        to = (at + shift(at)) % (NH * NY)
        pairs.append((at % NY * NH + at // NY, to % NY * NH + to // NY))
    return lax.ppermute(v, (Y, H), pairs)


def one_way(step):
    return lambda at: step


def either_way(at):
    return 2 if at % 2 == 0 else -2


def transpose_planes(v, flip):
    pairs = []
    for z in range(NZ):
        for t in range(NX * NH):
            pairs.append((z * NX * NH + t, t * NX * NH + (z ^ flip)))
    return lax.ppermute(v, (Z, X, H), pairs)


def copies_kernel(late_ref, v_ref, out_ref):
    del late_ref
    for i in range(out_ref.shape[0]):
        out_ref[i] = v_ref[...]


def spread_z(v, late):
    copies = pl.pallas_call(
        copies_kernel,
        out_shape=jax.ShapeDtypeStruct((NZ,) + v.shape, v.dtype),
        in_specs=[ANY, WHOLE],
        out_specs=WHOLE,
        compiler_params=pltpu.CompilerParams(vmem_limit_bytes=VMEM_LIMIT),
    )(late, v)
    return lax.all_to_all(copies, Z, 0, 0)


def cut_kernel(at_ref, values_ref, own_ref, after_ref, before_ref, across_ref):
    y, core = at_ref[0], at_ref[1]
    width = own_ref.shape[2] // 2
    for z in range(2):
        out_cols = slice(z * width, (z + 1) * width)
        for steps, out in ((0, own_ref), (1, after_ref), (3, before_ref), (2, across_ref)):
            block = z * NY + lax.rem(y + steps, NY)
            cols = pl.ds(pl.multiple_of(block * width, width), width)
            if steps == 0:
                out[:, :, out_cols] = values_ref[:, :, cols]
            else:
                out[:, out_cols] = values_ref[core, :, cols]


def cut_features(at, values):
    seqs, tokens, features = values.shape
    steps = NZ // 2
    part = features // NY // steps
    piece = jax.ShapeDtypeStruct((tokens, features // NY), values.dtype)
    piece_spec = pl.BlockSpec((tokens, part), lambda i: (0, i))
    return pl.pallas_call(
        cut_kernel,
        grid=(steps,),
        out_shape=(
            jax.ShapeDtypeStruct((seqs, tokens, features // NY), values.dtype),
            piece,
            piece,
            piece,
        ),
        in_specs=[SCALARS, pl.BlockSpec((seqs, tokens, part * NY), lambda i: (0, 0, i))],
        out_specs=(pl.BlockSpec((seqs, tokens, part), lambda i: (0, 0, i)),) + (piece_spec,) * 3,
        compiler_params=pltpu.CompilerParams(vmem_limit_bytes=VMEM_LIMIT),
    )(at, values)


def move_tokens(at, values):
    own, to_after, to_before, to_across = cut_features(at, values)
    pieces = [
        ring_y(to_after, one_way(1)),
        ring_y(to_before, one_way(-1)),
        ring_y(to_across, either_way),
    ]
    return own, pieces


def turn_kernel(lates, at_ref, *refs):
    own_ref, *pieces, basis_ref, out_ref, rows, basis, sems = refs[lates:]
    y, core = at_ref[0], at_ref[1]
    tokens = own_ref.shape[1]
    copies = [
        pltpu.make_async_copy(own_ref, rows.at[0:2], sems.at[0]),
        pltpu.make_async_copy(basis_ref, basis, sems.at[1]),
    ]
    for i, piece in enumerate(pieces):
        copies.append(pltpu.make_async_copy(piece, rows.at[2 + i], sems.at[2 + i]))
    for copy in copies:
        copy.start()
    for copy in copies:
        copy.wait()
    product = jnp.dot(
        rows[...].reshape(8 * tokens, rows.shape[2]),
        basis[...],
        preferred_element_type=jnp.float32,
    )
    parts = out_ref.shape[2]
    if parts == 1:
        columns = [product]
    else:
        half = out_ref.shape[5] // 2
        columns = []
        for c in range(parts):
            halves = [
                product[:, (parts * q + c) * half : (parts * q + c + 1) * half]
                for q in range(2)
            ]
            columns.append(jnp.concatenate(halves, axis=1))
    places = [(0, y), (1, y)]
    for seq in (core, 1 - core):
        places += [(seq, lax.rem(y + steps, NY)) for steps in (3, 1, 2)]
    for i, (seq, source) in enumerate(places):
        for c in range(parts):
            out_ref[seq, source // 2, c, lax.rem(source, 2)] = columns[c][
                i * tokens : (i + 1) * tokens
            ]


def turn(at, late, own, pieces, basis, parts):
    seqs, tokens, features = own.shape
    cols = basis.shape[1]
    out = pl.pallas_call(
        lambda *refs: turn_kernel(len(late), *refs),
        out_shape=jax.ShapeDtypeStruct(
            (seqs, 2, parts, 2, tokens, cols // parts), jnp.float32
        ),
        in_specs=[SCALARS] + [ANY] * (2 + len(late) + len(pieces)),
        out_specs=WHOLE,
        scratch_shapes=[
            pltpu.VMEM((8, tokens, features), own.dtype),
            pltpu.VMEM((features, cols), basis.dtype),
            pltpu.SemaphoreType.DMA((8,)),
        ],
        compiler_params=pltpu.CompilerParams(vmem_limit_bytes=TURN_LIMIT),
    )(at, *late, own, *pieces, basis)
    return out.reshape(NY * parts, 2 * tokens, cols // parts)


def round_kernel(late_ref, v_ref, out_ref):
    del late_ref
    out_ref[...] = v_ref[...].astype(out_ref.dtype)


def rounded(late, v):
    return pl.pallas_call(
        round_kernel,
        out_shape=jax.ShapeDtypeStruct(v.shape, jnp.bfloat16),
        in_specs=[ANY, WHOLE],
        out_specs=WHOLE,
        compiler_params=pltpu.CompilerParams(vmem_limit_bytes=VMEM_LIMIT),
    )(late, v)


def sum_acts_kernel(at_ref, full_ref, got_ref, out_ref):
    y, core = at_ref[0], at_ref[1]
    totals = []
    for c in range(NC):
        own = NC * y + c
        total = jnp.where(core == c, full_ref[own], got_ref[own].astype(jnp.float32))
        for steps in range(1, NY):
            source = NC * lax.rem(y + steps, NY) + c
            total = total + got_ref[source].astype(jnp.float32)
        totals.append(total)
    out_ref[...] = jnp.concatenate(totals, axis=1).astype(out_ref.dtype)


def sum_acts(at, full, got):
    _, rows, cols = full.shape
    return pl.pallas_call(
        sum_acts_kernel,
        out_shape=jax.ShapeDtypeStruct((rows, NC * cols), jnp.bfloat16),
        in_specs=[SCALARS, WHOLE, WHOLE],
        out_specs=WHOLE,
        compiler_params=pltpu.CompilerParams(vmem_limit_bytes=VMEM_LIMIT),
    )(at, full, got)


def sum_grads_kernel(late_ref, got_ref, out_ref):
    del late_ref
    total = got_ref[0] + got_ref[1] + got_ref[2] + got_ref[3]
    out_ref[...] = total


def sum_grads(late, got):
    return pl.pallas_call(
        sum_grads_kernel,
        out_shape=jax.ShapeDtypeStruct(got.shape[1:], got.dtype),
        in_specs=[ANY, WHOLE],
        out_specs=WHOLE,
        compiler_params=pltpu.CompilerParams(vmem_limit_bytes=VMEM_LIMIT),
    )(late, got)


def pair_kernel(at_ref, near_ref, far_ref, out_ref):
    even = at_ref[2] == 0
    near, far = near_ref[...], far_ref[...]
    first, second = jnp.where(even, near, far), jnp.where(even, far, near)
    for i in range(NX):
        out_ref[i, 0] = first
        out_ref[i, 1] = second


def paired(at, near, far):
    return pl.pallas_call(
        pair_kernel,
        out_shape=jax.ShapeDtypeStruct((NX, 2) + near.shape, near.dtype),
        in_specs=[SCALARS, WHOLE, WHOLE],
        out_specs=WHOLE,
        compiler_params=pltpu.CompilerParams(vmem_limit_bytes=VMEM_LIMIT),
    )(at, near, far)


def outer_kernel(at_ref, acts_ref, mine_ref, other_ref, out_ref):
    core = at_ref[1]
    quarter = out_ref.shape[2]
    for grads_ref, place in ((mine_ref, core), (other_ref, 1 - core)):
        product = lax.dot_general(
            acts_ref[...],
            grads_ref[...].astype(acts_ref.dtype),
            (((0,), (0,)), ((), ())),
            preferred_element_type=jnp.float32,
        ).astype(out_ref.dtype)
        for q in range(NY):
            out_ref[q, place] = product[q * quarter : (q + 1) * quarter]


def outer_product(at, acts, mine, other):
    quarter, cols = acts.shape[1] // NY, mine.shape[1]
    out = pl.pallas_call(
        outer_kernel,
        out_shape=jax.ShapeDtypeStruct((NY, NC, quarter, cols), jnp.bfloat16),
        in_specs=[SCALARS] + [WHOLE] * 3,
        out_specs=WHOLE,
        compiler_params=pltpu.CompilerParams(vmem_limit_bytes=VMEM_LIMIT),
    )(at, acts, mine, other)
    return out.reshape(NY * NC, quarter, cols)


def local(activations, out_grads, act_basis, grad_basis):
    at = jnp.stack([lax.axis_index(a) for a in (Y, C, H)]).astype(jnp.int32)
    act_cols, grad_cols = act_basis.shape[1], grad_basis.shape[1]
    act_rows = lax.all_gather(act_basis, Z, axis=0, tiled=True)

    grad_rows = spread_z(grad_basis, at).reshape(-1, grad_cols)
    grad_own, grad_pieces = move_tokens(at, out_grads)
    act_own, act_pieces = move_tokens(at, activations)
    grad_pieces = grad_pieces + [swap_cores(v) for v in grad_pieces]

    grad_part = turn(at, act_pieces, grad_own, grad_pieces, grad_rows, 1)
    grad_got = lax.all_to_all(grad_part, Y, 0, 0)
    act_pieces = act_pieces + [swap_cores(v) for v in act_pieces]
    act_part = turn(at, [grad_part], act_own, act_pieces, act_rows, NC)
    act_got = lax.all_to_all(rounded(at, act_part), (Y, C), 0, 0)

    grad_turned = sum_grads(act_part, grad_got)
    grad_panel = lax.all_gather(grad_turned, Z, axis=0, tiled=True)

    act_turned = sum_acts(at, act_part, act_got)
    near, far = transpose_planes(act_turned, 0), transpose_planes(act_turned, 1)
    pair = paired(at, near, far)
    act_panel = lax.all_to_all(pair, X, 0, 0).reshape(-1, act_cols)
    grad_panel = rounded(pair, grad_panel)

    outer = outer_product(at, act_panel, grad_panel, swap_cores(grad_panel))
    got = lax.all_to_all(outer, (Y, C), 0, 0).astype(jnp.float32)
    got = got.reshape(NY, -1, got.shape[2])
    first, second = got[0] + got[1], got[2] + got[3]
    count = activations.shape[0] * activations.shape[1] * NZ * NY
    return ((first * first + second * second) / count).T


def solution(mesh):
    fine = Mesh(mesh.devices.reshape(NZ, NY, NX, NH, NC), (Z, Y, X, H, C))
    dp, tensor = (Z, Y), (X, H, C)
    placed = (P(None, dp, None), P(None, dp, None), P(dp, tensor), P(dp, tensor))
    return jax.shard_map(
        local, mesh=fine, in_specs=placed, out_specs=P(tensor, dp), check_vma=False
    )
```

time: 212 us -> 172 us (0.81); the launches traced: 212 us -> 168 us
  waiting for transfers between devices: 83 us -> 22.8 us
  starting transfers between devices: 61.5 us -> 74.1 us
  Pallas kernels: 7.96 us -> 16.6 us
  blocking collectives: 39.3 us -> 32.6 us
  local copies, waits for them, and re-layouts: 5.19 us -> 7.64 us
    all_gather x1 -> x0, blocking collectives: 27.8 us -> none  [local(): grad_panel = lax.all_gather(grad_turned, Z, axis=0, tiled=True)]
    ppermute x6, waiting for transfers between devices: 23.1 us -> 1.05 us  [ring_y(): return lax.ppermute(v, (Y, H), pairs)]
    all_to_all x1 -> x2, blocking collectives: 11.5 us -> 32.6 us  [the longest x1 17.4 us: local(): act_got = lax.all_to_all(rounded(at, act_part), (Y, C), 0, 0)]
    all_gather x1, waiting for transfers between devices: 19.4 us -> 0.01 us  [local(): act_rows = lax.all_gather(act_basis, Z, axis=0, tiled=True)]
    all_to_all x3, waiting for transfers between devices: 27.8 us -> 9.84 us  [the longest x1 6.85 us: local(): act_panel = lax.all_to_all(pair, X, 0, 0).reshape(-1, act_cols)]
    ppermute x1 -> x2, starting transfers between devices: 3.96 us -> 16 us  [transpose_planes(): return lax.ppermute(v, (Z, X, H), pairs)]
    pallas_call x3 -> x9, Pallas kernels: 5.88 us -> 14.4 us  [the longest x2 9.32 us: turn(): pl.pallas_call(lambda *refs: turn_kernel(len(late), *refs), out_shape=jax...]
    unnamed x8 -> x46, local copies, waits for them, and re-layouts: 4.23 us -> 7.13 us
  transfers between devices with their start and end apart: 19 -> 20, of which waited for: 9 -> 7; matrix products, arithmetic and copies ran while one was open for 1% -> 0% of each run, Pallas kernels for 2% -> 9%
where the time goes in v4:
time: 172 us; the launch traced here: 168 us
  starting transfers between devices  74.1 us (43%)
  blocking collectives  32.6 us (19%)
  waiting for transfers between devices  22.8 us (13%)
  Pallas kernels  16.6 us (10%)
  between operations  13.8 us (8%)
  local copies, waits for them, and re-layouts  7.64 us (4%)
    ppermute x6, starting transfers between devices, ring_y(): return lax.ppermute(v, (Y, H), pairs)  21.8 us
    all_to_all x1, blocking collectives, local(): act_got = lax.all_to_all(rounded(at, act_part), (Y, C), 0, 0)  17.4 us
    ppermute x2, starting transfers between devices, transpose_planes(): return lax.ppermute(v, (Z, X, H), pairs)  16 us
    all_to_all x1, blocking collectives, local(): got = lax.all_to_all(outer, (Y, C), 0, 0).astype(jnp.float32)  15.1 us
    ppermute x7, starting transfers between devices, swap_cores(): return lax.ppermute(v, C, [(0, 1), (1, 0)])  14.4 us
    all_to_all x1, starting transfers between devices, spread_z(): return lax.all_to_all(copies, Z, 0, 0)  10.3 us
    pallas_call x2, Pallas kernels, turn(): pl.pallas_call(lambda *refs: turn_kernel(len(late), *refs), out_shape=jax...  9.32 us
    ppermute x2, waiting for transfers between devices, transpose_planes(): return lax.ppermute(v, (Z, X, H), pairs)  9.07 us
  transfers between devices with their start and end apart: 20, of which 7 were waited for; matrix products, arithmetic and copies ran while one was open for 0% of the time, Pallas kernels for 9%

profile of v4, /device:TPU:6, one launch (start us, length us, event | category | flops | bytes accessed | tf_op | source)
XLA Modules:
  0.0 168.4 jit_solution(9395868648934062192)
XLA Ops:
  6.5 0.7 all-gather.3.cloned.1.call-update
  7.3 0.1 pad_add_fusion.at_ref.late_ref.refs_0_
  7.3 0.9 copy-done.7
  8.2 1.0 shard_map.48
  9.3 10.3 %all-to-all-start = ((bf16[8,256,256]{2,1,0:T(8,128)(2,1)}), bf16[8,256,256]{2,1,0:T(8,128)(2,1)S(1)}, u32[]{:S(2)}, u32[]{:S(2)}) async-start(bf16[8,256,256]{2,1,0:T(8,128)(2,1)} %shard_map.48), calls=%async_computation | async-start | bytes 2097152 | tf_op jit(solution)/shard_map/all_to_all | solution.py:61
  19.6 0.0 copy-start.3
  19.6 1.1 shard_map.46
  20.7 0.8 copy-done.6
  21.5 3.5 %collective-permute-start = (bf16[64,2048]{1,0:T(8,128)(2,1)S(1)}, bf16[64,2048]{1,0:T(8,128)(2,1)S(1)}, u32[]{:S(2)}, u32[]{:S(2)}) collective-permute-start(bf16[64,2048]{1,0:T(8,128)(2,1)S(1)} %get-tuple-element.13), channel_id=1, source_target_pairs={{0,16},{16,32},{32,48},{48,2},{2,18},{18,34},{34,50},{50,0},{1,17}... | collective-permute-start | bytes 786440 | tf_op jit(solution)/shard_map/ppermute | solution.py:28
  25.0 1.1 shard_map.47
  26.1 0.8 copy-done.5
  26.9 3.5 %collective-permute-start.3 = (bf16[64,2048]{1,0:T(8,128)(2,1)S(1)}, bf16[64,2048]{1,0:T(8,128)(2,1)S(1)}, u32[]{:S(2)}, u32[]{:S(2)}) collective-permute-start(bf16[64,2048]{1,0:T(8,128)(2,1)S(1)} %get-tuple-element.17), channel_id=1, source_target_pairs={{0,16},{16,32},{32,48},{48,2},{2,18},{18,34},{34,50},{50,0},{1,17}... | collective-permute-start | bytes 786440 | tf_op jit(solution)/shard_map/ppermute | solution.py:28
  30.3 3.6 %collective-permute-start.4 = (bf16[64,2048]{1,0:T(8,128)(2,1)S(1)}, bf16[64,2048]{1,0:T(8,128)(2,1)S(1)}, u32[]{:S(2)}, u32[]{:S(2)}) collective-permute-start(bf16[64,2048]{1,0:T(8,128)(2,1)S(1)} %get-tuple-element.18), channel_id=1, source_target_pairs={{0,50},{16,0},{32,16},{48,32},{2,48},{18,2},{34,18},{50,34},{1,51}... | collective-permute-start | bytes 786440 | tf_op jit(solution)/shard_map/ppermute | solution.py:28
  33.9 4.1 %collective-permute-start.5 = (bf16[64,2048]{1,0:T(8,128)(2,1)S(1)}, bf16[64,2048]{1,0:T(8,128)(2,1)S(1)}, u32[]{:S(2)}, u32[]{:S(2)}) collective-permute-start(bf16[64,2048]{1,0:T(8,128)(2,1)S(1)} %get-tuple-element.19), channel_id=1, source_target_pairs={{0,32},{16,50},{32,2},{48,16},{2,34},{18,48},{34,0},{50,18},{1,33}... | collective-permute-start | bytes 786440 | tf_op jit(solution)/shard_map/ppermute | solution.py:28
  38.0 3.3 %collective-permute-start.1 = (bf16[64,2048]{1,0:T(8,128)(2,1)S(1)}, bf16[64,2048]{1,0:T(8,128)(2,1)S(1)}, u32[]{:S(2)}, u32[]{:S(2)}) collective-permute-start(bf16[64,2048]{1,0:T(8,128)(2,1)S(1)} %get-tuple-element.14), channel_id=1, source_target_pairs={{0,50},{16,0},{32,16},{48,32},{2,48},{18,2},{34,18},{50,34},{1,51}... | collective-permute-start | bytes 786440 | tf_op jit(solution)/shard_map/ppermute | solution.py:28
  41.2 0.0 collective-permute-done.refs_1_.refs_3_
  41.3 3.9 %collective-permute-start.2 = (bf16[64,2048]{1,0:T(8,128)(2,1)S(1)}, bf16[64,2048]{1,0:T(8,128)(2,1)S(1)}, u32[]{:S(2)}, u32[]{:S(2)}) collective-permute-start(bf16[64,2048]{1,0:T(8,128)(2,1)S(1)} %get-tuple-element.15), channel_id=1, source_target_pairs={{0,32},{16,50},{32,2},{48,16},{2,34},{18,48},{34,0},{50,18},{1,33}... | collective-permute-start | bytes 786440 | tf_op jit(solution)/shard_map/ppermute | solution.py:28
  45.2 0.0 collective-permute-done.3.refs_5_
  45.2 1.9 %collective-permute-start.6 = (bf16[64,2048]{1,0:T(8,128)(2,1)S(1)}, bf16[64,2048]{1,0:T(8,128)(2,1)S(1)}, u32[]{:S(2)}, u32[]{:S(2)}) collective-permute-start(bf16[64,2048]{1,0:T(8,128)(2,1)S(1)} %collective-permute-done.3.refs_5_), channel_id=1, source_target_pairs={{0,1},{1,0},{2,3},{3,2},{4,5},{5,4},{6,7},{7,6},{8,9},{9,8},{10,11... | collective-permute-start | bytes 786440 | tf_op jit(solution)/shard_map/ppermute | solution.py:20
  47.1 0.0 collective-permute-done.4.refs_6_
  47.2 2.4 %collective-permute-start.7 = (bf16[64,2048]{1,0:T(8,128)(2,1)S(1)}, bf16[64,2048]{1,0:T(8,128)(2,1)S(1)}, u32[]{:S(2)}, u32[]{:S(2)}) collective-permute-start(bf16[64,2048]{1,0:T(8,128)(2,1)S(1)} %collective-permute-done.4.refs_6_), channel_id=1, source_target_pairs={{0,1},{1,0},{2,3},{3,2},{4,5},{5,4},{6,7},{7,6},{8,9},{9,8},{10,11... | collective-permute-start | bytes 786440 | tf_op jit(solution)/shard_map/ppermute | solution.py:20
  49.6 0.0 collective-permute-done.5.refs_7_
  49.6 1.9 %collective-permute-start.8 = (bf16[64,2048]{1,0:T(8,128)(2,1)S(1)}, bf16[64,2048]{1,0:T(8,128)(2,1)S(1)}, u32[]{:S(2)}, u32[]{:S(2)}) collective-permute-start(bf16[64,2048]{1,0:T(8,128)(2,1)S(1)} %collective-permute-done.5.refs_7_), channel_id=1, source_target_pairs={{0,1},{1,0},{2,3},{3,2},{4,5},{5,4},{6,7},{7,6},{8,9},{9,8},{10,11... | collective-permute-start | bytes 786440 | tf_op jit(solution)/shard_map/ppermute | solution.py:20
  51.5 1.0 collective-permute-done.1.refs_2_.refs_4_
  52.6 0.0 collective-permute-done.2.refs_3_.refs_5_
  52.6 0.0 collective-permute-done.6.refs_8_
  52.6 0.0 collective-permute-done.7.refs_9_
  52.6 0.4 collective-permute-done.8.refs_10_
  53.0 3.0 %all-to-all-done = bf16[8,256,256]{2,1,0:T(8,128)(2,1)S(1)} async-done(((bf16[8,256,256]{2,1,0:T(8,128)(2,1)}), bf16[8,256,256]{2,1,0:T(8,128)(2,1)S(1)}, u32[]{:S(2)}, u32[]{:S(2)}) %all-to-all-start) | async-done | bytes 1048608 | tf_op jit(solution)/shard_map/all_to_all | solution.py:61
  56.1 0.9 copy-done.10
  57.0 4.1 %shard_map.49 = f32[2,2,1,2,64,256]{5,4,3,2,1,0:T(8,128)} custom-call(s32[3]{0:T(128)} %copy-done.8, bf16[64,2048]{1,0:T(8,128)(2,1)} %copy-done.11, bf16[64,2048]{1,0:T(8,128)(2,1)} %copy-done.12, bf16[64,2048]{1,0:T(8,128)(2,1)} %copy-done.13, bf16[2,64,2048]{2,1,0:T(8,128)(2,1)} %copy-done.5, bf16[64,2048]{1,0:T(8,128)(2,1)} %copy-done.14, ...), custom_call_target="tpu_custom_call" | custom-call | tf_op jit(solution)/shard_map/pallas_call | solution.py:153
  61.1 7.1 %all-to-all-start.3 = ((f32[4,128,256]{2,1,0:T(8,128)}), f32[4,128,256]{2,1,0:T(8,128)S(1)}, u32[]{:S(2)}, u32[]{:S(2)}) async-start(f32[4,128,256]{2,1,0:T(8,128)} %bitcast.16), calls=%async_computation.3 | async-start | bytes 1048576 | tf_op jit(solution)/shard_map/all_to_all | solution.py:281
  68.2 1.9 %collective-permute-start.10 = (bf16[64,2048]{1,0:T(8,128)(2,1)}, bf16[64,2048]{1,0:T(8,128)(2,1)S(1)}, u32[]{:S(2)}, u32[]{:S(2)}) collective-permute-start(bf16[64,2048]{1,0:T(8,128)(2,1)} %copy-done.12), channel_id=1, source_target_pairs={{0,1},{1,0},{2,3},{3,2},{4,5},{5,4},{6,7},{7,6},{8,9},{9,8},{10,11... | collective-permute-start | bytes 786440 | tf_op jit(solution)/shard_map/ppermute | solution.py:20
  70.1 2.4 %collective-permute-start.11 = (bf16[64,2048]{1,0:T(8,128)(2,1)}, bf16[64,2048]{1,0:T(8,128)(2,1)S(1)}, u32[]{:S(2)}, u32[]{:S(2)}) collective-permute-start(bf16[64,2048]{1,0:T(8,128)(2,1)} %copy-done.13), channel_id=1, source_target_pairs={{0,1},{1,0},{2,3},{3,2},{4,5},{5,4},{6,7},{7,6},{8,9},{9,8},{10,11... | collective-permute-start | bytes 786440 | tf_op jit(solution)/shard_map/ppermute | solution.py:20
  72.5 1.9 %collective-permute-start.9 = (bf16[64,2048]{1,0:T(8,128)(2,1)}, bf16[64,2048]{1,0:T(8,128)(2,1)S(1)}, u32[]{:S(2)}, u32[]{:S(2)}) collective-permute-start(bf16[64,2048]{1,0:T(8,128)(2,1)} %copy-done.11), channel_id=1, source_target_pairs={{0,1},{1,0},{2,3},{3,2},{4,5},{5,4},{6,7},{7,6},{8,9},{9,8},{10,11... | collective-permute-start | bytes 786440 | tf_op jit(solution)/shard_map/ppermute | solution.py:20
  74.4 0.0 collective-permute-done.10.refs_7_
  74.5 1.7 collective-permute-done.9.refs_6_
  76.1 0.7 copy-done.22
  76.8 5.3 %shard_map.50 = f32[2,2,2,2,64,192]{5,4,3,2,1,0:T(8,128)} custom-call(s32[3]{0:T(128)} %copy-done.8, f32[4,128,256]{2,1,0:T(8,128)} %bitcast.17, bf16[2,64,2048]{2,1,0:T(8,128)(2,1)} %copy-done.6, bf16[64,2048]{1,0:T(8,128)(2,1)} %copy-done.11, bf16[64,2048]{1,0:T(8,128)(2,1)} %copy-done.12, bf16[64,2048]{1,0:T(8,128)(2,1)} %copy-done.13, ...), custom_call_target="tpu_custom_call" | custom-call | tf_op jit(solution)/shard_map/pallas_call | solution.py:153
  82.1 0.0 all-to-all-done.3.got_ref
  82.1 1.2 copy-done
  83.3 0.7 shard_map.54
  84.0 0.0 all-gather.5.cloned.1.call-update
  84.1 0.6 copy-done.1
  84.6 0.1 shard_map.51
  84.7 0.3 copy.5
  85.0 17.4 %all_to_all.25 = bf16[8,128,192]{1,2,0:T(8,128)(2,1)S(1)} all-to-all(bf16[8,128,192]{1,2,0:T(8,128)(2,1)S(1)} %copy.5), channel_id=1, replica_groups=mesh['z'=8,'y'=4,'x'=4,'h'=2,'c'=2] {'y','c'}, dimensions={0} | all-to-all | bytes 786432 | tf_op jit(solution)/shard_map/all_to_all | solution.py:284
  102.4 0.2 copy.6.got_ref
  102.6 0.7 shard_map.52
  103.3 5.7 %collective-permute-start.12 = (bf16[128,384]{1,0:T(8,128)(2,1)S(1)}, bf16[128,384]{1,0:T(8,128)(2,1)S(1)}, u32[]{:S(2)}, u32[]{:S(2)}) collective-permute-start(bf16[128,384]{1,0:T(8,128)(2,1)S(1)} %shard_map.52), channel_id=1, source_target_pairs={{0,0},{2,64},{4,128},{6,192},{8,256},{10,320},{12,384},{14,448},{6... | collective-permute-start | bytes 294920 | tf_op jit(solution)/shard_map/ppermute | solution.py:44
  109.0 10.4 %collective-permute-start.13 = (bf16[128,384]{1,0:T(8,128)(2,1)S(1)}, bf16[128,384]{1,0:T(8,128)(2,1)S(1)}, u32[]{:S(2)}, u32[]{:S(2)}) collective-permute-start(bf16[128,384]{1,0:T(8,128)(2,1)S(1)} %shard_map.52), channel_id=1, source_target_pairs={{0,2},{2,66},{4,130},{6,194},{8,258},{10,322},{12,386},{14,450},{6... | collective-permute-start | bytes 294920 | tf_op jit(solution)/shard_map/ppermute | solution.py:44
  119.3 2.9 %collective-permute-done.12.near_ref = bf16[128,384]{1,0:T(8,128)(2,1)S(1)} collective-permute-done((bf16[128,384]{1,0:T(8,128)(2,1)S(1)}, bf16[128,384]{1,0:T(8,128)(2,1)S(1)}, u32[]{:S(2)}, u32[]{:S(2)}) %collective-permute-start.12) | collective-permute-done | bytes 98336 | tf_op jit(solution)/shard_map/ppermute | solution.py:44
  122.2 6.2 %collective-permute-done.13.far_ref = bf16[128,384]{1,0:T(8,128)(2,1)S(1)} collective-permute-done((bf16[128,384]{1,0:T(8,128)(2,1)S(1)}, bf16[128,384]{1,0:T(8,128)(2,1)S(1)}, u32[]{:S(2)}, u32[]{:S(2)}) %collective-permute-start.13) | collective-permute-done | bytes 98336 | tf_op jit(solution)/shard_map/ppermute | solution.py:44
  128.4 1.5 shard_map.53.late_ref
  129.9 4.5 %all-to-all-start.2 = ((bf16[4,2,128,384]{3,2,1,0:T(8,128)(2,1)}), bf16[4,2,128,384]{3,2,1,0:T(8,128)(2,1)S(1)}, u32[]{:S(2)}, u32[]{:S(2)}) async-start(bf16[4,2,128,384]{3,2,1,0:T(8,128)(2,1)} %shard_map.53.late_ref), calls=%async_computation.2 | async-start | bytes 1572864 | tf_op jit(solution)/shard_map/all_to_all | solution.py:292
  134.4 1.2 copy-done.4
  135.6 0.1 shard_map.55.mine_ref
  135.7 1.9 %collective-permute-start.14 = (bf16[1024,256]{1,0:T(8,128)(2,1)S(1)}, bf16[1024,256]{1,0:T(8,128)(2,1)S(1)}, u32[]{:S(2)}, u32[]{:S(2)}) collective-permute-start(bf16[1024,256]{1,0:T(8,128)(2,1)S(1)} %shard_map.55.mine_ref), channel_id=1, source_target_pairs={{0,1},{1,0},{2,3},{3,2},{4,5},{5,4},{6,7},{7,6},{8,9},{9,8},{10,11... | collective-permute-start | bytes 1572872 | tf_op jit(solution)/shard_map/ppermute | solution.py:20
  137.6 6.9 %all-to-all-done.2 = bf16[4,2,128,384]{3,2,1,0:T(8,128)(2,1)S(1)} async-done(((bf16[4,2,128,384]{3,2,1,0:T(8,128)(2,1)}), bf16[4,2,128,384]{3,2,1,0:T(8,128)(2,1)S(1)}, u32[]{:S(2)}, u32[]{:S(2)}) %all-to-all-start.2) | async-done | bytes 786464 | tf_op jit(solution)/shard_map/all_to_all | solution.py:292
  144.5 0.0 collective-permute-done.14.other_ref
  144.5 1.1 shard_map.56
  145.6 15.1 %all_to_all.26 = bf16[8,96,256]{2,1,0:T(8,128)(2,1)S(1)} all-to-all(bf16[8,96,256]{2,1,0:T(8,128)(2,1)S(1)} %bitcast.15), channel_id=1, replica_groups=mesh['z'=8,'y'=4,'x'=4,'h'=2,'c'=2] {'y','c'}, dimensions={0} | all-to-all | bytes 786432 | tf_op jit(solution)/shard_map/all_to_all | solution.py:296
  160.7 0.1 convert_element_type.3
  160.8 0.7 fusion.2
  (42 shorter events, 0.1 us)
Async XLA Ops:
  6.5 13.1 %copy-start.2 = (bf16[2,64,8192]{2,1,0:T(8,128)(2,1)S(1)}, bf16[2,64,8192]{2,1,0:T(8,128)(2,1)}, u32[]{:S(2)}) copy-start(bf16[2,64,8192]{2,1,0:T(8,128)(2,1)} %values_ref.2) | copy-start | bytes 6291460
  6.5 69.6 %all-gather.3.cloned.1.call-start = ((), (), s32[]{:S(2)}) async-start(), calls=%async_computation.5 | async-start | bytes 1769472 | tf_op jit(solution)/shard_map/all_gather | solution.py:273
  7.3 0.9 copy-start.7
  8.2 16.7 %copy-start.8 = (s32[3]{0:T(128)}, s32[3]{0:T(128)S(1)}, u32[]{:S(2)}) copy-start(s32[3]{0:T(128)S(1)} %pad_add_fusion.at_ref.late_ref.refs_0_) | copy-start | bytes 40
  9.3 46.7 %all-to-all-start = ((bf16[8,256,256]{2,1,0:T(8,128)(2,1)}), bf16[8,256,256]{2,1,0:T(8,128)(2,1)S(1)}, u32[]{:S(2)}, u32[]{:S(2)}) async-start(bf16[8,256,256]{2,1,0:T(8,128)(2,1)} %shard_map.48), calls=%async_computation | async-start | bytes 2097152 | tf_op jit(solution)/shard_map/all_to_all | solution.py:61
  19.6 5.4 %copy-start.3 = (bf16[2,64,8192]{2,1,0:T(8,128)(2,1)S(1)}, bf16[2,64,8192]{2,1,0:T(8,128)(2,1)}, u32[]{:S(2)}) copy-start(bf16[2,64,8192]{2,1,0:T(8,128)(2,1)} %values_ref.3) | copy-start | bytes 6291460
  20.7 0.8 copy-start.6
  21.5 19.8 %collective-permute-start = (bf16[64,2048]{1,0:T(8,128)(2,1)S(1)}, bf16[64,2048]{1,0:T(8,128)(2,1)S(1)}, u32[]{:S(2)}, u32[]{:S(2)}) collective-permute-start(bf16[64,2048]{1,0:T(8,128)(2,1)S(1)} %get-tuple-element.13), channel_id=1, source_target_pairs={{0,16},{16,32},{32,48},{48,2},{2,18},{18,34},{34,50},{50,0},{1,17}... | collective-permute-start | bytes 786440 | tf_op jit(solution)/shard_map/ppermute | solution.py:28
  26.1 0.8 copy-start.5
  26.9 18.3 %collective-permute-start.3 = (bf16[64,2048]{1,0:T(8,128)(2,1)S(1)}, bf16[64,2048]{1,0:T(8,128)(2,1)S(1)}, u32[]{:S(2)}, u32[]{:S(2)}) collective-permute-start(bf16[64,2048]{1,0:T(8,128)(2,1)S(1)} %get-tuple-element.17), channel_id=1, source_target_pairs={{0,16},{16,32},{32,48},{48,2},{2,18},{18,34},{34,50},{50,0},{1,17}... | collective-permute-start | bytes 786440 | tf_op jit(solution)/shard_map/ppermute | solution.py:28
  30.3 16.8 %collective-permute-start.4 = (bf16[64,2048]{1,0:T(8,128)(2,1)S(1)}, bf16[64,2048]{1,0:T(8,128)(2,1)S(1)}, u32[]{:S(2)}, u32[]{:S(2)}) collective-permute-start(bf16[64,2048]{1,0:T(8,128)(2,1)S(1)} %get-tuple-element.18), channel_id=1, source_target_pairs={{0,50},{16,0},{32,16},{48,32},{2,48},{18,2},{34,18},{50,34},{1,51}... | collective-permute-start | bytes 786440 | tf_op jit(solution)/shard_map/ppermute | solution.py:28
  33.9 15.7 %collective-permute-start.5 = (bf16[64,2048]{1,0:T(8,128)(2,1)S(1)}, bf16[64,2048]{1,0:T(8,128)(2,1)S(1)}, u32[]{:S(2)}, u32[]{:S(2)}) collective-permute-start(bf16[64,2048]{1,0:T(8,128)(2,1)S(1)} %get-tuple-element.19), channel_id=1, source_target_pairs={{0,32},{16,50},{32,2},{48,16},{2,34},{18,48},{34,0},{50,18},{1,33}... | collective-permute-start | bytes 786440 | tf_op jit(solution)/shard_map/ppermute | solution.py:28
  38.0 14.6 %collective-permute-start.1 = (bf16[64,2048]{1,0:T(8,128)(2,1)S(1)}, bf16[64,2048]{1,0:T(8,128)(2,1)S(1)}, u32[]{:S(2)}, u32[]{:S(2)}) collective-permute-start(bf16[64,2048]{1,0:T(8,128)(2,1)S(1)} %get-tuple-element.14), channel_id=1, source_target_pairs={{0,50},{16,0},{32,16},{48,32},{2,48},{18,2},{34,18},{50,34},{1,51}... | collective-permute-start | bytes 786440 | tf_op jit(solution)/shard_map/ppermute | solution.py:28
  41.3 14.8 %copy-start.11 = (bf16[64,2048]{1,0:T(8,128)(2,1)}, bf16[64,2048]{1,0:T(8,128)(2,1)S(1)}, u32[]{:S(2)}) copy-start(bf16[64,2048]{1,0:T(8,128)(2,1)S(1)} %collective-permute-done.refs_1_.refs_3_) | copy-start | bytes 786436
  41.3 11.3 %collective-permute-start.2 = (bf16[64,2048]{1,0:T(8,128)(2,1)S(1)}, bf16[64,2048]{1,0:T(8,128)(2,1)S(1)}, u32[]{:S(2)}, u32[]{:S(2)}) collective-permute-start(bf16[64,2048]{1,0:T(8,128)(2,1)S(1)} %get-tuple-element.15), channel_id=1, source_target_pairs={{0,32},{16,50},{32,2},{48,16},{2,34},{18,48},{34,0},{50,18},{1,33}... | collective-permute-start | bytes 786440 | tf_op jit(solution)/shard_map/ppermute | solution.py:28
  45.2 10.8 %copy-start.14 = (bf16[64,2048]{1,0:T(8,128)(2,1)}, bf16[64,2048]{1,0:T(8,128)(2,1)S(1)}, u32[]{:S(2)}) copy-start(bf16[64,2048]{1,0:T(8,128)(2,1)S(1)} %collective-permute-done.3.refs_5_) | copy-start | bytes 786436
  45.2 7.4 %collective-permute-start.6 = (bf16[64,2048]{1,0:T(8,128)(2,1)S(1)}, bf16[64,2048]{1,0:T(8,128)(2,1)S(1)}, u32[]{:S(2)}, u32[]{:S(2)}) collective-permute-start(bf16[64,2048]{1,0:T(8,128)(2,1)S(1)} %collective-permute-done.3.refs_5_), channel_id=1, source_target_pairs={{0,1},{1,0},{2,3},{3,2},{4,5},{5,4},{6,7},{7,6},{8,9},{9,8},{10,11... | collective-permute-start | bytes 786440 | tf_op jit(solution)/shard_map/ppermute | solution.py:20
  47.2 8.9 %copy-start.15 = (bf16[64,2048]{1,0:T(8,128)(2,1)}, bf16[64,2048]{1,0:T(8,128)(2,1)S(1)}, u32[]{:S(2)}) copy-start(bf16[64,2048]{1,0:T(8,128)(2,1)S(1)} %collective-permute-done.4.refs_6_) | copy-start | bytes 786436
  47.2 5.4 %collective-permute-start.7 = (bf16[64,2048]{1,0:T(8,128)(2,1)S(1)}, bf16[64,2048]{1,0:T(8,128)(2,1)S(1)}, u32[]{:S(2)}, u32[]{:S(2)}) collective-permute-start(bf16[64,2048]{1,0:T(8,128)(2,1)S(1)} %collective-permute-done.4.refs_6_), channel_id=1, source_target_pairs={{0,1},{1,0},{2,3},{3,2},{4,5},{5,4},{6,7},{7,6},{8,9},{9,8},{10,11... | collective-permute-start | bytes 786440 | tf_op jit(solution)/shard_map/ppermute | solution.py:20
  49.6 6.4 %copy-start.16 = (bf16[64,2048]{1,0:T(8,128)(2,1)}, bf16[64,2048]{1,0:T(8,128)(2,1)S(1)}, u32[]{:S(2)}) copy-start(bf16[64,2048]{1,0:T(8,128)(2,1)S(1)} %collective-permute-done.5.refs_7_) | copy-start | bytes 786436
  49.6 3.4 %collective-permute-start.8 = (bf16[64,2048]{1,0:T(8,128)(2,1)S(1)}, bf16[64,2048]{1,0:T(8,128)(2,1)S(1)}, u32[]{:S(2)}, u32[]{:S(2)}) collective-permute-start(bf16[64,2048]{1,0:T(8,128)(2,1)S(1)} %collective-permute-done.5.refs_7_), channel_id=1, source_target_pairs={{0,1},{1,0},{2,3},{3,2},{4,5},{5,4},{6,7},{7,6},{8,9},{9,8},{10,11... | collective-permute-start | bytes 786440 | tf_op jit(solution)/shard_map/ppermute | solution.py:20
  52.6 3.5 %copy-start.12 = (bf16[64,2048]{1,0:T(8,128)(2,1)}, bf16[64,2048]{1,0:T(8,128)(2,1)S(1)}, u32[]{:S(2)}) copy-start(bf16[64,2048]{1,0:T(8,128)(2,1)S(1)} %collective-permute-done.1.refs_2_.refs_4_) | copy-start | bytes 786436
  52.6 3.5 %copy-start.13 = (bf16[64,2048]{1,0:T(8,128)(2,1)}, bf16[64,2048]{1,0:T(8,128)(2,1)S(1)}, u32[]{:S(2)}) copy-start(bf16[64,2048]{1,0:T(8,128)(2,1)S(1)} %collective-permute-done.2.refs_3_.refs_5_) | copy-start | bytes 786436
  52.6 3.5 %copy-start.17 = (bf16[64,2048]{1,0:T(8,128)(2,1)}, bf16[64,2048]{1,0:T(8,128)(2,1)S(1)}, u32[]{:S(2)}) copy-start(bf16[64,2048]{1,0:T(8,128)(2,1)S(1)} %collective-permute-done.6.refs_8_) | copy-start | bytes 786436
  52.6 3.5 %copy-start.18 = (bf16[64,2048]{1,0:T(8,128)(2,1)}, bf16[64,2048]{1,0:T(8,128)(2,1)S(1)}, u32[]{:S(2)}) copy-start(bf16[64,2048]{1,0:T(8,128)(2,1)S(1)} %collective-permute-done.7.refs_9_) | copy-start | bytes 786436
  53.0 3.0 %copy-start.19 = (bf16[64,2048]{1,0:T(8,128)(2,1)}, bf16[64,2048]{1,0:T(8,128)(2,1)S(1)}, u32[]{:S(2)}) copy-start(bf16[64,2048]{1,0:T(8,128)(2,1)S(1)} %collective-permute-done.8.refs_10_) | copy-start | bytes 786436
  56.0 1.0 copy-start.10
  61.1 21.1 %all-to-all-start.3 = ((f32[4,128,256]{2,1,0:T(8,128)}), f32[4,128,256]{2,1,0:T(8,128)S(1)}, u32[]{:S(2)}, u32[]{:S(2)}) async-start(f32[4,128,256]{2,1,0:T(8,128)} %bitcast.16), calls=%async_computation.3 | async-start | bytes 1048576 | tf_op jit(solution)/shard_map/all_to_all | solution.py:281
  68.2 66.2 %all-gather.5.cloned.1.call-start = ((), (), s32[]{:S(2)}) async-start(), calls=%async_computation.6 | async-start | bytes 1179648 | tf_op jit(solution)/shard_map/all_gather | solution.py:287
  68.2 6.3 %collective-permute-start.10 = (bf16[64,2048]{1,0:T(8,128)(2,1)}, bf16[64,2048]{1,0:T(8,128)(2,1)S(1)}, u32[]{:S(2)}, u32[]{:S(2)}) collective-permute-start(bf16[64,2048]{1,0:T(8,128)(2,1)} %copy-done.12), channel_id=1, source_target_pairs={{0,1},{1,0},{2,3},{3,2},{4,5},{5,4},{6,7},{7,6},{8,9},{9,8},{10,11... | collective-permute-start | bytes 786440 | tf_op jit(solution)/shard_map/ppermute | solution.py:20
  70.1 4.4 %collective-permute-start.11 = (bf16[64,2048]{1,0:T(8,128)(2,1)}, bf16[64,2048]{1,0:T(8,128)(2,1)S(1)}, u32[]{:S(2)}, u32[]{:S(2)}) collective-permute-start(bf16[64,2048]{1,0:T(8,128)(2,1)} %copy-done.13), channel_id=1, source_target_pairs={{0,1},{1,0},{2,3},{3,2},{4,5},{5,4},{6,7},{7,6},{8,9},{9,8},{10,11... | collective-permute-start | bytes 786440 | tf_op jit(solution)/shard_map/ppermute | solution.py:20
  72.5 3.6 %collective-permute-start.9 = (bf16[64,2048]{1,0:T(8,128)(2,1)}, bf16[64,2048]{1,0:T(8,128)(2,1)S(1)}, u32[]{:S(2)}, u32[]{:S(2)}) collective-permute-start(bf16[64,2048]{1,0:T(8,128)(2,1)} %copy-done.11), channel_id=1, source_target_pairs={{0,1},{1,0},{2,3},{3,2},{4,5},{5,4},{6,7},{7,6},{8,9},{9,8},{10,11... | collective-permute-start | bytes 786440 | tf_op jit(solution)/shard_map/ppermute | solution.py:20
  74.4 1.7 %copy-start.20 = (bf16[64,2048]{1,0:T(8,128)(2,1)}, bf16[64,2048]{1,0:T(8,128)(2,1)S(1)}, u32[]{:S(2)}) copy-start(bf16[64,2048]{1,0:T(8,128)(2,1)S(1)} %collective-permute-done.10.refs_7_) | copy-start | bytes 786436
  74.4 1.7 %copy-start.21 = (bf16[64,2048]{1,0:T(8,128)(2,1)}, bf16[64,2048]{1,0:T(8,128)(2,1)S(1)}, u32[]{:S(2)}) copy-start(bf16[64,2048]{1,0:T(8,128)(2,1)S(1)} %collective-permute-done.11.refs_8_) | copy-start | bytes 786436
  76.1 0.7 copy-start.22
  76.8 7.2 %copy-start.9 = (s32[3]{0:T(128)S(1)}, s32[3]{0:T(128)}, u32[]{:S(2)}) copy-start(s32[3]{0:T(128)} %copy-done.8) | copy-start | bytes 40
  82.1 1.2 copy-start
  83.3 1.3 copy-start.1
  103.3 18.9 %collective-permute-start.12 = (bf16[128,384]{1,0:T(8,128)(2,1)S(1)}, bf16[128,384]{1,0:T(8,128)(2,1)S(1)}, u32[]{:S(2)}, u32[]{:S(2)}) collective-permute-start(bf16[128,384]{1,0:T(8,128)(2,1)S(1)} %shard_map.52), channel_id=1, source_target_pairs={{0,0},{2,64},{4,128},{6,192},{8,256},{10,320},{12,384},{14,448},{6... | collective-permute-start | bytes 294920 | tf_op jit(solution)/shard_map/ppermute | solution.py:44
  109.0 19.4 %collective-permute-start.13 = (bf16[128,384]{1,0:T(8,128)(2,1)S(1)}, bf16[128,384]{1,0:T(8,128)(2,1)S(1)}, u32[]{:S(2)}, u32[]{:S(2)}) collective-permute-start(bf16[128,384]{1,0:T(8,128)(2,1)S(1)} %shard_map.52), channel_id=1, source_target_pairs={{0,2},{2,66},{4,130},{6,194},{8,258},{10,322},{12,386},{14,450},{6... | collective-permute-start | bytes 294920 | tf_op jit(solution)/shard_map/ppermute | solution.py:44
  129.9 14.6 %all-to-all-start.2 = ((bf16[4,2,128,384]{3,2,1,0:T(8,128)(2,1)}), bf16[4,2,128,384]{3,2,1,0:T(8,128)(2,1)S(1)}, u32[]{:S(2)}, u32[]{:S(2)}) async-start(bf16[4,2,128,384]{3,2,1,0:T(8,128)(2,1)} %shard_map.53.late_ref), calls=%async_computation.2 | async-start | bytes 1572864 | tf_op jit(solution)/shard_map/all_to_all | solution.py:292
  134.4 1.2 copy-start.4
  135.7 8.8 %collective-permute-start.14 = (bf16[1024,256]{1,0:T(8,128)(2,1)S(1)}, bf16[1024,256]{1,0:T(8,128)(2,1)S(1)}, u32[]{:S(2)}, u32[]{:S(2)}) collective-permute-start(bf16[1024,256]{1,0:T(8,128)(2,1)S(1)} %shard_map.55.mine_ref), channel_id=1, source_target_pairs={{0,1},{1,0},{2,3},{3,2},{4,5},{5,4},{6,7},{7,6},{8,9},{9,8},{10,11... | collective-permute-start | bytes 1572872 | tf_op jit(solution)/shard_map/ppermute | solution.py:20
Sparse Core Ops, SparseCore 0:
  9.4 56.6 all-gather.2
  84.2 49.6 all-gather.4

commit v5 on v4

--- a/solution.py
+++ b/solution.py
@@ -20,20 +20,38 @@
     return lax.ppermute(v, C, [(0, 1), (1, 0)])
 
 
-def ring_y(v, shift):
+def permute(v, axes, sizes, move):
+    count = 1
+    for size in sizes:
+        count *= size
     pairs = []
-    for at in range(NH * NY):
-        to = (at + shift(at)) % (NH * NY)
-        pairs.append((at % NY * NH + at // NY, to % NY * NH + to // NY))
-    return lax.ppermute(v, (Y, H), pairs)
-
-
-def one_way(step):
-    return lambda at: step
-
-
-def either_way(at):
-    return 2 if at % 2 == 0 else -2
+    for at in range(count):
+        place, rest = [], at
+        for size in reversed(sizes):
+            place.insert(0, rest % size)
+            rest //= size
+        to = 0
+        for index, size in zip(move(*place), sizes):
+            to = to * size + index
+        pairs.append((at, to))
+    return lax.ppermute(v, axes, pairs)
+
+
+def on_ring(y, h, steps):
+    at = (h * NY + y + steps) % (NH * NY)
+    return at % NY, at // NY
+
+
+def to_neighbours(v):
+    return permute(
+        v, (Y, H, C), (NY, NH, NC), lambda y, h, c: (*on_ring(y, h, 1 - 2 * c), c)
+    )
+
+
+def to_across(v):
+    return permute(
+        v, (Y, H), (NY, NH), lambda y, h: on_ring(y, h, 2 if y % 2 == 0 else -2)
+    )
 
 
 def transpose_planes(v, flip):
@@ -61,61 +79,54 @@
     return lax.all_to_all(copies, Z, 0, 0)
 
 
-def cut_kernel(at_ref, values_ref, own_ref, after_ref, before_ref, across_ref):
+def cut_kernel(at_ref, values_ref, own_ref, near_ref, across_ref):
     y, core = at_ref[0], at_ref[1]
     width = own_ref.shape[2] // 2
     for z in range(2):
-        out_cols = slice(z * width, (z + 1) * width)
-        for steps, out in ((0, own_ref), (1, after_ref), (3, before_ref), (2, across_ref)):
+        out = slice(z * width, (z + 1) * width)
+        for steps, out_ref in ((0, own_ref), (1 + 2 * core, near_ref), (2, across_ref)):
             block = z * NY + lax.rem(y + steps, NY)
             cols = pl.ds(pl.multiple_of(block * width, width), width)
-            if steps == 0:
-                out[:, :, out_cols] = values_ref[:, :, cols]
+            if out_ref is across_ref:
+                out_ref[:, out] = values_ref[core, :, cols]
             else:
-                out[:, out_cols] = values_ref[core, :, cols]
+                out_ref[:, :, out] = values_ref[:, :, cols]
 
 
 def cut_features(at, values):
     seqs, tokens, features = values.shape
     steps = NZ // 2
     part = features // NY // steps
-    piece = jax.ShapeDtypeStruct((tokens, features // NY), values.dtype)
-    piece_spec = pl.BlockSpec((tokens, part), lambda i: (0, i))
+    both = jax.ShapeDtypeStruct((seqs, tokens, features // NY), values.dtype)
+    both_spec = pl.BlockSpec((seqs, tokens, part), lambda i: (0, 0, i))
     return pl.pallas_call(
         cut_kernel,
         grid=(steps,),
-        out_shape=(
-            jax.ShapeDtypeStruct((seqs, tokens, features // NY), values.dtype),
-            piece,
-            piece,
-            piece,
-        ),
+        out_shape=(both, both, jax.ShapeDtypeStruct((tokens, features // NY), values.dtype)),
         in_specs=[SCALARS, pl.BlockSpec((seqs, tokens, part * NY), lambda i: (0, 0, i))],
-        out_specs=(pl.BlockSpec((seqs, tokens, part), lambda i: (0, 0, i)),) + (piece_spec,) * 3,
+        out_specs=(both_spec, both_spec, pl.BlockSpec((tokens, part), lambda i: (0, i))),
         compiler_params=pltpu.CompilerParams(vmem_limit_bytes=VMEM_LIMIT),
     )(at, values)
 
 
 def move_tokens(at, values):
-    own, to_after, to_before, to_across = cut_features(at, values)
-    pieces = [
-        ring_y(to_after, one_way(1)),
-        ring_y(to_before, one_way(-1)),
-        ring_y(to_across, either_way),
-    ]
-    return own, pieces
+    own, near, across = cut_features(at, values)
+    return own, [to_neighbours(near), to_across(across)]
 
 
 def turn_kernel(lates, at_ref, *refs):
-    own_ref, *pieces, basis_ref, out_ref, rows, basis, sems = refs[lates:]
+    own_ref, near, across, near_other, across_other, basis_ref = refs[lates : lates + 6]
+    *outs, rows, basis, sems = refs[lates + 6 :]
     y, core = at_ref[0], at_ref[1]
     tokens = own_ref.shape[1]
     copies = [
         pltpu.make_async_copy(own_ref, rows.at[0:2], sems.at[0]),
-        pltpu.make_async_copy(basis_ref, basis, sems.at[1]),
+        pltpu.make_async_copy(near, rows.at[2:4], sems.at[1]),
+        pltpu.make_async_copy(near_other, rows.at[4:6], sems.at[2]),
+        pltpu.make_async_copy(across, rows.at[6], sems.at[3]),
+        pltpu.make_async_copy(across_other, rows.at[7], sems.at[4]),
+        pltpu.make_async_copy(basis_ref, basis, sems.at[5]),
     ]
-    for i, piece in enumerate(pieces):
-        copies.append(pltpu.make_async_copy(piece, rows.at[2 + i], sems.at[2 + i]))
     for copy in copies:
         copy.start()
     for copy in copies:
@@ -125,11 +136,11 @@
         basis[...],
         preferred_element_type=jnp.float32,
     )
-    parts = out_ref.shape[2]
+    parts = outs[0].shape[2]
     if parts == 1:
         columns = [product]
     else:
-        half = out_ref.shape[5] // 2
+        half = outs[0].shape[5] // 2
         columns = []
         for c in range(parts):
             halves = [
@@ -137,34 +148,33 @@
                 for q in range(2)
             ]
             columns.append(jnp.concatenate(halves, axis=1))
-    places = [(0, y), (1, y)]
-    for seq in (core, 1 - core):
-        places += [(seq, lax.rem(y + steps, NY)) for steps in (3, 1, 2)]
+    back, on = lax.rem(y + 3 - 2 * core, NY), lax.rem(y + 1 + 2 * core, NY)
+    two = lax.rem(y + 2, NY)
+    places = [(0, y), (1, y), (0, back), (1, back), (0, on), (1, on), (core, two), (1 - core, two)]
     for i, (seq, source) in enumerate(places):
         for c in range(parts):
-            out_ref[seq, source // 2, c, lax.rem(source, 2)] = columns[c][
-                i * tokens : (i + 1) * tokens
-            ]
-
-
-def turn(at, late, own, pieces, basis, parts):
+            value = columns[c][i * tokens : (i + 1) * tokens]
+            for out_ref in outs:
+                out_ref[seq, source // 2, c, lax.rem(source, 2)] = value.astype(out_ref.dtype)
+
+
+def turn(at, late, own, pieces, basis, parts, dtypes):
     seqs, tokens, features = own.shape
     cols = basis.shape[1]
-    out = pl.pallas_call(
+    shape = (seqs, 2, parts, 2, tokens, cols // parts)
+    outs = pl.pallas_call(
         lambda *refs: turn_kernel(len(late), *refs),
-        out_shape=jax.ShapeDtypeStruct(
-            (seqs, 2, parts, 2, tokens, cols // parts), jnp.float32
-        ),
+        out_shape=tuple(jax.ShapeDtypeStruct(shape, dtype) for dtype in dtypes),
         in_specs=[SCALARS] + [ANY] * (2 + len(late) + len(pieces)),
-        out_specs=WHOLE,
+        out_specs=(WHOLE,) * len(dtypes),
         scratch_shapes=[
             pltpu.VMEM((8, tokens, features), own.dtype),
             pltpu.VMEM((features, cols), basis.dtype),
-            pltpu.SemaphoreType.DMA((8,)),
+            pltpu.SemaphoreType.DMA((6,)),
         ],
         compiler_params=pltpu.CompilerParams(vmem_limit_bytes=TURN_LIMIT),
     )(at, *late, own, *pieces, basis)
-    return out.reshape(NY * parts, 2 * tokens, cols // parts)
+    return [out.reshape(NY * parts, 2 * tokens, cols // parts) for out in outs]
 
 
 def round_kernel(late_ref, v_ref, out_ref):
@@ -277,11 +287,13 @@
     act_own, act_pieces = move_tokens(at, activations)
     grad_pieces = grad_pieces + [swap_cores(v) for v in grad_pieces]
 
-    grad_part = turn(at, act_pieces, grad_own, grad_pieces, grad_rows, 1)
+    (grad_part,) = turn(at, act_pieces, grad_own, grad_pieces, grad_rows, 1, [jnp.float32])
     grad_got = lax.all_to_all(grad_part, Y, 0, 0)
     act_pieces = act_pieces + [swap_cores(v) for v in act_pieces]
-    act_part = turn(at, [grad_part], act_own, act_pieces, act_rows, NC)
-    act_got = lax.all_to_all(rounded(at, act_part), (Y, C), 0, 0)
+    act_part, act_send = turn(
+        at, [grad_part], act_own, act_pieces, act_rows, NC, [jnp.float32, jnp.bfloat16]
+    )
+    act_got = lax.all_to_all(act_send, (Y, C), 0, 0)
 
     grad_turned = sum_grads(act_part, grad_got)
     grad_panel = lax.all_gather(grad_turned, Z, axis=0, tiled=True)

time: 172 us -> 167 us (0.971)
  starting transfers between devices: 74.1 us -> 62.7 us
  waiting for transfers between devices: 22.8 us -> 32.3 us
  blocking collectives: 32.6 us -> 30.1 us
    ppermute x6 -> x4, starting transfers between devices: 21.8 us -> 15.5 us  [permute(): return lax.ppermute(v, axes, pairs)]
    ppermute x6 -> x4, waiting for transfers between devices: 1.05 us -> 6.75 us  [permute(): return lax.ppermute(v, axes, pairs)]
    all_to_all x1, waiting for transfers between devices: 0.01 us -> 2.29 us  [local(): grad_got = lax.all_to_all(grad_part, Y, 0, 0)]
    all_to_all x1, blocking collectives: 17.4 us -> 15.2 us  [local(): act_got = lax.all_to_all(act_send, (Y, C), 0, 0)]
    all_to_all x1, starting transfers between devices: 7.1 us -> 4.98 us  [local(): grad_got = lax.all_to_all(grad_part, Y, 0, 0)]
    ppermute x7 -> x5, starting transfers between devices: 14.4 us -> 12.9 us  [swap_cores(): return lax.ppermute(v, C, [(0, 1), (1, 0)])]
    unnamed x46 -> x38, local copies, waits for them, and re-layouts: 7.13 us -> 7.24 us
  transfers between devices with their start and end apart: 20 -> 16, of which waited for: 7 -> 8; matrix products, arithmetic and copies ran while one was open for 0% -> 0% of each run, Pallas kernels for 9% -> 9%
where the time goes in v5:
time: 167 us; the launch traced here: 164 us
  starting transfers between devices  62.7 us (38%)
  waiting for transfers between devices  32.3 us (19%)
  blocking collectives  30.1 us (18%)
  Pallas kernels  16.7 us (10%)
  between operations  13.7 us (8%)
  local copies, waits for them, and re-layouts  7.75 us (5%)
    ppermute x4, starting transfers between devices, permute(): return lax.ppermute(v, axes, pairs)  15.5 us
    all_to_all x1, blocking collectives, local(): act_got = lax.all_to_all(act_send, (Y, C), 0, 0)  15.2 us
    all_to_all x1, blocking collectives, local(): got = lax.all_to_all(outer, (Y, C), 0, 0).astype(jnp.float32)  14.9 us
    ppermute x2, starting transfers between devices, transpose_planes(): return lax.ppermute(v, (Z, X, H), pairs)  14.5 us
    ppermute x5, starting transfers between devices, swap_cores(): return lax.ppermute(v, C, [(0, 1), (1, 0)])  12.9 us
    all_to_all x1, starting transfers between devices, spread_z(): return lax.all_to_all(copies, Z, 0, 0)  10.3 us
    ppermute x2, waiting for transfers between devices, transpose_planes(): return lax.ppermute(v, (Z, X, H), pairs)  10.3 us
    pallas_call x2, Pallas kernels, turn(): pl.pallas_call(lambda *refs: turn_kernel(len(late), *refs), out_shape=tup...  9.48 us
  transfers between devices with their start and end apart: 16, of which 8 were waited for; matrix products, arithmetic and copies ran while one was open for 0% of the time, Pallas kernels for 9%

profile of v5, /device:TPU:6, one launch (start us, length us, event | category | flops | bytes accessed | tf_op | source)
XLA Modules:
  0.0 164.1 jit_solution(18136859359675078149)
XLA Ops:
  6.5 0.0 all-gather.3.cloned.1.call-start
  6.5 0.7 all-gather.3.cloned.1.call-update
  7.3 0.1 pad_add_fusion.at_ref.late_ref.refs_0_
  7.3 0.9 copy-done.7
  8.2 1.0 shard_map.48
  9.3 10.3 %all-to-all-start = ((bf16[8,256,256]{2,1,0:T(8,128)(2,1)}), bf16[8,256,256]{2,1,0:T(8,128)(2,1)S(1)}, u32[]{:S(2)}, u32[]{:S(2)}) async-start(bf16[8,256,256]{2,1,0:T(8,128)(2,1)} %shard_map.48), calls=%async_computation | async-start | bytes 2097152 | tf_op jit(solution)/shard_map/all_to_all | solution.py:79
  19.6 0.0 copy-done.2
  19.6 0.0 copy-start.3
  19.6 1.1 shard_map.47
  20.7 0.8 copy-done.6
  21.5 3.5 %collective-permute-start.2 = (bf16[2,64,2048]{2,1,0:T(8,128)(2,1)S(1)}, bf16[2,64,2048]{2,1,0:T(8,128)(2,1)S(1)}, u32[]{:S(2)}, u32[]{:S(2)}) collective-permute-start(bf16[2,64,2048]{2,1,0:T(8,128)(2,1)S(1)} %get-tuple-element.16), channel_id=1, source_target_pairs={{0,16},{1,51},{2,18},{3,49},{16,32},{17,1},{18,34},{19,3},{32,48},... | collective-permute-start | bytes 1572872 | tf_op jit(solution)/shard_map/ppermute | solution.py:37
  25.0 4.5 %collective-permute-start.3 = (bf16[64,2048]{1,0:T(8,128)(2,1)S(1)}, bf16[64,2048]{1,0:T(8,128)(2,1)S(1)}, u32[]{:S(2)}, u32[]{:S(2)}) collective-permute-start(bf16[64,2048]{1,0:T(8,128)(2,1)S(1)} %get-tuple-element.17), channel_id=1, source_target_pairs={{0,32},{2,34},{16,50},{18,48},{32,2},{34,0},{48,16},{50,18},{1,33}... | collective-permute-start | bytes 786440 | tf_op jit(solution)/shard_map/ppermute | solution.py:37
  29.5 1.1 shard_map.46
  30.6 0.8 copy-done.5
  31.4 2.7 %collective-permute-start = (bf16[2,64,2048]{2,1,0:T(8,128)(2,1)S(1)}, bf16[2,64,2048]{2,1,0:T(8,128)(2,1)S(1)}, u32[]{:S(2)}, u32[]{:S(2)}) collective-permute-start(bf16[2,64,2048]{2,1,0:T(8,128)(2,1)S(1)} %get-tuple-element.13), channel_id=1, source_target_pairs={{0,16},{1,51},{2,18},{3,49},{16,32},{17,1},{18,34},{19,3},{32,48},... | collective-permute-start | bytes 1572872 | tf_op jit(solution)/shard_map/ppermute | solution.py:37
  34.1 1.1 collective-permute-done.2.refs_4_
  35.2 4.6 %collective-permute-start.4 = (bf16[2,64,2048]{2,1,0:T(8,128)(2,1)S(1)}, bf16[2,64,2048]{2,1,0:T(8,128)(2,1)}, u32[]{:S(2)}, u32[]{:S(2)}) collective-permute-start(bf16[2,64,2048]{2,1,0:T(8,128)(2,1)S(1)} %collective-permute-done.2.refs_4_), channel_id=1, source_target_pairs={{0,1},{1,0},{2,3},{3,2},{4,5},{5,4},{6,7},{7,6},{8,9},{9,8},{10,11... | collective-permute-start | bytes 1572872 | tf_op jit(solution)/shard_map/ppermute | solution.py:20
  39.8 4.8 %collective-permute-start.1 = (bf16[64,2048]{1,0:T(8,128)(2,1)S(1)}, bf16[64,2048]{1,0:T(8,128)(2,1)S(1)}, u32[]{:S(2)}, u32[]{:S(2)}) collective-permute-start(bf16[64,2048]{1,0:T(8,128)(2,1)S(1)} %get-tuple-element.14), channel_id=1, source_target_pairs={{0,32},{2,34},{16,50},{18,48},{32,2},{34,0},{48,16},{50,18},{1,33}... | collective-permute-start | bytes 786440 | tf_op jit(solution)/shard_map/ppermute | solution.py:37
  44.6 0.0 collective-permute-done.3.refs_5_
  44.6 0.0 copy-start.16
  44.6 2.1 %collective-permute-start.5 = (bf16[64,2048]{1,0:T(8,128)(2,1)S(1)}, bf16[64,2048]{1,0:T(8,128)(2,1)S(1)}, u32[]{:S(2)}, u32[]{:S(2)}) collective-permute-start(bf16[64,2048]{1,0:T(8,128)(2,1)S(1)} %collective-permute-done.3.refs_5_), channel_id=1, source_target_pairs={{0,1},{1,0},{2,3},{3,2},{4,5},{5,4},{6,7},{7,6},{8,9},{9,8},{10,11... | collective-permute-start | bytes 786440 | tf_op jit(solution)/shard_map/ppermute | solution.py:20
  46.8 5.6 %collective-permute-done.1.refs_2_.refs_4_ = bf16[64,2048]{1,0:T(8,128)(2,1)S(1)} collective-permute-done((bf16[64,2048]{1,0:T(8,128)(2,1)S(1)}, bf16[64,2048]{1,0:T(8,128)(2,1)S(1)}, u32[]{:S(2)}, u32[]{:S(2)}) %collective-permute-start.1) | collective-permute-done | bytes 262176 | tf_op jit(solution)/shard_map/ppermute | solution.py:37
  52.4 0.0 collective-permute-done.refs_1_.refs_3_
  52.4 0.0 collective-permute-done.5.refs_7_
  52.4 0.0 collective-permute-done.4.refs_6_
  52.4 3.6 %all-to-all-done = bf16[8,256,256]{2,1,0:T(8,128)(2,1)S(1)} async-done(((bf16[8,256,256]{2,1,0:T(8,128)(2,1)}), bf16[8,256,256]{2,1,0:T(8,128)(2,1)S(1)}, u32[]{:S(2)}, u32[]{:S(2)}) %all-to-all-start) | async-done | bytes 1048608 | tf_op jit(solution)/shard_map/all_to_all | solution.py:79
  56.0 0.0 copy-done.16
  56.0 1.0 copy-done.10
  57.0 4.1 %shard_map.49 = f32[2,2,1,2,64,256]{5,4,3,2,1,0:T(8,128)} custom-call(s32[3]{0:T(128)} %copy-done.8, bf16[2,64,2048]{2,1,0:T(8,128)(2,1)} %copy-done.11, bf16[64,2048]{1,0:T(8,128)(2,1)} %copy-done.12, bf16[2,64,2048]{2,1,0:T(8,128)(2,1)} %copy-done.6, bf16[2,64,2048]{2,1,0:T(8,128)(2,1)} %copy-done.13, bf16[64,2048]{1,0:T(8,128)(2,1)} %copy-done.16, ...), custom_call_target="tpu_custom_call" | custom-call | tf_op jit(solution)/shard_map/pallas_call | solution.py:165
  61.1 5.0 %all-to-all-start.3 = ((f32[4,128,256]{2,1,0:T(8,128)}), f32[4,128,256]{2,1,0:T(8,128)S(1)}, u32[]{:S(2)}, u32[]{:S(2)}) async-start(f32[4,128,256]{2,1,0:T(8,128)} %bitcast.16), calls=%async_computation.3 | async-start | bytes 1048576 | tf_op jit(solution)/shard_map/all_to_all | solution.py:291
  66.1 1.9 %collective-permute-start.6 = (bf16[2,64,2048]{2,1,0:T(8,128)(2,1)}, bf16[2,64,2048]{2,1,0:T(8,128)(2,1)S(1)}, u32[]{:S(2)}, u32[]{:S(2)}) collective-permute-start(bf16[2,64,2048]{2,1,0:T(8,128)(2,1)} %copy-done.11), channel_id=1, source_target_pairs={{0,1},{1,0},{2,3},{3,2},{4,5},{5,4},{6,7},{7,6},{8,9},{9,8},{10,11... | collective-permute-start | bytes 1572872 | tf_op jit(solution)/shard_map/ppermute | solution.py:20
  68.0 2.4 %collective-permute-start.7 = (bf16[64,2048]{1,0:T(8,128)(2,1)}, bf16[64,2048]{1,0:T(8,128)(2,1)S(1)}, u32[]{:S(2)}, u32[]{:S(2)}) collective-permute-start(bf16[64,2048]{1,0:T(8,128)(2,1)} %copy-done.12), channel_id=1, source_target_pairs={{0,1},{1,0},{2,3},{3,2},{4,5},{5,4},{6,7},{7,6},{8,9},{9,8},{10,11... | collective-permute-start | bytes 786440 | tf_op jit(solution)/shard_map/ppermute | solution.py:20
  70.4 1.4 collective-permute-done.7.refs_6_
  71.8 0.0 collective-permute-done.6.refs_5_
  71.8 0.0 all-gather.3.cloned.1.call-done.refs_7_
  71.8 0.7 copy-done.18
  72.5 0.2 copy-done.14
  72.7 5.4 %shard_map.50 = (f32[2,2,2,2,64,192]{5,4,3,2,1,0:T(8,128)}, bf16[2,2,2,2,64,192]{5,4,3,2,1,0:T(8,128)(2,1)}) custom-call(s32[3]{0:T(128)} %copy-done.8, f32[4,128,256]{2,1,0:T(8,128)} %bitcast.17, bf16[2,64,2048]{2,1,0:T(8,128)(2,1)} %copy-done.5, bf16[2,64,2048]{2,1,0:T(8,128)(2,1)} %copy-done.11, bf16[64,2048]{1,0:T(8,128)(2,1)} %copy-done.12, ...), custom_call_target="tpu_custom_call" | custom-call | tf_op jit(solution)/shard_map/pallas_call | solution.py:165
  78.1 2.3 %all-to-all-done.3.got_ref = f32[4,128,256]{2,1,0:T(8,128)S(1)} async-done(((f32[4,128,256]{2,1,0:T(8,128)}), f32[4,128,256]{2,1,0:T(8,128)S(1)}, u32[]{:S(2)}, u32[]{:S(2)}) %all-to-all-start.3) | async-done | bytes 524320 | tf_op jit(solution)/shard_map/all_to_all | solution.py:291
  80.4 1.2 copy-done
  81.6 0.7 shard_map.53
  82.3 0.0 all-gather.5.cloned.1.call-update
  82.3 0.4 copy-done.15
  82.7 0.3 copy.5
  83.0 15.2 %all_to_all.25 = bf16[8,128,192]{1,2,0:T(8,128)(2,1)S(1)} all-to-all(bf16[8,128,192]{1,2,0:T(8,128)(2,1)S(1)} %copy.5), channel_id=1, replica_groups=mesh['z'=8,'y'=4,'x'=4,'h'=2,'c'=2] {'y','c'}, dimensions={0} | all-to-all | bytes 786432 | tf_op jit(solution)/shard_map/all_to_all | solution.py:296
  98.2 0.2 copy.6.got_ref
  98.4 0.0 copy-done.1
  98.4 0.0 copy-done.9
  98.4 0.7 shard_map.51
  99.1 3.3 %collective-permute-start.8 = (bf16[128,384]{1,0:T(8,128)(2,1)S(1)}, bf16[128,384]{1,0:T(8,128)(2,1)S(1)}, u32[]{:S(2)}, u32[]{:S(2)}) collective-permute-start(bf16[128,384]{1,0:T(8,128)(2,1)S(1)} %shard_map.51), channel_id=1, source_target_pairs={{0,0},{2,64},{4,128},{6,192},{8,256},{10,320},{12,384},{14,448},{6... | collective-permute-start | bytes 294920 | tf_op jit(solution)/shard_map/ppermute | solution.py:62
  102.4 11.2 %collective-permute-start.9 = (bf16[128,384]{1,0:T(8,128)(2,1)S(1)}, bf16[128,384]{1,0:T(8,128)(2,1)S(1)}, u32[]{:S(2)}, u32[]{:S(2)}) collective-permute-start(bf16[128,384]{1,0:T(8,128)(2,1)S(1)} %shard_map.51), channel_id=1, source_target_pairs={{0,2},{2,66},{4,130},{6,194},{8,258},{10,322},{12,386},{14,450},{6... | collective-permute-start | bytes 294920 | tf_op jit(solution)/shard_map/ppermute | solution.py:62
  113.6 4.5 %collective-permute-done.8.near_ref = bf16[128,384]{1,0:T(8,128)(2,1)S(1)} collective-permute-done((bf16[128,384]{1,0:T(8,128)(2,1)S(1)}, bf16[128,384]{1,0:T(8,128)(2,1)S(1)}, u32[]{:S(2)}, u32[]{:S(2)}) %collective-permute-start.8) | collective-permute-done | bytes 98336 | tf_op jit(solution)/shard_map/ppermute | solution.py:62
  118.1 5.8 %collective-permute-done.9.far_ref = bf16[128,384]{1,0:T(8,128)(2,1)S(1)} collective-permute-done((bf16[128,384]{1,0:T(8,128)(2,1)S(1)}, bf16[128,384]{1,0:T(8,128)(2,1)S(1)}, u32[]{:S(2)}, u32[]{:S(2)}) %collective-permute-start.9) | collective-permute-done | bytes 98336 | tf_op jit(solution)/shard_map/ppermute | solution.py:62
  123.9 1.5 shard_map.52.late_ref
  125.4 4.5 %all-to-all-start.2 = ((bf16[4,2,128,384]{3,2,1,0:T(8,128)(2,1)}), bf16[4,2,128,384]{3,2,1,0:T(8,128)(2,1)S(1)}, u32[]{:S(2)}, u32[]{:S(2)}) async-start(bf16[4,2,128,384]{3,2,1,0:T(8,128)(2,1)} %shard_map.52.late_ref), calls=%async_computation.2 | async-start | bytes 1572864 | tf_op jit(solution)/shard_map/all_to_all | solution.py:304
  129.9 1.2 copy-done.4
  131.1 0.1 shard_map.54.mine_ref
  131.1 1.9 %collective-permute-start.10 = (bf16[1024,256]{1,0:T(8,128)(2,1)S(1)}, bf16[1024,256]{1,0:T(8,128)(2,1)S(1)}, u32[]{:S(2)}, u32[]{:S(2)}) collective-permute-start(bf16[1024,256]{1,0:T(8,128)(2,1)S(1)} %shard_map.54.mine_ref), channel_id=1, source_target_pairs={{0,1},{1,0},{2,3},{3,2},{4,5},{5,4},{6,7},{7,6},{8,9},{9,8},{10,11... | collective-permute-start | bytes 1572872 | tf_op jit(solution)/shard_map/ppermute | solution.py:20
  133.1 7.3 %all-to-all-done.2 = bf16[4,2,128,384]{3,2,1,0:T(8,128)(2,1)S(1)} async-done(((bf16[4,2,128,384]{3,2,1,0:T(8,128)(2,1)}), bf16[4,2,128,384]{3,2,1,0:T(8,128)(2,1)S(1)}, u32[]{:S(2)}, u32[]{:S(2)}) %all-to-all-start.2) | async-done | bytes 786464 | tf_op jit(solution)/shard_map/all_to_all | solution.py:304
  140.4 0.0 collective-permute-done.10.other_ref
  140.4 1.1 shard_map.55
  141.5 14.9 %all_to_all.26 = bf16[8,96,256]{2,1,0:T(8,128)(2,1)S(1)} all-to-all(bf16[8,96,256]{2,1,0:T(8,128)(2,1)S(1)} %bitcast.15), channel_id=1, replica_groups=mesh['z'=8,'y'=4,'x'=4,'h'=2,'c'=2] {'y','c'}, dimensions={0} | all-to-all | bytes 786432 | tf_op jit(solution)/shard_map/all_to_all | solution.py:308
  156.5 0.1 convert_element_type.3
  156.5 0.7 fusion.2
  (25 shorter events, 0.0 us)
Async XLA Ops:
  6.5 13.1 %copy-start.2 = (bf16[2,64,8192]{2,1,0:T(8,128)(2,1)S(1)}, bf16[2,64,8192]{2,1,0:T(8,128)(2,1)}, u32[]{:S(2)}) copy-start(bf16[2,64,8192]{2,1,0:T(8,128)(2,1)} %values_ref.3) | copy-start | bytes 6291460
  6.5 65.2 %all-gather.3.cloned.1.call-start = ((), (), s32[]{:S(2)}) async-start(), calls=%async_computation.5 | async-start | bytes 1769472 | tf_op jit(solution)/shard_map/all_gather | solution.py:283
  7.3 0.9 copy-start.7
  8.2 21.2 %copy-start.8 = (s32[3]{0:T(128)}, s32[3]{0:T(128)S(1)}, u32[]{:S(2)}) copy-start(s32[3]{0:T(128)S(1)} %pad_add_fusion.at_ref.late_ref.refs_0_) | copy-start | bytes 40
  9.3 46.7 %all-to-all-start = ((bf16[8,256,256]{2,1,0:T(8,128)(2,1)}), bf16[8,256,256]{2,1,0:T(8,128)(2,1)S(1)}, u32[]{:S(2)}, u32[]{:S(2)}) async-start(bf16[8,256,256]{2,1,0:T(8,128)(2,1)} %shard_map.48), calls=%async_computation | async-start | bytes 2097152 | tf_op jit(solution)/shard_map/all_to_all | solution.py:79
  19.6 9.9 %copy-start.3 = (bf16[2,64,8192]{2,1,0:T(8,128)(2,1)S(1)}, bf16[2,64,8192]{2,1,0:T(8,128)(2,1)}, u32[]{:S(2)}) copy-start(bf16[2,64,8192]{2,1,0:T(8,128)(2,1)} %values_ref.2) | copy-start | bytes 6291460
  20.7 0.8 copy-start.6
  21.5 13.7 %collective-permute-start.2 = (bf16[2,64,2048]{2,1,0:T(8,128)(2,1)S(1)}, bf16[2,64,2048]{2,1,0:T(8,128)(2,1)S(1)}, u32[]{:S(2)}, u32[]{:S(2)}) collective-permute-start(bf16[2,64,2048]{2,1,0:T(8,128)(2,1)S(1)} %get-tuple-element.16), channel_id=1, source_target_pairs={{0,16},{1,51},{2,18},{3,49},{16,32},{17,1},{18,34},{19,3},{32,48},... | collective-permute-start | bytes 1572872 | tf_op jit(solution)/shard_map/ppermute | solution.py:37
  25.0 19.6 %collective-permute-start.3 = (bf16[64,2048]{1,0:T(8,128)(2,1)S(1)}, bf16[64,2048]{1,0:T(8,128)(2,1)S(1)}, u32[]{:S(2)}, u32[]{:S(2)}) collective-permute-start(bf16[64,2048]{1,0:T(8,128)(2,1)S(1)} %get-tuple-element.17), channel_id=1, source_target_pairs={{0,32},{2,34},{16,50},{18,48},{32,2},{34,0},{48,16},{50,18},{1,33}... | collective-permute-start | bytes 786440 | tf_op jit(solution)/shard_map/ppermute | solution.py:37
  30.6 0.8 copy-start.5
  31.4 21.0 %collective-permute-start = (bf16[2,64,2048]{2,1,0:T(8,128)(2,1)S(1)}, bf16[2,64,2048]{2,1,0:T(8,128)(2,1)S(1)}, u32[]{:S(2)}, u32[]{:S(2)}) collective-permute-start(bf16[2,64,2048]{2,1,0:T(8,128)(2,1)S(1)} %get-tuple-element.13), channel_id=1, source_target_pairs={{0,16},{1,51},{2,18},{3,49},{16,32},{17,1},{18,34},{19,3},{32,48},... | collective-permute-start | bytes 1572872 | tf_op jit(solution)/shard_map/ppermute | solution.py:37
  35.2 17.2 %copy-start.13 = (bf16[2,64,2048]{2,1,0:T(8,128)(2,1)}, bf16[2,64,2048]{2,1,0:T(8,128)(2,1)S(1)}, u32[]{:S(2)}) copy-start(bf16[2,64,2048]{2,1,0:T(8,128)(2,1)S(1)} %collective-permute-done.2.refs_4_) | copy-start | bytes 1572868
  35.2 17.2 %collective-permute-start.4 = (bf16[2,64,2048]{2,1,0:T(8,128)(2,1)S(1)}, bf16[2,64,2048]{2,1,0:T(8,128)(2,1)}, u32[]{:S(2)}, u32[]{:S(2)}) collective-permute-start(bf16[2,64,2048]{2,1,0:T(8,128)(2,1)S(1)} %collective-permute-done.2.refs_4_), channel_id=1, source_target_pairs={{0,1},{1,0},{2,3},{3,2},{4,5},{5,4},{6,7},{7,6},{8,9},{9,8},{10,11... | collective-permute-start | bytes 1572872 | tf_op jit(solution)/shard_map/ppermute | solution.py:20
  39.8 12.6 %collective-permute-start.1 = (bf16[64,2048]{1,0:T(8,128)(2,1)S(1)}, bf16[64,2048]{1,0:T(8,128)(2,1)S(1)}, u32[]{:S(2)}, u32[]{:S(2)}) collective-permute-start(bf16[64,2048]{1,0:T(8,128)(2,1)S(1)} %get-tuple-element.14), channel_id=1, source_target_pairs={{0,32},{2,34},{16,50},{18,48},{32,2},{34,0},{48,16},{50,18},{1,33}... | collective-permute-start | bytes 786440 | tf_op jit(solution)/shard_map/ppermute | solution.py:37
  44.6 11.4 %copy-start.16 = (bf16[64,2048]{1,0:T(8,128)(2,1)}, bf16[64,2048]{1,0:T(8,128)(2,1)S(1)}, u32[]{:S(2)}) copy-start(bf16[64,2048]{1,0:T(8,128)(2,1)S(1)} %collective-permute-done.3.refs_5_) | copy-start | bytes 786436
  44.6 7.8 %collective-permute-start.5 = (bf16[64,2048]{1,0:T(8,128)(2,1)S(1)}, bf16[64,2048]{1,0:T(8,128)(2,1)S(1)}, u32[]{:S(2)}, u32[]{:S(2)}) collective-permute-start(bf16[64,2048]{1,0:T(8,128)(2,1)S(1)} %collective-permute-done.3.refs_5_), channel_id=1, source_target_pairs={{0,1},{1,0},{2,3},{3,2},{4,5},{5,4},{6,7},{7,6},{8,9},{9,8},{10,11... | collective-permute-start | bytes 786440 | tf_op jit(solution)/shard_map/ppermute | solution.py:20
  52.4 3.6 %copy-start.12 = (bf16[64,2048]{1,0:T(8,128)(2,1)}, bf16[64,2048]{1,0:T(8,128)(2,1)S(1)}, u32[]{:S(2)}) copy-start(bf16[64,2048]{1,0:T(8,128)(2,1)S(1)} %collective-permute-done.1.refs_2_.refs_4_) | copy-start | bytes 786436
  52.4 3.6 %copy-start.11 = (bf16[2,64,2048]{2,1,0:T(8,128)(2,1)}, bf16[2,64,2048]{2,1,0:T(8,128)(2,1)S(1)}, u32[]{:S(2)}) copy-start(bf16[2,64,2048]{2,1,0:T(8,128)(2,1)S(1)} %collective-permute-done.refs_1_.refs_3_) | copy-start | bytes 1572868
  52.4 3.6 %copy-start.17 = (bf16[64,2048]{1,0:T(8,128)(2,1)}, bf16[64,2048]{1,0:T(8,128)(2,1)S(1)}, u32[]{:S(2)}) copy-start(bf16[64,2048]{1,0:T(8,128)(2,1)S(1)} %collective-permute-done.5.refs_7_) | copy-start | bytes 786436
  56.0 1.0 copy-start.10
  61.1 19.3 %all-to-all-start.3 = ((f32[4,128,256]{2,1,0:T(8,128)}), f32[4,128,256]{2,1,0:T(8,128)S(1)}, u32[]{:S(2)}, u32[]{:S(2)}) async-start(f32[4,128,256]{2,1,0:T(8,128)} %bitcast.16), calls=%async_computation.3 | async-start | bytes 1048576 | tf_op jit(solution)/shard_map/all_to_all | solution.py:291
  66.1 63.8 %all-gather.5.cloned.1.call-start = ((), (), s32[]{:S(2)}) async-start(), calls=%async_computation.6 | async-start | bytes 1179648 | tf_op jit(solution)/shard_map/all_gather | solution.py:299
  66.1 5.7 %collective-permute-start.6 = (bf16[2,64,2048]{2,1,0:T(8,128)(2,1)}, bf16[2,64,2048]{2,1,0:T(8,128)(2,1)S(1)}, u32[]{:S(2)}, u32[]{:S(2)}) collective-permute-start(bf16[2,64,2048]{2,1,0:T(8,128)(2,1)} %copy-done.11), channel_id=1, source_target_pairs={{0,1},{1,0},{2,3},{3,2},{4,5},{5,4},{6,7},{7,6},{8,9},{9,8},{10,11... | collective-permute-start | bytes 1572872 | tf_op jit(solution)/shard_map/ppermute | solution.py:20
  68.0 3.8 %collective-permute-start.7 = (bf16[64,2048]{1,0:T(8,128)(2,1)}, bf16[64,2048]{1,0:T(8,128)(2,1)S(1)}, u32[]{:S(2)}, u32[]{:S(2)}) collective-permute-start(bf16[64,2048]{1,0:T(8,128)(2,1)} %copy-done.12), channel_id=1, source_target_pairs={{0,1},{1,0},{2,3},{3,2},{4,5},{5,4},{6,7},{7,6},{8,9},{9,8},{10,11... | collective-permute-start | bytes 786440 | tf_op jit(solution)/shard_map/ppermute | solution.py:20
  71.8 0.7 copy-start.18
  71.8 0.9 copy-start.14
  80.4 1.2 copy-start
  81.6 1.1 copy-start.15
  81.6 16.8 %copy-start.1 = (f32[2,2,2,2,64,192]{5,4,3,2,1,0:T(8,128)S(1)}, f32[2,2,2,2,64,192]{5,4,3,2,1,0:T(8,128)}, u32[]{:S(2)}) copy-start(f32[2,2,2,2,64,192]{5,4,3,2,1,0:T(8,128)} %get-tuple-element.19) | copy-start | bytes 2359300
  81.6 16.8 %copy-start.9 = (s32[3]{0:T(128)S(1)}, s32[3]{0:T(128)}, u32[]{:S(2)}) copy-start(s32[3]{0:T(128)} %copy-done.8) | copy-start | bytes 40
  99.1 19.0 %collective-permute-start.8 = (bf16[128,384]{1,0:T(8,128)(2,1)S(1)}, bf16[128,384]{1,0:T(8,128)(2,1)S(1)}, u32[]{:S(2)}, u32[]{:S(2)}) collective-permute-start(bf16[128,384]{1,0:T(8,128)(2,1)S(1)} %shard_map.51), channel_id=1, source_target_pairs={{0,0},{2,64},{4,128},{6,192},{8,256},{10,320},{12,384},{14,448},{6... | collective-permute-start | bytes 294920 | tf_op jit(solution)/shard_map/ppermute | solution.py:62
  102.4 21.5 %collective-permute-start.9 = (bf16[128,384]{1,0:T(8,128)(2,1)S(1)}, bf16[128,384]{1,0:T(8,128)(2,1)S(1)}, u32[]{:S(2)}, u32[]{:S(2)}) collective-permute-start(bf16[128,384]{1,0:T(8,128)(2,1)S(1)} %shard_map.51), channel_id=1, source_target_pairs={{0,2},{2,66},{4,130},{6,194},{8,258},{10,322},{12,386},{14,450},{6... | collective-permute-start | bytes 294920 | tf_op jit(solution)/shard_map/ppermute | solution.py:62
  125.4 15.0 %all-to-all-start.2 = ((bf16[4,2,128,384]{3,2,1,0:T(8,128)(2,1)}), bf16[4,2,128,384]{3,2,1,0:T(8,128)(2,1)S(1)}, u32[]{:S(2)}, u32[]{:S(2)}) async-start(bf16[4,2,128,384]{3,2,1,0:T(8,128)(2,1)} %shard_map.52.late_ref), calls=%async_computation.2 | async-start | bytes 1572864 | tf_op jit(solution)/shard_map/all_to_all | solution.py:304
  129.9 1.2 copy-start.4
  131.1 9.2 %collective-permute-start.10 = (bf16[1024,256]{1,0:T(8,128)(2,1)S(1)}, bf16[1024,256]{1,0:T(8,128)(2,1)S(1)}, u32[]{:S(2)}, u32[]{:S(2)}) collective-permute-start(bf16[1024,256]{1,0:T(8,128)(2,1)S(1)} %shard_map.54.mine_ref), channel_id=1, source_target_pairs={{0,1},{1,0},{2,3},{3,2},{4,5},{5,4},{6,7},{7,6},{8,9},{9,8},{10,11... | collective-permute-start | bytes 1572872 | tf_op jit(solution)/shard_map/ppermute | solution.py:20
Sparse Core Ops, SparseCore 0:
  9.4 56.5 all-gather.2
  82.4 46.3 all-gather.4

commit v6 on v5

--- a/solution.py
+++ b/solution.py
@@ -172,7 +172,9 @@
             pltpu.VMEM((features, cols), basis.dtype),
             pltpu.SemaphoreType.DMA((6,)),
         ],
-        compiler_params=pltpu.CompilerParams(vmem_limit_bytes=TURN_LIMIT),
+        compiler_params=pltpu.CompilerParams(
+            vmem_limit_bytes=TURN_LIMIT if parts > 1 else VMEM_LIMIT
+        ),
     )(at, *late, own, *pieces, basis)
     return [out.reshape(NY * parts, 2 * tokens, cols // parts) for out in outs]
 

time: 167 us -> 166 us (level)
  local copies, waits for them, and re-layouts: 7.75 us -> 10.1 us
  Pallas kernels: 16.7 us -> 14.9 us
    unnamed x38 -> x40, local copies, waits for them, and re-layouts: 7.24 us -> 9.62 us
    pallas_call x2, Pallas kernels: 9.48 us -> 7.68 us  [turn(): pl.pallas_call(lambda *refs: turn_kernel(len(late), *refs), out_shape=tup...]
  transfers between devices with their start and end apart: 16 -> 16, of which waited for: 8 -> 8; matrix products, arithmetic and copies ran while one was open for 0% -> 0% of each run, Pallas kernels for 9% -> 8%
where the time goes in v6:
time: 166 us; the launch traced here: 163 us
  starting transfers between devices  62.7 us (38%)
  waiting for transfers between devices  30.8 us (19%)
  blocking collectives  30 us (18%)
  Pallas kernels  14.9 us (9%)
  between operations  13.7 us (8%)
  local copies, waits for them, and re-layouts  10.1 us (6%)
    ppermute x4, starting transfers between devices, permute(): return lax.ppermute(v, axes, pairs)  15.6 us
    all_to_all x1, blocking collectives, local(): act_got = lax.all_to_all(act_send, (Y, C), 0, 0)  15.1 us
    all_to_all x1, blocking collectives, local(): got = lax.all_to_all(outer, (Y, C), 0, 0).astype(jnp.float32)  14.9 us
    ppermute x2, starting transfers between devices, transpose_planes(): return lax.ppermute(v, (Z, X, H), pairs)  14.4 us
    ppermute x5, starting transfers between devices, swap_cores(): return lax.ppermute(v, C, [(0, 1), (1, 0)])  12.9 us
    ppermute x2, waiting for transfers between devices, transpose_planes(): return lax.ppermute(v, (Z, X, H), pairs)  10.3 us
    all_to_all x1, starting transfers between devices, spread_z(): return lax.all_to_all(copies, Z, 0, 0)  10.3 us
    unnamed x40, local copies, waits for them, and re-layouts  9.62 us
  transfers between devices with their start and end apart: 16, of which 8 were waited for; matrix products, arithmetic and copies ran while one was open for 0% of the time, Pallas kernels for 8%

profile of v6, /device:TPU:6, one launch (start us, length us, event | category | flops | bytes accessed | tf_op | source)
XLA Modules:
  0.0 163.0 jit_solution(9809027203425403139)
XLA Ops:
  6.5 0.0 all-gather.3.cloned.1.call-start
  6.5 0.7 all-gather.3.cloned.1.call-update
  7.3 0.1 pad_add_fusion.at_ref.late_ref.refs_0_
  7.3 0.9 copy-done.14
  8.2 1.0 shard_map.48
  9.3 10.3 %all-to-all-start = ((bf16[8,256,256]{2,1,0:T(8,128)(2,1)}), bf16[8,256,256]{2,1,0:T(8,128)(2,1)S(1)}, u32[]{:S(2)}, u32[]{:S(2)}) async-start(bf16[8,256,256]{2,1,0:T(8,128)(2,1)} %shard_map.48), calls=%async_computation | async-start | bytes 2097152 | tf_op jit(solution)/shard_map/all_to_all | solution.py:79
  19.6 0.0 copy-done.3
  19.6 0.0 copy-start.4
  19.6 1.1 shard_map.47
  20.7 0.8 copy-done.8
  21.5 3.6 %collective-permute-start.2 = (bf16[2,64,2048]{2,1,0:T(8,128)(2,1)S(1)}, bf16[2,64,2048]{2,1,0:T(8,128)(2,1)S(1)}, u32[]{:S(2)}, u32[]{:S(2)}) collective-permute-start(bf16[2,64,2048]{2,1,0:T(8,128)(2,1)S(1)} %get-tuple-element.16), channel_id=1, source_target_pairs={{0,16},{1,51},{2,18},{3,49},{16,32},{17,1},{18,34},{19,3},{32,48},... | collective-permute-start | bytes 1572872 | tf_op jit(solution)/shard_map/ppermute | solution.py:37
  25.1 4.5 %collective-permute-start.3 = (bf16[64,2048]{1,0:T(8,128)(2,1)S(1)}, bf16[64,2048]{1,0:T(8,128)(2,1)S(1)}, u32[]{:S(2)}, u32[]{:S(2)}) collective-permute-start(bf16[64,2048]{1,0:T(8,128)(2,1)S(1)} %get-tuple-element.17), channel_id=1, source_target_pairs={{0,32},{2,34},{16,50},{18,48},{32,2},{34,0},{48,16},{50,18},{1,33}... | collective-permute-start | bytes 786440 | tf_op jit(solution)/shard_map/ppermute | solution.py:37
  29.6 1.1 shard_map.46
  30.7 0.8 copy-done.7
  31.5 2.7 %collective-permute-start = (bf16[2,64,2048]{2,1,0:T(8,128)(2,1)S(1)}, bf16[2,64,2048]{2,1,0:T(8,128)(2,1)S(1)}, u32[]{:S(2)}, u32[]{:S(2)}) collective-permute-start(bf16[2,64,2048]{2,1,0:T(8,128)(2,1)S(1)} %get-tuple-element.13), channel_id=1, source_target_pairs={{0,16},{1,51},{2,18},{3,49},{16,32},{17,1},{18,34},{19,3},{32,48},... | collective-permute-start | bytes 1572872 | tf_op jit(solution)/shard_map/ppermute | solution.py:37
  34.2 1.1 collective-permute-done.2.refs_4_
  35.3 4.6 %collective-permute-start.4 = (bf16[2,64,2048]{2,1,0:T(8,128)(2,1)S(1)}, bf16[2,64,2048]{2,1,0:T(8,128)(2,1)S(1)}, u32[]{:S(2)}, u32[]{:S(2)}) collective-permute-start(bf16[2,64,2048]{2,1,0:T(8,128)(2,1)S(1)} %collective-permute-done.2.refs_4_), channel_id=1, source_target_pairs={{0,1},{1,0},{2,3},{3,2},{4,5},{5,4},{6,7},{7,6},{8,9},{9,8},{10,11... | collective-permute-start | bytes 1572872 | tf_op jit(solution)/shard_map/ppermute | solution.py:20
  39.9 4.8 %collective-permute-start.1 = (bf16[64,2048]{1,0:T(8,128)(2,1)S(1)}, bf16[64,2048]{1,0:T(8,128)(2,1)S(1)}, u32[]{:S(2)}, u32[]{:S(2)}) collective-permute-start(bf16[64,2048]{1,0:T(8,128)(2,1)S(1)} %get-tuple-element.14), channel_id=1, source_target_pairs={{0,32},{2,34},{16,50},{18,48},{32,2},{34,0},{48,16},{50,18},{1,33}... | collective-permute-start | bytes 786440 | tf_op jit(solution)/shard_map/ppermute | solution.py:37
  44.7 0.0 collective-permute-done.3.refs_5_
  44.7 2.1 %collective-permute-start.5 = (bf16[64,2048]{1,0:T(8,128)(2,1)S(1)}, bf16[64,2048]{1,0:T(8,128)(2,1)S(1)}, u32[]{:S(2)}, u32[]{:S(2)}) collective-permute-start(bf16[64,2048]{1,0:T(8,128)(2,1)S(1)} %collective-permute-done.3.refs_5_), channel_id=1, source_target_pairs={{0,1},{1,0},{2,3},{3,2},{4,5},{5,4},{6,7},{7,6},{8,9},{9,8},{10,11... | collective-permute-start | bytes 786440 | tf_op jit(solution)/shard_map/ppermute | solution.py:20
  46.9 0.0 copy-start.10
  46.9 0.7 copy-done.10
  47.6 4.9 %collective-permute-done.1.refs_2_.refs_4_ = bf16[64,2048]{1,0:T(8,128)(2,1)S(1)} collective-permute-done((bf16[64,2048]{1,0:T(8,128)(2,1)S(1)}, bf16[64,2048]{1,0:T(8,128)(2,1)S(1)}, u32[]{:S(2)}, u32[]{:S(2)}) %collective-permute-start.1) | collective-permute-done | bytes 262176 | tf_op jit(solution)/shard_map/ppermute | solution.py:37
  52.5 0.0 collective-permute-done.refs_1_.refs_3_
  52.5 0.0 collective-permute-done.5.refs_7_
  52.5 0.7 copy-done.12
  53.3 0.0 collective-permute-done.4.refs_6_
  53.3 2.7 %all-to-all-done = bf16[8,256,256]{2,1,0:T(8,128)(2,1)S(1)} async-done(((bf16[8,256,256]{2,1,0:T(8,128)(2,1)}), bf16[8,256,256]{2,1,0:T(8,128)(2,1)S(1)}, u32[]{:S(2)}, u32[]{:S(2)}) %all-to-all-start) | async-done | bytes 1048608 | tf_op jit(solution)/shard_map/all_to_all | solution.py:79
  56.0 0.9 copy-done.11
  57.0 0.9 copy-done.13
  57.9 2.3 %shard_map.49 = f32[2,2,1,2,64,256]{5,4,3,2,1,0:T(8,128)} custom-call(s32[3]{0:T(128)S(1)} %pad_add_fusion.at_ref.late_ref.refs_0_, bf16[2,64,2048]{2,1,0:T(8,128)(2,1)S(1)} %collective-permute-done.refs_1_.refs_3_, bf16[64,2048]{1,0:T(8,128)(2,1)S(1)} %collective-permute-done.1.refs_2_.refs_4_, bf16[2,64,2048]{2,1,0:T(8,128)(2,1)S(1)} %copy-done.9, ...), custom_call_target="tpu_custom_call" | custom-call | tf_op jit(solution)/shard_map/pallas_call | solution.py:165
  60.2 5.0 %all-to-all-start.3 = ((f32[4,128,256]{2,1,0:T(8,128)}), f32[4,128,256]{2,1,0:T(8,128)S(1)}, u32[]{:S(2)}, u32[]{:S(2)}) async-start(f32[4,128,256]{2,1,0:T(8,128)} %bitcast.4.refs_1_), calls=%async_computation.3 | async-start | bytes 1048576 | tf_op jit(solution)/shard_map/all_to_all | solution.py:293
  65.2 1.9 %collective-permute-start.6 = (bf16[2,64,2048]{2,1,0:T(8,128)(2,1)S(1)}, bf16[2,64,2048]{2,1,0:T(8,128)(2,1)S(1)}, u32[]{:S(2)}, u32[]{:S(2)}) collective-permute-start(bf16[2,64,2048]{2,1,0:T(8,128)(2,1)S(1)} %collective-permute-done.refs_1_.refs_3_), channel_id=1, source_target_pairs={{0,1},{1,0},{2,3},{3,2},{4,5},{5,4},{6,7},{7,6},{8,9},{9,8},{10,11... | collective-permute-start | bytes 1572872 | tf_op jit(solution)/shard_map/ppermute | solution.py:20
  67.1 2.4 %collective-permute-start.7 = (bf16[64,2048]{1,0:T(8,128)(2,1)S(1)}, bf16[64,2048]{1,0:T(8,128)(2,1)S(1)}, u32[]{:S(2)}, u32[]{:S(2)}) collective-permute-start(bf16[64,2048]{1,0:T(8,128)(2,1)S(1)} %collective-permute-done.1.refs_2_.refs_4_), channel_id=1, source_target_pairs={{0,1},{1,0},{2,3},{3,2},{4,5},{5,4},{6,7},{7,6},{8,9},{9,8},{10,11... | collective-permute-start | bytes 786440 | tf_op jit(solution)/shard_map/ppermute | solution.py:20
  69.6 1.1 collective-permute-done.7.refs_6_
  70.7 0.0 collective-permute-done.6.refs_5_
  70.7 0.0 all-gather.3.cloned.1.call-done.refs_7_
  70.7 0.7 copy-done.19
  71.4 0.2 copy-done.17
  71.6 5.4 %shard_map.50 = (f32[2,2,2,2,64,192]{5,4,3,2,1,0:T(8,128)}, bf16[2,2,2,2,64,192]{5,4,3,2,1,0:T(8,128)(2,1)}) custom-call(s32[3]{0:T(128)} %copy-done.15, f32[4,128,256]{2,1,0:T(8,128)} %bitcast.4.refs_1_, bf16[2,64,2048]{2,1,0:T(8,128)(2,1)} %copy-done.7, bf16[2,64,2048]{2,1,0:T(8,128)(2,1)} %copy-done.2, bf16[64,2048]{1,0:T(8,128)(2,1)} %copy-done.5, ...), custom_call_target="tpu_custom_call" | custom-call | tf_op jit(solution)/shard_map/pallas_call | solution.py:165
  77.0 2.5 %all-to-all-done.3.got_ref = f32[4,128,256]{2,1,0:T(8,128)S(1)} async-done(((f32[4,128,256]{2,1,0:T(8,128)}), f32[4,128,256]{2,1,0:T(8,128)S(1)}, u32[]{:S(2)}, u32[]{:S(2)}) %all-to-all-start.3) | async-done | bytes 524320 | tf_op jit(solution)/shard_map/all_to_all | solution.py:293
  79.5 1.2 copy-done
  80.7 0.7 shard_map.53
  81.4 0.0 all-gather.5.cloned.1.call-update
  81.4 0.4 copy-done.18
  81.8 0.3 copy.5
  82.1 15.1 %all_to_all.25 = bf16[8,128,192]{1,2,0:T(8,128)(2,1)S(1)} all-to-all(bf16[8,128,192]{1,2,0:T(8,128)(2,1)S(1)} %copy.5), channel_id=1, replica_groups=mesh['z'=8,'y'=4,'x'=4,'h'=2,'c'=2] {'y','c'}, dimensions={0} | all-to-all | bytes 786432 | tf_op jit(solution)/shard_map/all_to_all | solution.py:298
  97.2 0.2 copy.6.got_ref
  97.4 0.7 shard_map.51
  98.1 4.0 %collective-permute-start.8 = (bf16[128,384]{1,0:T(8,128)(2,1)S(1)}, bf16[128,384]{1,0:T(8,128)(2,1)S(1)}, u32[]{:S(2)}, u32[]{:S(2)}) collective-permute-start(bf16[128,384]{1,0:T(8,128)(2,1)S(1)} %shard_map.51), channel_id=1, source_target_pairs={{0,0},{2,64},{4,128},{6,192},{8,256},{10,320},{12,384},{14,448},{6... | collective-permute-start | bytes 294920 | tf_op jit(solution)/shard_map/ppermute | solution.py:62
  102.0 10.4 %collective-permute-start.9 = (bf16[128,384]{1,0:T(8,128)(2,1)S(1)}, bf16[128,384]{1,0:T(8,128)(2,1)S(1)}, u32[]{:S(2)}, u32[]{:S(2)}) collective-permute-start(bf16[128,384]{1,0:T(8,128)(2,1)S(1)} %shard_map.51), channel_id=1, source_target_pairs={{0,2},{2,66},{4,130},{6,194},{8,258},{10,322},{12,386},{14,450},{6... | collective-permute-start | bytes 294920 | tf_op jit(solution)/shard_map/ppermute | solution.py:62
  112.5 4.5 %collective-permute-done.8.near_ref = bf16[128,384]{1,0:T(8,128)(2,1)S(1)} collective-permute-done((bf16[128,384]{1,0:T(8,128)(2,1)S(1)}, bf16[128,384]{1,0:T(8,128)(2,1)S(1)}, u32[]{:S(2)}, u32[]{:S(2)}) %collective-permute-start.8) | collective-permute-done | bytes 98336 | tf_op jit(solution)/shard_map/ppermute | solution.py:62
  117.0 5.8 %collective-permute-done.9.far_ref = bf16[128,384]{1,0:T(8,128)(2,1)S(1)} collective-permute-done((bf16[128,384]{1,0:T(8,128)(2,1)S(1)}, bf16[128,384]{1,0:T(8,128)(2,1)S(1)}, u32[]{:S(2)}, u32[]{:S(2)}) %collective-permute-start.9) | collective-permute-done | bytes 98336 | tf_op jit(solution)/shard_map/ppermute | solution.py:62
  122.8 1.5 shard_map.52.late_ref
  124.3 4.5 %all-to-all-start.2 = ((bf16[4,2,128,384]{3,2,1,0:T(8,128)(2,1)}), bf16[4,2,128,384]{3,2,1,0:T(8,128)(2,1)S(1)}, u32[]{:S(2)}, u32[]{:S(2)}) async-start(bf16[4,2,128,384]{3,2,1,0:T(8,128)(2,1)} %shard_map.52.late_ref), calls=%async_computation.2 | async-start | bytes 1572864 | tf_op jit(solution)/shard_map/all_to_all | solution.py:306
  128.8 1.2 copy-done.6
  130.0 0.1 shard_map.54.mine_ref
  130.1 1.9 %collective-permute-start.10 = (bf16[1024,256]{1,0:T(8,128)(2,1)S(1)}, bf16[1024,256]{1,0:T(8,128)(2,1)S(1)}, u32[]{:S(2)}, u32[]{:S(2)}) collective-permute-start(bf16[1024,256]{1,0:T(8,128)(2,1)S(1)} %shard_map.54.mine_ref), channel_id=1, source_target_pairs={{0,1},{1,0},{2,3},{3,2},{4,5},{5,4},{6,7},{7,6},{8,9},{9,8},{10,11... | collective-permute-start | bytes 1572872 | tf_op jit(solution)/shard_map/ppermute | solution.py:20
  132.0 7.3 %all-to-all-done.2 = bf16[4,2,128,384]{3,2,1,0:T(8,128)(2,1)S(1)} async-done(((bf16[4,2,128,384]{3,2,1,0:T(8,128)(2,1)}), bf16[4,2,128,384]{3,2,1,0:T(8,128)(2,1)S(1)}, u32[]{:S(2)}, u32[]{:S(2)}) %all-to-all-start.2) | async-done | bytes 786464 | tf_op jit(solution)/shard_map/all_to_all | solution.py:306
  139.3 0.0 collective-permute-done.10.other_ref
  139.3 1.1 shard_map.55
  140.5 14.9 %all_to_all.26 = bf16[8,96,256]{2,1,0:T(8,128)(2,1)S(1)} all-to-all(bf16[8,96,256]{2,1,0:T(8,128)(2,1)S(1)} %bitcast.16), channel_id=1, replica_groups=mesh['z'=8,'y'=4,'x'=4,'h'=2,'c'=2] {'y','c'}, dimensions={0} | all-to-all | bytes 786432 | tf_op jit(solution)/shard_map/all_to_all | solution.py:310
  155.4 0.1 convert_element_type.3
  155.5 0.7 fusion.2
  (27 shorter events, 0.0 us)
Async XLA Ops:
  6.5 13.1 %copy-start.3 = (bf16[2,64,8192]{2,1,0:T(8,128)(2,1)S(1)}, bf16[2,64,8192]{2,1,0:T(8,128)(2,1)}, u32[]{:S(2)}) copy-start(bf16[2,64,8192]{2,1,0:T(8,128)(2,1)} %values_ref.3) | copy-start | bytes 6291460
  6.5 64.2 %all-gather.3.cloned.1.call-start = ((), (), s32[]{:S(2)}) async-start(), calls=%async_computation.5 | async-start | bytes 1769472 | tf_op jit(solution)/shard_map/all_gather | solution.py:285
  7.3 0.9 copy-start.14
  8.2 47.8 %copy-start.15 = (s32[3]{0:T(128)}, s32[3]{0:T(128)S(1)}, u32[]{:S(2)}) copy-start(s32[3]{0:T(128)S(1)} %pad_add_fusion.at_ref.late_ref.refs_0_) | copy-start | bytes 40
  9.3 46.7 %all-to-all-start = ((bf16[8,256,256]{2,1,0:T(8,128)(2,1)}), bf16[8,256,256]{2,1,0:T(8,128)(2,1)S(1)}, u32[]{:S(2)}, u32[]{:S(2)}) async-start(bf16[8,256,256]{2,1,0:T(8,128)(2,1)} %shard_map.48), calls=%async_computation | async-start | bytes 2097152 | tf_op jit(solution)/shard_map/all_to_all | solution.py:79
  19.6 10.0 %copy-start.4 = (bf16[2,64,8192]{2,1,0:T(8,128)(2,1)S(1)}, bf16[2,64,8192]{2,1,0:T(8,128)(2,1)}, u32[]{:S(2)}) copy-start(bf16[2,64,8192]{2,1,0:T(8,128)(2,1)} %values_ref.2) | copy-start | bytes 6291460
  20.7 0.8 copy-start.8
  21.5 34.5 %copy-start.9 = (bf16[2,64,2048]{2,1,0:T(8,128)(2,1)S(1)}, bf16[2,64,2048]{2,1,0:T(8,128)(2,1)}, u32[]{:S(2)}) copy-start(bf16[2,64,2048]{2,1,0:T(8,128)(2,1)} %copy-done.8) | copy-start | bytes 1572868
  21.5 13.9 %collective-permute-start.2 = (bf16[2,64,2048]{2,1,0:T(8,128)(2,1)S(1)}, bf16[2,64,2048]{2,1,0:T(8,128)(2,1)S(1)}, u32[]{:S(2)}, u32[]{:S(2)}) collective-permute-start(bf16[2,64,2048]{2,1,0:T(8,128)(2,1)S(1)} %get-tuple-element.16), channel_id=1, source_target_pairs={{0,16},{1,51},{2,18},{3,49},{16,32},{17,1},{18,34},{19,3},{32,48},... | collective-permute-start | bytes 1572872 | tf_op jit(solution)/shard_map/ppermute | solution.py:37
  25.1 19.6 %collective-permute-start.3 = (bf16[64,2048]{1,0:T(8,128)(2,1)S(1)}, bf16[64,2048]{1,0:T(8,128)(2,1)S(1)}, u32[]{:S(2)}, u32[]{:S(2)}) collective-permute-start(bf16[64,2048]{1,0:T(8,128)(2,1)S(1)} %get-tuple-element.17), channel_id=1, source_target_pairs={{0,32},{2,34},{16,50},{18,48},{32,2},{34,0},{48,16},{50,18},{1,33}... | collective-permute-start | bytes 786440 | tf_op jit(solution)/shard_map/ppermute | solution.py:37
  30.7 0.8 copy-start.7
  31.5 21.0 %collective-permute-start = (bf16[2,64,2048]{2,1,0:T(8,128)(2,1)S(1)}, bf16[2,64,2048]{2,1,0:T(8,128)(2,1)S(1)}, u32[]{:S(2)}, u32[]{:S(2)}) collective-permute-start(bf16[2,64,2048]{2,1,0:T(8,128)(2,1)S(1)} %get-tuple-element.13), channel_id=1, source_target_pairs={{0,16},{1,51},{2,18},{3,49},{16,32},{17,1},{18,34},{19,3},{32,48},... | collective-permute-start | bytes 1572872 | tf_op jit(solution)/shard_map/ppermute | solution.py:37
  35.3 17.9 %collective-permute-start.4 = (bf16[2,64,2048]{2,1,0:T(8,128)(2,1)S(1)}, bf16[2,64,2048]{2,1,0:T(8,128)(2,1)S(1)}, u32[]{:S(2)}, u32[]{:S(2)}) collective-permute-start(bf16[2,64,2048]{2,1,0:T(8,128)(2,1)S(1)} %collective-permute-done.2.refs_4_), channel_id=1, source_target_pairs={{0,1},{1,0},{2,3},{3,2},{4,5},{5,4},{6,7},{7,6},{8,9},{9,8},{10,11... | collective-permute-start | bytes 1572872 | tf_op jit(solution)/shard_map/ppermute | solution.py:20
  39.9 12.6 %collective-permute-start.1 = (bf16[64,2048]{1,0:T(8,128)(2,1)S(1)}, bf16[64,2048]{1,0:T(8,128)(2,1)S(1)}, u32[]{:S(2)}, u32[]{:S(2)}) collective-permute-start(bf16[64,2048]{1,0:T(8,128)(2,1)S(1)} %get-tuple-element.14), channel_id=1, source_target_pairs={{0,32},{2,34},{16,50},{18,48},{32,2},{34,0},{48,16},{50,18},{1,33}... | collective-permute-start | bytes 786440 | tf_op jit(solution)/shard_map/ppermute | solution.py:37
  44.7 7.8 %collective-permute-start.5 = (bf16[64,2048]{1,0:T(8,128)(2,1)S(1)}, bf16[64,2048]{1,0:T(8,128)(2,1)S(1)}, u32[]{:S(2)}, u32[]{:S(2)}) collective-permute-start(bf16[64,2048]{1,0:T(8,128)(2,1)S(1)} %collective-permute-done.3.refs_5_), channel_id=1, source_target_pairs={{0,1},{1,0},{2,3},{3,2},{4,5},{5,4},{6,7},{7,6},{8,9},{9,8},{10,11... | collective-permute-start | bytes 786440 | tf_op jit(solution)/shard_map/ppermute | solution.py:20
  46.9 0.7 copy-start.10
  52.5 14.7 %copy-start.5 = (bf16[64,2048]{1,0:T(8,128)(2,1)}, bf16[64,2048]{1,0:T(8,128)(2,1)S(1)}, u32[]{:S(2)}) copy-start(bf16[64,2048]{1,0:T(8,128)(2,1)S(1)} %collective-permute-done.1.refs_2_.refs_4_) | copy-start | bytes 786436
  52.5 12.7 %copy-start.2 = (bf16[2,64,2048]{2,1,0:T(8,128)(2,1)}, bf16[2,64,2048]{2,1,0:T(8,128)(2,1)S(1)}, u32[]{:S(2)}) copy-start(bf16[2,64,2048]{2,1,0:T(8,128)(2,1)S(1)} %collective-permute-done.refs_1_.refs_3_) | copy-start | bytes 1572868
  52.5 0.8 copy-start.12
  56.0 1.0 copy-start.11
  57.0 0.9 copy-start.13
  60.2 19.3 %all-to-all-start.3 = ((f32[4,128,256]{2,1,0:T(8,128)}), f32[4,128,256]{2,1,0:T(8,128)S(1)}, u32[]{:S(2)}, u32[]{:S(2)}) async-start(f32[4,128,256]{2,1,0:T(8,128)} %bitcast.4.refs_1_), calls=%async_computation.3 | async-start | bytes 1048576 | tf_op jit(solution)/shard_map/all_to_all | solution.py:293
  65.2 63.6 %all-gather.5.cloned.1.call-start = ((), (), s32[]{:S(2)}) async-start(), calls=%async_computation.6 | async-start | bytes 1179648 | tf_op jit(solution)/shard_map/all_gather | solution.py:301
  65.2 5.5 %collective-permute-start.6 = (bf16[2,64,2048]{2,1,0:T(8,128)(2,1)S(1)}, bf16[2,64,2048]{2,1,0:T(8,128)(2,1)S(1)}, u32[]{:S(2)}, u32[]{:S(2)}) collective-permute-start(bf16[2,64,2048]{2,1,0:T(8,128)(2,1)S(1)} %collective-permute-done.refs_1_.refs_3_), channel_id=1, source_target_pairs={{0,1},{1,0},{2,3},{3,2},{4,5},{5,4},{6,7},{7,6},{8,9},{9,8},{10,11... | collective-permute-start | bytes 1572872 | tf_op jit(solution)/shard_map/ppermute | solution.py:20
  67.1 3.6 %collective-permute-start.7 = (bf16[64,2048]{1,0:T(8,128)(2,1)S(1)}, bf16[64,2048]{1,0:T(8,128)(2,1)S(1)}, u32[]{:S(2)}, u32[]{:S(2)}) collective-permute-start(bf16[64,2048]{1,0:T(8,128)(2,1)S(1)} %collective-permute-done.1.refs_2_.refs_4_), channel_id=1, source_target_pairs={{0,1},{1,0},{2,3},{3,2},{4,5},{5,4},{6,7},{7,6},{8,9},{9,8},{10,11... | collective-permute-start | bytes 786440 | tf_op jit(solution)/shard_map/ppermute | solution.py:20
  70.7 0.7 copy-start.19
  70.7 0.9 copy-start.17
  79.5 1.2 copy-start
  80.7 1.1 copy-start.18
  80.7 16.7 %copy-start.1 = (f32[2,2,2,2,64,192]{5,4,3,2,1,0:T(8,128)S(1)}, f32[2,2,2,2,64,192]{5,4,3,2,1,0:T(8,128)}, u32[]{:S(2)}) copy-start(f32[2,2,2,2,64,192]{5,4,3,2,1,0:T(8,128)} %get-tuple-element.19) | copy-start | bytes 2359300
  80.7 16.7 %copy-start.16 = (s32[3]{0:T(128)S(1)}, s32[3]{0:T(128)}, u32[]{:S(2)}) copy-start(s32[3]{0:T(128)} %copy-done.15) | copy-start | bytes 40
  98.1 18.9 %collective-permute-start.8 = (bf16[128,384]{1,0:T(8,128)(2,1)S(1)}, bf16[128,384]{1,0:T(8,128)(2,1)S(1)}, u32[]{:S(2)}, u32[]{:S(2)}) collective-permute-start(bf16[128,384]{1,0:T(8,128)(2,1)S(1)} %shard_map.51), channel_id=1, source_target_pairs={{0,0},{2,64},{4,128},{6,192},{8,256},{10,320},{12,384},{14,448},{6... | collective-permute-start | bytes 294920 | tf_op jit(solution)/shard_map/ppermute | solution.py:62
  102.0 20.8 %collective-permute-start.9 = (bf16[128,384]{1,0:T(8,128)(2,1)S(1)}, bf16[128,384]{1,0:T(8,128)(2,1)S(1)}, u32[]{:S(2)}, u32[]{:S(2)}) collective-permute-start(bf16[128,384]{1,0:T(8,128)(2,1)S(1)} %shard_map.51), channel_id=1, source_target_pairs={{0,2},{2,66},{4,130},{6,194},{8,258},{10,322},{12,386},{14,450},{6... | collective-permute-start | bytes 294920 | tf_op jit(solution)/shard_map/ppermute | solution.py:62
  124.3 15.0 %all-to-all-start.2 = ((bf16[4,2,128,384]{3,2,1,0:T(8,128)(2,1)}), bf16[4,2,128,384]{3,2,1,0:T(8,128)(2,1)S(1)}, u32[]{:S(2)}, u32[]{:S(2)}) async-start(bf16[4,2,128,384]{3,2,1,0:T(8,128)(2,1)} %shard_map.52.late_ref), calls=%async_computation.2 | async-start | bytes 1572864 | tf_op jit(solution)/shard_map/all_to_all | solution.py:306
  128.8 1.2 copy-start.6
  130.1 9.2 %collective-permute-start.10 = (bf16[1024,256]{1,0:T(8,128)(2,1)S(1)}, bf16[1024,256]{1,0:T(8,128)(2,1)S(1)}, u32[]{:S(2)}, u32[]{:S(2)}) collective-permute-start(bf16[1024,256]{1,0:T(8,128)(2,1)S(1)} %shard_map.54.mine_ref), channel_id=1, source_target_pairs={{0,1},{1,0},{2,3},{3,2},{4,5},{5,4},{6,7},{7,6},{8,9},{9,8},{10,11... | collective-permute-start | bytes 1572872 | tf_op jit(solution)/shard_map/ppermute | solution.py:20
Sparse Core Ops, SparseCore 0:
  9.4 56.5 all-gather.2
  81.6 46.8 all-gather.4

commit v7 on v6

--- a/solution.py
+++ b/solution.py
@@ -14,6 +14,10 @@
 WHOLE = pl.BlockSpec(memory_space=pltpu.VMEM)
 IN_HBM = pl.BlockSpec(memory_space=pltpu.HBM)
 ANY = pl.BlockSpec(memory_space=pl.ANY)
+
+
+def cost(flops, moved):
+    return pl.CostEstimate(flops=flops, bytes_accessed=moved, transcendentals=0)
 
 
 def swap_cores(v):
@@ -74,6 +78,7 @@
         out_shape=jax.ShapeDtypeStruct((NZ,) + v.shape, v.dtype),
         in_specs=[ANY, WHOLE],
         out_specs=WHOLE,
+        cost_estimate=cost(0, 2 * (NZ + 1) * v.size),
         compiler_params=pltpu.CompilerParams(vmem_limit_bytes=VMEM_LIMIT),
     )(late, v)
     return lax.all_to_all(copies, Z, 0, 0)
@@ -105,6 +110,7 @@
         out_shape=(both, both, jax.ShapeDtypeStruct((tokens, features // NY), values.dtype)),
         in_specs=[SCALARS, pl.BlockSpec((seqs, tokens, part * NY), lambda i: (0, 0, i))],
         out_specs=(both_spec, both_spec, pl.BlockSpec((tokens, part), lambda i: (0, i))),
+        cost_estimate=cost(0, 4 * values.size),
         compiler_params=pltpu.CompilerParams(vmem_limit_bytes=VMEM_LIMIT),
     )(at, values)
 
@@ -172,6 +178,10 @@
             pltpu.VMEM((features, cols), basis.dtype),
             pltpu.SemaphoreType.DMA((6,)),
         ],
+        cost_estimate=cost(
+            16 * tokens * features * cols,
+            2 * (8 * tokens + cols) * features + 32 * tokens * cols,
+        ),
         compiler_params=pltpu.CompilerParams(
             vmem_limit_bytes=TURN_LIMIT if parts > 1 else VMEM_LIMIT
         ),
@@ -190,6 +200,7 @@
         out_shape=jax.ShapeDtypeStruct(v.shape, jnp.bfloat16),
         in_specs=[ANY, WHOLE],
         out_specs=WHOLE,
+        cost_estimate=cost(0, 6 * v.size),
         compiler_params=pltpu.CompilerParams(vmem_limit_bytes=VMEM_LIMIT),
     )(late, v)
 
@@ -214,6 +225,7 @@
         out_shape=jax.ShapeDtypeStruct((rows, NC * cols), jnp.bfloat16),
         in_specs=[SCALARS, WHOLE, WHOLE],
         out_specs=WHOLE,
+        cost_estimate=cost(full.size, 4 * full.size + 2 * got.size),
         compiler_params=pltpu.CompilerParams(vmem_limit_bytes=VMEM_LIMIT),
     )(at, full, got)
 
@@ -230,6 +242,7 @@
         out_shape=jax.ShapeDtypeStruct(got.shape[1:], got.dtype),
         in_specs=[ANY, WHOLE],
         out_specs=WHOLE,
+        cost_estimate=cost(got.size, 5 * got.size),
         compiler_params=pltpu.CompilerParams(vmem_limit_bytes=VMEM_LIMIT),
     )(late, got)
 
@@ -249,6 +262,7 @@
         out_shape=jax.ShapeDtypeStruct((NX, 2) + near.shape, near.dtype),
         in_specs=[SCALARS, WHOLE, WHOLE],
         out_specs=WHOLE,
+        cost_estimate=cost(0, 20 * near.size),
         compiler_params=pltpu.CompilerParams(vmem_limit_bytes=VMEM_LIMIT),
     )(at, near, far)
 
@@ -274,6 +288,9 @@
         out_shape=jax.ShapeDtypeStruct((NY, NC, quarter, cols), jnp.bfloat16),
         in_specs=[SCALARS] + [WHOLE] * 3,
         out_specs=WHOLE,
+        cost_estimate=cost(
+            4 * acts.size * mine.shape[1], 2 * (acts.size + 2 * mine.size) + 2 * NY * NC * quarter * cols
+        ),
         compiler_params=pltpu.CompilerParams(vmem_limit_bytes=VMEM_LIMIT),
     )(at, acts, mine, other)
     return out.reshape(NY * NC, quarter, cols)

time: 166 us -> 166 us (level)
  no operation moved by 1% of the time
where the time goes in v7:
time: 166 us; the launch traced here: 163 us
  starting transfers between devices  62.7 us (38%)
  waiting for transfers between devices  30.8 us (19%)
  blocking collectives  30 us (18%)
  Pallas kernels  14.9 us (9%)
  between operations  13.7 us (8%)
  local copies, waits for them, and re-layouts  10.1 us (6%)
    ppermute x4, starting transfers between devices, permute(): return lax.ppermute(v, axes, pairs)  15.6 us
    all_to_all x1, blocking collectives, local(): act_got = lax.all_to_all(act_send, (Y, C), 0, 0)  15.1 us
    all_to_all x1, blocking collectives, local(): got = lax.all_to_all(outer, (Y, C), 0, 0).astype(jnp.float32)  14.9 us
    ppermute x2, starting transfers between devices, transpose_planes(): return lax.ppermute(v, (Z, X, H), pairs)  14.4 us
    ppermute x5, starting transfers between devices, swap_cores(): return lax.ppermute(v, C, [(0, 1), (1, 0)])  12.9 us
    ppermute x2, waiting for transfers between devices, transpose_planes(): return lax.ppermute(v, (Z, X, H), pairs)  10.3 us
    all_to_all x1, starting transfers between devices, spread_z(): return lax.all_to_all(copies, Z, 0, 0)  10.3 us
    unnamed x40, local copies, waits for them, and re-layouts  9.62 us
  transfers between devices with their start and end apart: 16, of which 8 were waited for; matrix products, arithmetic and copies ran while one was open for 0% of the time, Pallas kernels for 8%

profile of v7, /device:TPU:6, one launch (start us, length us, event | category | flops | bytes accessed | tf_op | source)
XLA Modules:
  0.0 163.0 jit_solution(9809027203425403139)
XLA Ops:
  6.5 0.0 all-gather.3.cloned.1.call-start
  6.5 0.7 all-gather.3.cloned.1.call-update
  7.3 0.1 pad_add_fusion.at_ref.late_ref.refs_0_
  7.3 0.9 copy-done.14
  8.2 1.0 shard_map.48
  9.3 10.3 %all-to-all-start = ((bf16[8,256,256]{2,1,0:T(8,128)(2,1)}), bf16[8,256,256]{2,1,0:T(8,128)(2,1)S(1)}, u32[]{:S(2)}, u32[]{:S(2)}) async-start(bf16[8,256,256]{2,1,0:T(8,128)(2,1)} %shard_map.48), calls=%async_computation | async-start | bytes 2097152 | tf_op jit(solution)/shard_map/all_to_all | solution.py:84
  19.6 0.0 copy-done.3
  19.6 0.0 copy-start.4
  19.6 1.1 shard_map.47
  20.7 0.8 copy-done.8
  21.5 3.6 %collective-permute-start.2 = (bf16[2,64,2048]{2,1,0:T(8,128)(2,1)S(1)}, bf16[2,64,2048]{2,1,0:T(8,128)(2,1)S(1)}, u32[]{:S(2)}, u32[]{:S(2)}) collective-permute-start(bf16[2,64,2048]{2,1,0:T(8,128)(2,1)S(1)} %get-tuple-element.16), channel_id=1, source_target_pairs={{0,16},{1,51},{2,18},{3,49},{16,32},{17,1},{18,34},{19,3},{32,48},... | collective-permute-start | bytes 1572872 | tf_op jit(solution)/shard_map/ppermute | solution.py:41
  25.1 4.5 %collective-permute-start.3 = (bf16[64,2048]{1,0:T(8,128)(2,1)S(1)}, bf16[64,2048]{1,0:T(8,128)(2,1)S(1)}, u32[]{:S(2)}, u32[]{:S(2)}) collective-permute-start(bf16[64,2048]{1,0:T(8,128)(2,1)S(1)} %get-tuple-element.17), channel_id=1, source_target_pairs={{0,32},{2,34},{16,50},{18,48},{32,2},{34,0},{48,16},{50,18},{1,33}... | collective-permute-start | bytes 786440 | tf_op jit(solution)/shard_map/ppermute | solution.py:41
  29.6 1.1 shard_map.46
  30.7 0.8 copy-done.7
  31.5 2.7 %collective-permute-start = (bf16[2,64,2048]{2,1,0:T(8,128)(2,1)S(1)}, bf16[2,64,2048]{2,1,0:T(8,128)(2,1)S(1)}, u32[]{:S(2)}, u32[]{:S(2)}) collective-permute-start(bf16[2,64,2048]{2,1,0:T(8,128)(2,1)S(1)} %get-tuple-element.13), channel_id=1, source_target_pairs={{0,16},{1,51},{2,18},{3,49},{16,32},{17,1},{18,34},{19,3},{32,48},... | collective-permute-start | bytes 1572872 | tf_op jit(solution)/shard_map/ppermute | solution.py:41
  34.2 1.1 collective-permute-done.2.refs_4_
  35.3 4.6 %collective-permute-start.4 = (bf16[2,64,2048]{2,1,0:T(8,128)(2,1)S(1)}, bf16[2,64,2048]{2,1,0:T(8,128)(2,1)S(1)}, u32[]{:S(2)}, u32[]{:S(2)}) collective-permute-start(bf16[2,64,2048]{2,1,0:T(8,128)(2,1)S(1)} %collective-permute-done.2.refs_4_), channel_id=1, source_target_pairs={{0,1},{1,0},{2,3},{3,2},{4,5},{5,4},{6,7},{7,6},{8,9},{9,8},{10,11... | collective-permute-start | bytes 1572872 | tf_op jit(solution)/shard_map/ppermute | solution.py:24
  39.9 4.8 %collective-permute-start.1 = (bf16[64,2048]{1,0:T(8,128)(2,1)S(1)}, bf16[64,2048]{1,0:T(8,128)(2,1)S(1)}, u32[]{:S(2)}, u32[]{:S(2)}) collective-permute-start(bf16[64,2048]{1,0:T(8,128)(2,1)S(1)} %get-tuple-element.14), channel_id=1, source_target_pairs={{0,32},{2,34},{16,50},{18,48},{32,2},{34,0},{48,16},{50,18},{1,33}... | collective-permute-start | bytes 786440 | tf_op jit(solution)/shard_map/ppermute | solution.py:41
  44.7 0.0 collective-permute-done.3.refs_5_
  44.7 2.1 %collective-permute-start.5 = (bf16[64,2048]{1,0:T(8,128)(2,1)S(1)}, bf16[64,2048]{1,0:T(8,128)(2,1)S(1)}, u32[]{:S(2)}, u32[]{:S(2)}) collective-permute-start(bf16[64,2048]{1,0:T(8,128)(2,1)S(1)} %collective-permute-done.3.refs_5_), channel_id=1, source_target_pairs={{0,1},{1,0},{2,3},{3,2},{4,5},{5,4},{6,7},{7,6},{8,9},{9,8},{10,11... | collective-permute-start | bytes 786440 | tf_op jit(solution)/shard_map/ppermute | solution.py:24
  46.9 0.0 copy-start.10
  46.9 0.7 copy-done.10
  47.6 4.9 %collective-permute-done.1.refs_2_.refs_4_ = bf16[64,2048]{1,0:T(8,128)(2,1)S(1)} collective-permute-done((bf16[64,2048]{1,0:T(8,128)(2,1)S(1)}, bf16[64,2048]{1,0:T(8,128)(2,1)S(1)}, u32[]{:S(2)}, u32[]{:S(2)}) %collective-permute-start.1) | collective-permute-done | bytes 262176 | tf_op jit(solution)/shard_map/ppermute | solution.py:41
  52.5 0.0 collective-permute-done.refs_1_.refs_3_
  52.5 0.0 collective-permute-done.5.refs_7_
  52.5 0.7 copy-done.12
  53.3 0.0 collective-permute-done.4.refs_6_
  53.3 2.7 %all-to-all-done = bf16[8,256,256]{2,1,0:T(8,128)(2,1)S(1)} async-done(((bf16[8,256,256]{2,1,0:T(8,128)(2,1)}), bf16[8,256,256]{2,1,0:T(8,128)(2,1)S(1)}, u32[]{:S(2)}, u32[]{:S(2)}) %all-to-all-start) | async-done | bytes 1048608 | tf_op jit(solution)/shard_map/all_to_all | solution.py:84
  56.0 0.9 copy-done.11
  57.0 0.9 copy-done.13
  57.9 2.3 %shard_map.49 = f32[2,2,1,2,64,256]{5,4,3,2,1,0:T(8,128)} custom-call(s32[3]{0:T(128)S(1)} %pad_add_fusion.at_ref.late_ref.refs_0_, bf16[2,64,2048]{2,1,0:T(8,128)(2,1)S(1)} %collective-permute-done.refs_1_.refs_3_, bf16[64,2048]{1,0:T(8,128)(2,1)S(1)} %collective-permute-done.1.refs_2_.refs_4_, bf16[2,64,2048]{2,1,0:T(8,128)(2,1)S(1)} %copy-done.9, ...), custom_call_target="tpu_custom_call" | custom-call | flops 536870912 | bytes 3670016 | tf_op jit(solution)/shard_map/pallas_call | solution.py:171
  60.2 5.0 %all-to-all-start.3 = ((f32[4,128,256]{2,1,0:T(8,128)}), f32[4,128,256]{2,1,0:T(8,128)S(1)}, u32[]{:S(2)}, u32[]{:S(2)}) async-start(f32[4,128,256]{2,1,0:T(8,128)} %bitcast.4.refs_1_), calls=%async_computation.3 | async-start | bytes 1048576 | tf_op jit(solution)/shard_map/all_to_all | solution.py:310
  65.2 1.9 %collective-permute-start.6 = (bf16[2,64,2048]{2,1,0:T(8,128)(2,1)S(1)}, bf16[2,64,2048]{2,1,0:T(8,128)(2,1)S(1)}, u32[]{:S(2)}, u32[]{:S(2)}) collective-permute-start(bf16[2,64,2048]{2,1,0:T(8,128)(2,1)S(1)} %collective-permute-done.refs_1_.refs_3_), channel_id=1, source_target_pairs={{0,1},{1,0},{2,3},{3,2},{4,5},{5,4},{6,7},{7,6},{8,9},{9,8},{10,11... | collective-permute-start | bytes 1572872 | tf_op jit(solution)/shard_map/ppermute | solution.py:24
  67.1 2.4 %collective-permute-start.7 = (bf16[64,2048]{1,0:T(8,128)(2,1)S(1)}, bf16[64,2048]{1,0:T(8,128)(2,1)S(1)}, u32[]{:S(2)}, u32[]{:S(2)}) collective-permute-start(bf16[64,2048]{1,0:T(8,128)(2,1)S(1)} %collective-permute-done.1.refs_2_.refs_4_), channel_id=1, source_target_pairs={{0,1},{1,0},{2,3},{3,2},{4,5},{5,4},{6,7},{7,6},{8,9},{9,8},{10,11... | collective-permute-start | bytes 786440 | tf_op jit(solution)/shard_map/ppermute | solution.py:24
  69.6 1.1 collective-permute-done.7.refs_6_
  70.7 0.0 collective-permute-done.6.refs_5_
  70.7 0.0 all-gather.3.cloned.1.call-done.refs_7_
  70.7 0.7 copy-done.19
  71.4 0.2 copy-done.17
  71.6 5.4 %shard_map.50 = (f32[2,2,2,2,64,192]{5,4,3,2,1,0:T(8,128)}, bf16[2,2,2,2,64,192]{5,4,3,2,1,0:T(8,128)(2,1)}) custom-call(s32[3]{0:T(128)} %copy-done.15, f32[4,128,256]{2,1,0:T(8,128)} %bitcast.4.refs_1_, bf16[2,64,2048]{2,1,0:T(8,128)(2,1)} %copy-done.7, bf16[2,64,2048]{2,1,0:T(8,128)(2,1)} %copy-done.2, bf16[64,2048]{1,0:T(8,128)(2,1)} %copy-done.5, ...), custom_call_target="tpu_custom_call" | custom-call | flops 805306368 | bytes 4456448 | tf_op jit(solution)/shard_map/pallas_call | solution.py:171
  77.0 2.5 %all-to-all-done.3.got_ref = f32[4,128,256]{2,1,0:T(8,128)S(1)} async-done(((f32[4,128,256]{2,1,0:T(8,128)}), f32[4,128,256]{2,1,0:T(8,128)S(1)}, u32[]{:S(2)}, u32[]{:S(2)}) %all-to-all-start.3) | async-done | bytes 524320 | tf_op jit(solution)/shard_map/all_to_all | solution.py:310
  79.5 1.2 copy-done
  80.7 0.7 shard_map.53
  81.4 0.0 all-gather.5.cloned.1.call-update
  81.4 0.4 copy-done.18
  81.8 0.3 copy.5
  82.1 15.1 %all_to_all.25 = bf16[8,128,192]{1,2,0:T(8,128)(2,1)S(1)} all-to-all(bf16[8,128,192]{1,2,0:T(8,128)(2,1)S(1)} %copy.5), channel_id=1, replica_groups=mesh['z'=8,'y'=4,'x'=4,'h'=2,'c'=2] {'y','c'}, dimensions={0} | all-to-all | bytes 786432 | tf_op jit(solution)/shard_map/all_to_all | solution.py:315
  97.2 0.2 copy.6.got_ref
  97.4 0.7 shard_map.51
  98.1 4.0 %collective-permute-start.8 = (bf16[128,384]{1,0:T(8,128)(2,1)S(1)}, bf16[128,384]{1,0:T(8,128)(2,1)S(1)}, u32[]{:S(2)}, u32[]{:S(2)}) collective-permute-start(bf16[128,384]{1,0:T(8,128)(2,1)S(1)} %shard_map.51), channel_id=1, source_target_pairs={{0,0},{2,64},{4,128},{6,192},{8,256},{10,320},{12,384},{14,448},{6... | collective-permute-start | bytes 294920 | tf_op jit(solution)/shard_map/ppermute | solution.py:66
  102.0 10.4 %collective-permute-start.9 = (bf16[128,384]{1,0:T(8,128)(2,1)S(1)}, bf16[128,384]{1,0:T(8,128)(2,1)S(1)}, u32[]{:S(2)}, u32[]{:S(2)}) collective-permute-start(bf16[128,384]{1,0:T(8,128)(2,1)S(1)} %shard_map.51), channel_id=1, source_target_pairs={{0,2},{2,66},{4,130},{6,194},{8,258},{10,322},{12,386},{14,450},{6... | collective-permute-start | bytes 294920 | tf_op jit(solution)/shard_map/ppermute | solution.py:66
  112.5 4.5 %collective-permute-done.8.near_ref = bf16[128,384]{1,0:T(8,128)(2,1)S(1)} collective-permute-done((bf16[128,384]{1,0:T(8,128)(2,1)S(1)}, bf16[128,384]{1,0:T(8,128)(2,1)S(1)}, u32[]{:S(2)}, u32[]{:S(2)}) %collective-permute-start.8) | collective-permute-done | bytes 98336 | tf_op jit(solution)/shard_map/ppermute | solution.py:66
  117.0 5.8 %collective-permute-done.9.far_ref = bf16[128,384]{1,0:T(8,128)(2,1)S(1)} collective-permute-done((bf16[128,384]{1,0:T(8,128)(2,1)S(1)}, bf16[128,384]{1,0:T(8,128)(2,1)S(1)}, u32[]{:S(2)}, u32[]{:S(2)}) %collective-permute-start.9) | collective-permute-done | bytes 98336 | tf_op jit(solution)/shard_map/ppermute | solution.py:66
  122.8 1.5 shard_map.52.late_ref
  124.3 4.5 %all-to-all-start.2 = ((bf16[4,2,128,384]{3,2,1,0:T(8,128)(2,1)}), bf16[4,2,128,384]{3,2,1,0:T(8,128)(2,1)S(1)}, u32[]{:S(2)}, u32[]{:S(2)}) async-start(bf16[4,2,128,384]{3,2,1,0:T(8,128)(2,1)} %shard_map.52.late_ref), calls=%async_computation.2 | async-start | bytes 1572864 | tf_op jit(solution)/shard_map/all_to_all | solution.py:323
  128.8 1.2 copy-done.6
  130.0 0.1 shard_map.54.mine_ref
  130.1 1.9 %collective-permute-start.10 = (bf16[1024,256]{1,0:T(8,128)(2,1)S(1)}, bf16[1024,256]{1,0:T(8,128)(2,1)S(1)}, u32[]{:S(2)}, u32[]{:S(2)}) collective-permute-start(bf16[1024,256]{1,0:T(8,128)(2,1)S(1)} %shard_map.54.mine_ref), channel_id=1, source_target_pairs={{0,1},{1,0},{2,3},{3,2},{4,5},{5,4},{6,7},{7,6},{8,9},{9,8},{10,11... | collective-permute-start | bytes 1572872 | tf_op jit(solution)/shard_map/ppermute | solution.py:24
  132.0 7.3 %all-to-all-done.2 = bf16[4,2,128,384]{3,2,1,0:T(8,128)(2,1)S(1)} async-done(((bf16[4,2,128,384]{3,2,1,0:T(8,128)(2,1)}), bf16[4,2,128,384]{3,2,1,0:T(8,128)(2,1)S(1)}, u32[]{:S(2)}, u32[]{:S(2)}) %all-to-all-start.2) | async-done | bytes 786464 | tf_op jit(solution)/shard_map/all_to_all | solution.py:323
  139.3 0.0 collective-permute-done.10.other_ref
  139.3 1.1 shard_map.55
  140.5 14.9 %all_to_all.26 = bf16[8,96,256]{2,1,0:T(8,128)(2,1)S(1)} all-to-all(bf16[8,96,256]{2,1,0:T(8,128)(2,1)S(1)} %bitcast.16), channel_id=1, replica_groups=mesh['z'=8,'y'=4,'x'=4,'h'=2,'c'=2] {'y','c'}, dimensions={0} | all-to-all | bytes 786432 | tf_op jit(solution)/shard_map/all_to_all | solution.py:327
  155.4 0.1 convert_element_type.3
  155.5 0.7 fusion.2
  (27 shorter events, 0.0 us)
Async XLA Ops:
  6.5 13.1 %copy-start.3 = (bf16[2,64,8192]{2,1,0:T(8,128)(2,1)S(1)}, bf16[2,64,8192]{2,1,0:T(8,128)(2,1)}, u32[]{:S(2)}) copy-start(bf16[2,64,8192]{2,1,0:T(8,128)(2,1)} %values_ref.3) | copy-start | bytes 6291460
  6.5 64.2 %all-gather.3.cloned.1.call-start = ((), (), s32[]{:S(2)}) async-start(), calls=%async_computation.5 | async-start | bytes 1769472 | tf_op jit(solution)/shard_map/all_gather | solution.py:302
  7.3 0.9 copy-start.14
  8.2 47.8 %copy-start.15 = (s32[3]{0:T(128)}, s32[3]{0:T(128)S(1)}, u32[]{:S(2)}) copy-start(s32[3]{0:T(128)S(1)} %pad_add_fusion.at_ref.late_ref.refs_0_) | copy-start | bytes 40
  9.3 46.7 %all-to-all-start = ((bf16[8,256,256]{2,1,0:T(8,128)(2,1)}), bf16[8,256,256]{2,1,0:T(8,128)(2,1)S(1)}, u32[]{:S(2)}, u32[]{:S(2)}) async-start(bf16[8,256,256]{2,1,0:T(8,128)(2,1)} %shard_map.48), calls=%async_computation | async-start | bytes 2097152 | tf_op jit(solution)/shard_map/all_to_all | solution.py:84
  19.6 10.0 %copy-start.4 = (bf16[2,64,8192]{2,1,0:T(8,128)(2,1)S(1)}, bf16[2,64,8192]{2,1,0:T(8,128)(2,1)}, u32[]{:S(2)}) copy-start(bf16[2,64,8192]{2,1,0:T(8,128)(2,1)} %values_ref.2) | copy-start | bytes 6291460
  20.7 0.8 copy-start.8
  21.5 34.5 %copy-start.9 = (bf16[2,64,2048]{2,1,0:T(8,128)(2,1)S(1)}, bf16[2,64,2048]{2,1,0:T(8,128)(2,1)}, u32[]{:S(2)}) copy-start(bf16[2,64,2048]{2,1,0:T(8,128)(2,1)} %copy-done.8) | copy-start | bytes 1572868
  21.5 13.9 %collective-permute-start.2 = (bf16[2,64,2048]{2,1,0:T(8,128)(2,1)S(1)}, bf16[2,64,2048]{2,1,0:T(8,128)(2,1)S(1)}, u32[]{:S(2)}, u32[]{:S(2)}) collective-permute-start(bf16[2,64,2048]{2,1,0:T(8,128)(2,1)S(1)} %get-tuple-element.16), channel_id=1, source_target_pairs={{0,16},{1,51},{2,18},{3,49},{16,32},{17,1},{18,34},{19,3},{32,48},... | collective-permute-start | bytes 1572872 | tf_op jit(solution)/shard_map/ppermute | solution.py:41
  25.1 19.6 %collective-permute-start.3 = (bf16[64,2048]{1,0:T(8,128)(2,1)S(1)}, bf16[64,2048]{1,0:T(8,128)(2,1)S(1)}, u32[]{:S(2)}, u32[]{:S(2)}) collective-permute-start(bf16[64,2048]{1,0:T(8,128)(2,1)S(1)} %get-tuple-element.17), channel_id=1, source_target_pairs={{0,32},{2,34},{16,50},{18,48},{32,2},{34,0},{48,16},{50,18},{1,33}... | collective-permute-start | bytes 786440 | tf_op jit(solution)/shard_map/ppermute | solution.py:41
  30.7 0.8 copy-start.7
  31.5 21.0 %collective-permute-start = (bf16[2,64,2048]{2,1,0:T(8,128)(2,1)S(1)}, bf16[2,64,2048]{2,1,0:T(8,128)(2,1)S(1)}, u32[]{:S(2)}, u32[]{:S(2)}) collective-permute-start(bf16[2,64,2048]{2,1,0:T(8,128)(2,1)S(1)} %get-tuple-element.13), channel_id=1, source_target_pairs={{0,16},{1,51},{2,18},{3,49},{16,32},{17,1},{18,34},{19,3},{32,48},... | collective-permute-start | bytes 1572872 | tf_op jit(solution)/shard_map/ppermute | solution.py:41
  35.3 17.9 %collective-permute-start.4 = (bf16[2,64,2048]{2,1,0:T(8,128)(2,1)S(1)}, bf16[2,64,2048]{2,1,0:T(8,128)(2,1)S(1)}, u32[]{:S(2)}, u32[]{:S(2)}) collective-permute-start(bf16[2,64,2048]{2,1,0:T(8,128)(2,1)S(1)} %collective-permute-done.2.refs_4_), channel_id=1, source_target_pairs={{0,1},{1,0},{2,3},{3,2},{4,5},{5,4},{6,7},{7,6},{8,9},{9,8},{10,11... | collective-permute-start | bytes 1572872 | tf_op jit(solution)/shard_map/ppermute | solution.py:24
  39.9 12.6 %collective-permute-start.1 = (bf16[64,2048]{1,0:T(8,128)(2,1)S(1)}, bf16[64,2048]{1,0:T(8,128)(2,1)S(1)}, u32[]{:S(2)}, u32[]{:S(2)}) collective-permute-start(bf16[64,2048]{1,0:T(8,128)(2,1)S(1)} %get-tuple-element.14), channel_id=1, source_target_pairs={{0,32},{2,34},{16,50},{18,48},{32,2},{34,0},{48,16},{50,18},{1,33}... | collective-permute-start | bytes 786440 | tf_op jit(solution)/shard_map/ppermute | solution.py:41
  44.7 7.8 %collective-permute-start.5 = (bf16[64,2048]{1,0:T(8,128)(2,1)S(1)}, bf16[64,2048]{1,0:T(8,128)(2,1)S(1)}, u32[]{:S(2)}, u32[]{:S(2)}) collective-permute-start(bf16[64,2048]{1,0:T(8,128)(2,1)S(1)} %collective-permute-done.3.refs_5_), channel_id=1, source_target_pairs={{0,1},{1,0},{2,3},{3,2},{4,5},{5,4},{6,7},{7,6},{8,9},{9,8},{10,11... | collective-permute-start | bytes 786440 | tf_op jit(solution)/shard_map/ppermute | solution.py:24
  46.9 0.7 copy-start.10
  52.5 14.7 %copy-start.5 = (bf16[64,2048]{1,0:T(8,128)(2,1)}, bf16[64,2048]{1,0:T(8,128)(2,1)S(1)}, u32[]{:S(2)}) copy-start(bf16[64,2048]{1,0:T(8,128)(2,1)S(1)} %collective-permute-done.1.refs_2_.refs_4_) | copy-start | bytes 786436
  52.5 12.7 %copy-start.2 = (bf16[2,64,2048]{2,1,0:T(8,128)(2,1)}, bf16[2,64,2048]{2,1,0:T(8,128)(2,1)S(1)}, u32[]{:S(2)}) copy-start(bf16[2,64,2048]{2,1,0:T(8,128)(2,1)S(1)} %collective-permute-done.refs_1_.refs_3_) | copy-start | bytes 1572868
  52.5 0.8 copy-start.12
  56.0 1.0 copy-start.11
  57.0 0.9 copy-start.13
  60.2 19.3 %all-to-all-start.3 = ((f32[4,128,256]{2,1,0:T(8,128)}), f32[4,128,256]{2,1,0:T(8,128)S(1)}, u32[]{:S(2)}, u32[]{:S(2)}) async-start(f32[4,128,256]{2,1,0:T(8,128)} %bitcast.4.refs_1_), calls=%async_computation.3 | async-start | bytes 1048576 | tf_op jit(solution)/shard_map/all_to_all | solution.py:310
  65.2 63.6 %all-gather.5.cloned.1.call-start = ((), (), s32[]{:S(2)}) async-start(), calls=%async_computation.6 | async-start | bytes 1179648 | tf_op jit(solution)/shard_map/all_gather | solution.py:318
  65.2 5.5 %collective-permute-start.6 = (bf16[2,64,2048]{2,1,0:T(8,128)(2,1)S(1)}, bf16[2,64,2048]{2,1,0:T(8,128)(2,1)S(1)}, u32[]{:S(2)}, u32[]{:S(2)}) collective-permute-start(bf16[2,64,2048]{2,1,0:T(8,128)(2,1)S(1)} %collective-permute-done.refs_1_.refs_3_), channel_id=1, source_target_pairs={{0,1},{1,0},{2,3},{3,2},{4,5},{5,4},{6,7},{7,6},{8,9},{9,8},{10,11... | collective-permute-start | bytes 1572872 | tf_op jit(solution)/shard_map/ppermute | solution.py:24
  67.1 3.6 %collective-permute-start.7 = (bf16[64,2048]{1,0:T(8,128)(2,1)S(1)}, bf16[64,2048]{1,0:T(8,128)(2,1)S(1)}, u32[]{:S(2)}, u32[]{:S(2)}) collective-permute-start(bf16[64,2048]{1,0:T(8,128)(2,1)S(1)} %collective-permute-done.1.refs_2_.refs_4_), channel_id=1, source_target_pairs={{0,1},{1,0},{2,3},{3,2},{4,5},{5,4},{6,7},{7,6},{8,9},{9,8},{10,11... | collective-permute-start | bytes 786440 | tf_op jit(solution)/shard_map/ppermute | solution.py:24
  70.7 0.7 copy-start.19
  70.7 0.9 copy-start.17
  79.5 1.2 copy-start
  80.7 1.1 copy-start.18
  80.7 16.7 %copy-start.1 = (f32[2,2,2,2,64,192]{5,4,3,2,1,0:T(8,128)S(1)}, f32[2,2,2,2,64,192]{5,4,3,2,1,0:T(8,128)}, u32[]{:S(2)}) copy-start(f32[2,2,2,2,64,192]{5,4,3,2,1,0:T(8,128)} %get-tuple-element.19) | copy-start | bytes 2359300
  80.7 16.7 %copy-start.16 = (s32[3]{0:T(128)S(1)}, s32[3]{0:T(128)}, u32[]{:S(2)}) copy-start(s32[3]{0:T(128)} %copy-done.15) | copy-start | bytes 40
  98.1 18.9 %collective-permute-start.8 = (bf16[128,384]{1,0:T(8,128)(2,1)S(1)}, bf16[128,384]{1,0:T(8,128)(2,1)S(1)}, u32[]{:S(2)}, u32[]{:S(2)}) collective-permute-start(bf16[128,384]{1,0:T(8,128)(2,1)S(1)} %shard_map.51), channel_id=1, source_target_pairs={{0,0},{2,64},{4,128},{6,192},{8,256},{10,320},{12,384},{14,448},{6... | collective-permute-start | bytes 294920 | tf_op jit(solution)/shard_map/ppermute | solution.py:66
  102.0 20.8 %collective-permute-start.9 = (bf16[128,384]{1,0:T(8,128)(2,1)S(1)}, bf16[128,384]{1,0:T(8,128)(2,1)S(1)}, u32[]{:S(2)}, u32[]{:S(2)}) collective-permute-start(bf16[128,384]{1,0:T(8,128)(2,1)S(1)} %shard_map.51), channel_id=1, source_target_pairs={{0,2},{2,66},{4,130},{6,194},{8,258},{10,322},{12,386},{14,450},{6... | collective-permute-start | bytes 294920 | tf_op jit(solution)/shard_map/ppermute | solution.py:66
  124.3 15.0 %all-to-all-start.2 = ((bf16[4,2,128,384]{3,2,1,0:T(8,128)(2,1)}), bf16[4,2,128,384]{3,2,1,0:T(8,128)(2,1)S(1)}, u32[]{:S(2)}, u32[]{:S(2)}) async-start(bf16[4,2,128,384]{3,2,1,0:T(8,128)(2,1)} %shard_map.52.late_ref), calls=%async_computation.2 | async-start | bytes 1572864 | tf_op jit(solution)/shard_map/all_to_all | solution.py:323
  128.8 1.2 copy-start.6
  130.1 9.2 %collective-permute-start.10 = (bf16[1024,256]{1,0:T(8,128)(2,1)S(1)}, bf16[1024,256]{1,0:T(8,128)(2,1)S(1)}, u32[]{:S(2)}, u32[]{:S(2)}) collective-permute-start(bf16[1024,256]{1,0:T(8,128)(2,1)S(1)} %shard_map.54.mine_ref), channel_id=1, source_target_pairs={{0,1},{1,0},{2,3},{3,2},{4,5},{5,4},{6,7},{7,6},{8,9},{9,8},{10,11... | collective-permute-start | bytes 1572872 | tf_op jit(solution)/shard_map/ppermute | solution.py:24
Sparse Core Ops, SparseCore 0:
  9.4 56.5 all-gather.2
  81.6 46.8 all-gather.4
